TPU v7x, 128 devices: a whole 4x4x4 slice. The times are simulated.
128 devices in a mesh: gx: 32 (over y, x, core), gy: 4 (over z).
Axes of the slice: x: 4, y: 4, z: 4, core: 2. Of those that a mesh axis runs over, the one named last changes fastest.
Arguments:
- adjoint_source: float32 [4, 256, 256, 512], P(None, 'gx', 'gy'), may hold values from -40 to 40, as said below
- conductivity: float32 [256, 256, 512], P('gx', 'gy'), may hold values from 0.1 to 10
- electrodes: int32 [4], replicated, may hold values from 0 to 65535
Outputs:
- solution_field: float32 [4, 256, 256, 512], P(None, 'gx', 'gy')
- residual: float32 [4, 256, 256, 512], P(None, 'gx', 'gy')
Inputs may be any that keep to these rules, and one draw needn't show every extreme that they name: `electrodes`: each entry is a surface cell index, its first coordinate times 256 plus its second. `adjoint_source`: drawn afresh cell by cell.
All inputs are finite; a program needn't handle non-finite values.
Results may differ from a plain program's by a relative error of at most 0.0003.
Values sent between devices are 32-bit elements; how exact they have to be, the bound alone decides.
No kernel may reach another device: no remote copies, remote signals or barrier semaphores. Data moves between devices by JAX's collectives and lax.ppermute only.
A program may use at most 128 MiB of HBM per device.

v0:
```python
import math

import jax
import jax.numpy as jnp
from jax import lax
from jax.sharding import PartitionSpec as P

ITERS = 2


def with_halo(block, sides, width):
    for axis, dim in sides:
        count = lax.axis_size(axis)
        forward = [(i, i + 1) for i in range(count - 1)]
        backward = [(target, source) for source, target in forward]
        low = lax.ppermute(
            lax.slice_in_dim(block, block.shape[dim] - width, None, axis=dim), axis, forward
        )
        high = lax.ppermute(lax.slice_in_dim(block, 0, width, axis=dim), axis, backward)
        block = jnp.concatenate([low, block, high], axis=dim)
    return block


def face_coefficients(padded):
    center = padded[1:-1, 1:-1, 1:-1]

    def face(neighbour):
        return jnp.where(neighbour > 0.0, 0.5 * (center + neighbour), center)

    return (
        face(padded[2:, 1:-1, 1:-1]),
        face(padded[:-2, 1:-1, 1:-1]),
        face(padded[1:-1, 2:, 1:-1]),
        face(padded[1:-1, :-2, 1:-1]),
        face(padded[1:-1, 1:-1, 2:]),
        face(padded[1:-1, 1:-1, :-2]),
    )


def apply_operator(rimmed, coeffs):
    padded = jnp.pad(rimmed, ((0, 0), (0, 0), (0, 0), (1, 1)))
    center = padded[:, 1:-1, 1:-1, 1:-1]
    others = (
        padded[:, 2:, 1:-1, 1:-1],
        padded[:, :-2, 1:-1, 1:-1],
        padded[:, 1:-1, 2:, 1:-1],
        padded[:, 1:-1, :-2, 1:-1],
        padded[:, 1:-1, 1:-1, 2:],
        padded[:, 1:-1, 1:-1, :-2],
    )
    total = jnp.zeros(center.shape, jnp.float32)
    for coeff, other in zip(coeffs, others):
        total = total + coeff[None] * (center - other)
    return total


def gram(left, right):
    return jnp.einsum("ixyz,jxyz->ij", left, right, precision=lax.Precision.HIGHEST)


def combine(matrix, block):
    return jnp.einsum("ij,ixyz->jxyz", matrix, block, precision=lax.Precision.HIGHEST)


def small_solve(spd, rhs):
    factor = jnp.linalg.cholesky(spd)
    return jax.scipy.linalg.cho_solve((factor, True), rhs)


def direction_image(direction, coeffs):
    rimmed = with_halo(direction, (("gx", 1), ("gy", 2)), 1)
    return apply_operator(rimmed, coeffs)


def residual_norm(residual):
    return lax.psum(gram(residual, residual), ("gx", "gy"))


def shards(adjoint_source, conductivity, electrodes):
    rim_sigma = with_halo(conductivity, (("gx", 0), ("gy", 1)), 1)
    coeffs = face_coefficients(jnp.pad(rim_sigma, ((0, 0), (0, 0), (1, 1))))
    cells_x = adjoint_source.shape[1]
    cells_y = adjoint_source.shape[2]
    cells_z = adjoint_source.shape[3]
    total_x = cells_x * lax.axis_size("gx")
    total_y = cells_y * lax.axis_size("gy")
    current = math.sqrt(total_x * total_y * cells_z)
    start_x = lax.axis_index("gx") * cells_x
    start_y = lax.axis_index("gy") * cells_y
    row_x = electrodes // total_y
    row_y = electrodes % total_y
    mark_x = ((start_x + jnp.arange(cells_x, dtype=jnp.int32))[None, :] == row_x[:, None]).astype(
        jnp.float32
    )
    mark_y = ((start_y + jnp.arange(cells_y, dtype=jnp.int32))[None, :] == row_y[:, None]).astype(
        jnp.float32
    )
    spike = current * (mark_x[:, :, None] * mark_y[:, None, :])
    right_side = adjoint_source.at[:, :, :, 0].add(spike)
    solution_field = jnp.zeros_like(right_side)
    residual = right_side
    direction = right_side
    norm_now = residual_norm(residual)
    for step in range(ITERS):
        image = direction_image(direction, coeffs)
        curvature = lax.psum(gram(direction, image), ("gx", "gy"))
        alpha = small_solve(curvature, norm_now)
        solution_field = solution_field + combine(alpha, direction)
        residual = residual - combine(alpha, image)
        if step + 1 < ITERS:
            norm_next = residual_norm(residual)
            beta = small_solve(norm_now, norm_next)
            direction = residual + combine(beta, direction)
            norm_now = norm_next
    return (solution_field, residual)


def solution(mesh):
    placed = (P(None, "gx", "gy", None), P("gx", "gy", None), P())
    return jax.shard_map(
        shards,
        mesh=mesh,
        in_specs=placed,
        out_specs=(P(None, "gx", "gy", None), P(None, "gx", "gy", None)),
        check_vma=False,
    )
```

profile of v0, /device:TPU:1, one launch (start us, length us, event | category | flops | bytes accessed | tf_op | source)
XLA Modules:
  0.0 452.0 jit_solution(3211990552666266134)
XLA Ops:
  1.6 3.3 collective-permute-start
  5.0 3.1 collective-permute-start.2
  8.9 4.9 %copy.24 = f32[4,8,64,512]{3,0,2,1:T(4,128)S(1)} copy(f32[4,8,64,512]{3,2,1,0:T(8,128)} %param.8) | data formatting | bytes 8388608 | tf_op args[0]
  16.2 8.9 %scatter-add.4 = f32[4,8,64,512]{3,0,2,1:T(4,128)} dynamic-update-slice(f32[4,8,64,512]{3,0,2,1:T(4,128)} %copy-done, f32[4,8,64,1]{3,0,2,1:T(4,128)S(1)} %slice_add_fusion, s32[]{:T(128)} %constant.100.clone.1, s32[]{:T(128)} %constant.100.clone.1, s32[]{:T(128)} %constant.100.clone.1, s32[]{:T(128)} %constant.100.clone.1) | dynamic-update-slice | bytes 16388 | tf_op jit(solution)/shard_map/scatter-add | solution.py:99
  26.5 2.5 collective-permute-start.3
  31.4 3.5 collective-permute-start.6
  36.5 18.0 %convolution_bitcast_fusion.5 = f32[4,4]{0,1:T(4,128)S(1)} fusion(f32[4,8,64,512]{3,0,2,1:T(4,128)S(1)} %copy-done.1), kind=kOutput, calls=%fused_computation.75 | convolution fusion | flops 50331648 | bytes 4194368 | tf_op jit(solution)/shard_map/ixyz,jxyz->ij/dot_general | solution.py:58
  55.3 4.2 collective-permute-start.7
  62.3 3.1 collective-permute-done.5
  65.4 11.7 %select_maximum_fusion.4 = f32[4,10,66,514]{3,0,2,1:T(4,128)S(1)} fusion(f32[4,10,1,512]{3,0,2,1:T(4,128)S(1)} %collective-permute-done.5, f32[4,10,1,512]{3,0,2,1:T(4,128)S(1)} %collective-permute-done.7, f32[4,1,64,512]{3,0,2,1:T(4,128)S(1)} %collective-permute-done.1, f32[4,8,64,512]{3,0,2,1:T(4,128)S(1)} %copy-done.1, ...), kind=kLoop, calls=%fused_computation.6 | loop fusion | flops 16283520 | bytes 10834560 | tf_op jit(solution)/shard_map/concatenate | solution.py:20
  77.2 10.1 %fusion.17 = f32[4,8,64,512]{3,0,2,1:T(4,128)S(1)} fusion(f32[4,8,64,512]{3,0,2,1:T(4,128)S(1)} %copy-done.1, f32[4,10,66,514]{3,0,2,1:T(4,128)S(1)} %select_maximum_fusion.4, f32[4,10,1,512]{3,0,2,1:T(4,128)S(1)} %collective-permute-done.7, f32[4,1,64,512]{3,0,2,1:T(4,128)S(1)} %collective-permute-done.1, f32[4,1,64,512]{3,0,2,1:T(4,128)S(1)} %collective-permute-done.3, ...), kind=kLoop, calls=%fused_computation.38 | loop fusion | flops 26214400 | bytes 24281088 | tf_op jit(solution)/shard_map/add | solution.py:53
  87.3 2.0 copy-done.6
  89.3 18.3 %convolution_bitcast_fusion.6 = f32[4,4]{0,1:T(4,128)S(1)} fusion(f32[4,8,64,512]{3,0,2,1:T(4,128)S(1)} %copy-done.1, f32[4,8,64,512]{3,0,2,1:T(4,128)S(1)} %fusion.17), kind=kOutput, calls=%fused_computation.76 | convolution fusion | flops 50331648 | bytes 8388672 | tf_op jit(solution)/shard_map/ixyz,jxyz->ij/dot_general | solution.py:58
  107.6 69.0 %all-reduce.3 = (f32[4,4]{0,1:T(4,128)S(1)}, f32[4,4]{0,1:T(4,128)S(1)}) all-reduce(f32[4,4]{0,1:T(4,128)S(1)} %convolution_bitcast_fusion.5, f32[4,4]{0,1:T(4,128)S(1)} %convolution_bitcast_fusion.6), channel_id=1, replica_groups=mesh['gx'=32,'gy'=4] {'gx','gy'}, use_global_device_ids=true, to_apply=%region_3.5 | all-reduce | flops 32 | bytes 256 | tf_op jit(solution)/shard_map/psum | solution.py:76
  180.7 10.3 %convolution_subtract_fusion.1 = f32[4,8,64,512]{3,0,2,1:T(4,128)S(1)} fusion(f32[4,8,64,512]{3,0,2,1:T(4,128)} %scatter-add.4, f32[4,4,1,1]{0,1,3,2:T(4,128)S(1)} %convolution_bitcast_fusion.4, f32[4,8,64,512]{3,0,2,1:T(4,128)} %copy-done.6), kind=kOutput, calls=%fused_computation.66 | convolution fusion | flops 51380224 | bytes 12582976 | tf_op jit(solution)/shard_map/ij,ixyz->jxyz/dot_general | solution.py:62
  193.1 19.1 %convolution_bitcast_fusion.3 = f32[4,4]{1,0:T(4,128)S(1)} fusion(f32[4,8,64,512]{3,0,2,1:T(4,128)S(1)} %convolution_subtract_fusion.1), kind=kOutput, calls=%fused_computation.73 | convolution fusion | flops 50331648 | bytes 4194368 | tf_op jit(solution)/shard_map/ixyz,jxyz->ij/dot_general | solution.py:58
  212.6 63.7 %psum.30 = f32[4,4]{1,0:T(4,128)S(1)} all-reduce(f32[4,4]{1,0:T(4,128)S(1)} %convolution_bitcast_fusion.3), channel_id=1, replica_groups=mesh['gx'=32,'gy'=4] {'gx','gy'}, use_global_device_ids=true, to_apply=%region_4.7 | all-reduce | flops 16 | bytes 128 | tf_op jit(solution)/shard_map/psum | solution.py:76
  276.7 10.1 %convolution_add_fusion.1 = f32[4,8,64,512]{3,0,2,1:T(4,128)S(1)} fusion(f32[4,8,64,512]{3,0,2,1:T(4,128)} %copy-done.3, f32[4,4,1,1]{0,1,3,2:T(4,128)S(1)} %convolution_bitcast_fusion.2, f32[4,8,64,512]{3,0,2,1:T(4,128)} %scatter-add.4), kind=kOutput, calls=%fused_computation.65 | convolution fusion | flops 51380224 | bytes 12582976 | tf_op jit(solution)/shard_map/ij,ixyz->jxyz/dot_general | solution.py:62
  288.8 2.4 collective-permute-start.8
  291.3 3.7 collective-permute-done.9
  294.9 4.4 collective-permute-done.8
  299.4 3.0 collective-permute-start.11
  304.0 3.9 collective-permute-done.10
  307.9 12.2 %select_maximum_fusion = f32[4,10,66,514]{3,0,2,1:T(4,128)S(1)} fusion(f32[4,10,1,512]{3,0,2,1:T(4,128)S(1)} %collective-permute-done.10, f32[4,10,1,512]{3,0,2,1:T(4,128)S(1)} %collective-permute-done.11, f32[4,1,64,512]{3,0,2,1:T(4,128)S(1)} %collective-permute-done.8, f32[4,8,64,512]{3,0,2,1:T(4,128)S(1)} %convolution_add_fusion.1, ...), kind=kLoop, calls=%fused_computation.2 | loop fusion | flops 16283520 | bytes 10834560 | tf_op jit(solution)/shard_map/concatenate | solution.py:20
  320.1 10.1 %fusion.2 = f32[4,8,64,512]{3,0,2,1:T(4,128)S(1)} fusion(f32[4,8,64,512]{3,0,2,1:T(4,128)S(1)} %convolution_add_fusion.1, f32[4,10,66,514]{3,0,2,1:T(4,128)S(1)} %select_maximum_fusion, f32[4,10,1,512]{3,0,2,1:T(4,128)S(1)} %collective-permute-done.11, f32[4,1,64,512]{3,0,2,1:T(4,128)S(1)} %collective-permute-done.8, ...), kind=kLoop, calls=%fused_computation.13 | loop fusion | flops 26214400 | bytes 24281088 | tf_op jit(solution)/shard_map/add | solution.py:53
  330.2 18.3 %convolution_bitcast_fusion.1 = f32[4,4]{0,1:T(4,128)S(1)} fusion(f32[4,8,64,512]{3,0,2,1:T(4,128)S(1)} %convolution_add_fusion.1, f32[4,8,64,512]{3,0,2,1:T(4,128)S(1)} %fusion.2), kind=kOutput, calls=%fused_computation.71 | convolution fusion | flops 50331648 | bytes 8388672 | tf_op jit(solution)/shard_map/ixyz,jxyz->ij/dot_general | solution.py:58
  348.5 9.2 %fusion.59 = f32[4,8,64,512]{3,0,2,1:T(4,128)} fusion(f32[4,4,1,1]{0,1,3,2:T(4,128)S(1)} %convolution_bitcast_fusion.4, f32[4,8,64,512]{3,0,2,1:T(4,128)S(1)} %copy-done.2), kind=kOutput, calls=%fused_computation.145 | convolution fusion | flops 50331648 | bytes 8388672 | tf_op jit(solution)/shard_map/ij,ixyz->jxyz/dot_general | solution.py:62
  357.7 66.2 %psum.31 = f32[4,4]{0,1:T(4,128)S(1)} all-reduce(f32[4,4]{0,1:T(4,128)S(1)} %convolution_bitcast_fusion.1), channel_id=1, replica_groups=mesh['gx'=32,'gy'=4] {'gx','gy'}, use_global_device_ids=true, to_apply=%region_5.8 | all-reduce | flops 16 | bytes 128 | tf_op jit(solution)/shard_map/psum | solution.py:106
  426.4 10.3 %convolution_subtract_fusion = f32[4,8,64,512]{3,0,2,1:T(4,128)S(1)} fusion(f32[4,8,64,512]{3,0,2,1:T(4,128)} %copy-done.3, f32[4,4,1,1]{0,1,3,2:T(4,128)S(1)} %convolution_bitcast_fusion, f32[4,8,64,512]{3,0,2,1:T(4,128)} %copy-done.7), kind=kOutput, calls=%fused_computation.63 | convolution fusion | flops 51380224 | bytes 12582976 | tf_op jit(solution)/shard_map/ij,ixyz->jxyz/dot_general | solution.py:62
  436.7 8.4 %convolution_add_fusion = f32[4,8,64,512]{3,0,2,1:T(4,128)S(1)} fusion(f32[4,8,64,512]{3,0,2,1:T(4,128)S(1)} %copy-done.8, f32[4,4,1,1]{0,1,3,2:T(4,128)S(1)} %convolution_bitcast_fusion, f32[4,8,64,512]{3,0,2,1:T(4,128)S(1)} %copy-done.5), kind=kOutput, calls=%fused_computation.64 | convolution fusion | flops 51380224 | bytes 12582976 | tf_op jit(solution)/shard_map/ij,ixyz->jxyz/dot_general | solution.py:62
  445.1 3.3 copy.38
  448.4 3.3 copy.39
  (90 shorter events, 26.0 us)
Async XLA Ops:
  1.6 29.4 %collective-permute-start = (f32[1,64,512]{2,1,0:T(8,128)S(1)}, f32[1,64,512]{2,1,0:T(8,128)S(1)}, u32[]{:S(2)}, u32[]{:S(2)}) collective-permute-start(f32[1,64,512]{2,1,0:T(8,128)S(1)} %get-tuple-element.41), channel_id=1, source_target_pairs={{4,0},{8,4},{12,8},{16,12},{20,16},{24,20},{28,24},{32,28},{36,32}... | collective-permute-start | bytes 393224 | tf_op jit(solution)/shard_map/ppermute | solution.py:19
  5.0 26.0 %collective-permute-start.2 = (f32[1,64,512]{2,1,0:T(8,128)S(1)}, f32[1,64,512]{2,1,0:T(8,128)S(1)}, u32[]{:S(2)}, u32[]{:S(2)}) collective-permute-start(f32[1,64,512]{2,1,0:T(8,128)S(1)} %get-tuple-element.42), channel_id=1, source_target_pairs={{0,4},{4,8},{8,12},{12,16},{16,20},{20,24},{24,28},{28,32},{32,36}... | collective-permute-start | bytes 393224 | tf_op jit(solution)/shard_map/ppermute | solution.py:16
  13.8 2.0 copy-start
  13.8 17.2 %copy-start.15 = (f32[8,64,512]{2,1,0:T(8,128)S(1)}, f32[8,64,512]{2,1,0:T(8,128)}, u32[]{:S(2)}) copy-start(f32[8,64,512]{2,1,0:T(8,128)} %param.9) | copy-start | bytes 3145732
  25.1 11.4 %copy-start.1 = (f32[4,8,64,512]{3,0,2,1:T(4,128)S(1)}, f32[4,8,64,512]{3,0,2,1:T(4,128)}, u32[]{:S(2)}) copy-start(f32[4,8,64,512]{3,0,2,1:T(4,128)} %scatter-add.4) | copy-start | bytes 12582916
  26.5 28.7 %collective-permute-start.3 = (f32[4,1,64,512]{3,0,2,1:T(4,128)S(1)}, f32[4,1,64,512]{3,0,2,1:T(4,128)S(1)}, u32[]{:S(2)}, u32[]{:S(2)}) collective-permute-start(f32[4,1,64,512]{3,0,2,1:T(4,128)S(1)} %get-tuple-element.28), channel_id=1, source_target_pairs={{0,4},{4,8},{8,12},{12,16},{16,20},{20,24},{24,28},{28,32},{32,36}... | collective-permute-start | bytes 1572872 | tf_op jit(solution)/shard_map/ppermute | solution.py:16
  29.0 26.2 %collective-permute-start.1 = (f32[4,1,64,512]{3,0,2,1:T(4,128)S(1)}, f32[4,1,64,512]{3,0,2,1:T(4,128)S(1)}, u32[]{:S(2)}, u32[]{:S(2)}) collective-permute-start(f32[4,1,64,512]{3,0,2,1:T(4,128)S(1)} %get-tuple-element.29), channel_id=1, source_target_pairs={{4,0},{8,4},{12,8},{16,12},{20,16},{24,20},{28,24},{32,28},{36,32}... | collective-permute-start | bytes 1572872 | tf_op jit(solution)/shard_map/ppermute | solution.py:19
  31.4 23.0 %collective-permute-start.6 = (f32[10,1,512]{2,1,0:T(1,128)S(1)}, f32[10,1,512]{2,1,0:T(1,128)S(1)}, u32[]{:S(2)}, u32[]{:S(2)}) collective-permute-start(f32[10,1,512]{2,1,0:T(1,128)S(1)} %get-tuple-element.34), channel_id=1, source_target_pairs={{0,1},{1,2},{2,3},{4,5},{5,6},{6,7},{8,9},{9,10},{10,11},{12,13},{... | collective-permute-start | bytes 61448 | tf_op jit(solution)/shard_map/ppermute | solution.py:16
  35.0 19.5 %collective-permute-start.4 = (f32[10,1,512]{2,1,0:T(1,128)S(1)}, f32[10,1,512]{2,1,0:T(1,128)S(1)}, u32[]{:S(2)}, u32[]{:S(2)}) collective-permute-start(f32[10,1,512]{2,1,0:T(1,128)S(1)} %get-tuple-element.35), channel_id=1, source_target_pairs={{1,0},{2,1},{3,2},{5,4},{6,5},{7,6},{9,8},{10,9},{11,10},{13,12},{... | collective-permute-start | bytes 61448 | tf_op jit(solution)/shard_map/ppermute | solution.py:19
  54.5 6.7 %copy-start.16 = (f32[8,64,512]{2,1,0:T(8,128)S(1)}, f32[8,64,512]{2,1,0:T(8,128)}, u32[]{:S(2)}) copy-start(f32[8,64,512]{2,1,0:T(8,128)} %param.9) | copy-start | bytes 3145732
  55.3 7.0 %collective-permute-start.7 = (f32[4,10,1,512]{3,0,2,1:T(4,128)S(1)}, f32[4,10,1,512]{3,0,2,1:T(4,128)S(1)}, u32[]{:S(2)}, u32[]{:S(2)}) collective-permute-start(f32[4,10,1,512]{3,0,2,1:T(4,128)S(1)} %get-tuple-element.24), channel_id=1, source_target_pairs={{0,1},{1,2},{2,3},{4,5},{5,6},{6,7},{8,9},{9,10},{10,11},{12,13},{... | collective-permute-start | bytes 245768 | tf_op jit(solution)/shard_map/ppermute | solution.py:16
  59.5 5.9 %collective-permute-start.5 = (f32[4,10,1,512]{3,0,2,1:T(4,128)S(1)}, f32[4,10,1,512]{3,0,2,1:T(4,128)S(1)}, u32[]{:S(2)}, u32[]{:S(2)}) collective-permute-start(f32[4,10,1,512]{3,0,2,1:T(4,128)S(1)} %get-tuple-element.25), channel_id=1, source_target_pairs={{1,0},{2,1},{3,2},{5,4},{6,5},{7,6},{9,8},{10,9},{11,10},{13,12},{... | collective-permute-start | bytes 245768 | tf_op jit(solution)/shard_map/ppermute | solution.py:19
  62.2 14.9 %copy-start.9 = (f32[8,64,512]{2,1,0:T(8,128)}, f32[8,64,512]{2,1,0:T(8,128)S(1)}, u32[]{:S(2)}) copy-start(f32[8,64,512]{2,1,0:T(8,128)S(1)} %get-tuple-element.33) | copy-start | bytes 3145732
  62.2 14.9 %copy-start.11 = (f32[8,64,512]{2,1,0:T(8,128)}, f32[8,64,512]{2,1,0:T(8,128)S(1)}, u32[]{:S(2)}) copy-start(f32[8,64,512]{2,1,0:T(8,128)S(1)} %get-tuple-element.39) | copy-start | bytes 3145732
  62.2 14.9 %copy-start.13 = (f32[8,64,512]{2,1,0:T(8,128)}, f32[8,64,512]{2,1,0:T(8,128)S(1)}, u32[]{:S(2)}) copy-start(f32[8,64,512]{2,1,0:T(8,128)S(1)} %get-tuple-element.40) | copy-start | bytes 3145732
  87.3 2.0 copy-start.6
  191.1 2.0 copy-start.3
  286.8 43.3 %copy-start.4 = (f32[4,8,64,512]{3,0,2,1:T(4,128)}, f32[4,8,64,512]{3,0,2,1:T(4,128)S(1)}, u32[]{:S(2)}) copy-start(f32[4,8,64,512]{3,0,2,1:T(4,128)S(1)} %convolution_add_fusion.1) | copy-start | bytes 12582916
  286.9 8.0 %collective-permute-start.9 = (f32[4,1,64,512]{3,0,2,1:T(4,128)S(1)}, f32[4,1,64,512]{3,0,2,1:T(4,128)S(1)}, u32[]{:S(2)}, u32[]{:S(2)}) collective-permute-start(f32[4,1,64,512]{3,0,2,1:T(4,128)S(1)} %get-tuple-element.26), channel_id=1, source_target_pairs={{0,4},{4,8},{8,12},{12,16},{16,20},{20,24},{24,28},{28,32},{32,36}... | collective-permute-start | bytes 1572872 | tf_op jit(solution)/shard_map/ppermute | solution.py:16
  288.8 10.5 %collective-permute-start.8 = (f32[4,1,64,512]{3,0,2,1:T(4,128)S(1)}, f32[4,1,64,512]{3,0,2,1:T(4,128)S(1)}, u32[]{:S(2)}, u32[]{:S(2)}) collective-permute-start(f32[4,1,64,512]{3,0,2,1:T(4,128)S(1)} %get-tuple-element.27), channel_id=1, source_target_pairs={{4,0},{8,4},{12,8},{16,12},{20,16},{24,20},{28,24},{32,28},{36,32}... | collective-permute-start | bytes 1572872 | tf_op jit(solution)/shard_map/ppermute | solution.py:19
  299.4 4.6 %collective-permute-start.11 = (f32[4,10,1,512]{3,0,2,1:T(4,128)S(1)}, f32[4,10,1,512]{3,0,2,1:T(4,128)S(1)}, u32[]{:S(2)}, u32[]{:S(2)}) collective-permute-start(f32[4,10,1,512]{3,0,2,1:T(4,128)S(1)} %get-tuple-element.22), channel_id=1, source_target_pairs={{0,1},{1,2},{2,3},{4,5},{5,6},{6,7},{8,9},{9,10},{10,11},{12,13},{... | collective-permute-start | bytes 245768 | tf_op jit(solution)/shard_map/ppermute | solution.py:16
  302.4 17.6 %copy-start.10 = (f32[8,64,512]{2,1,0:T(8,128)S(1)}, f32[8,64,512]{2,1,0:T(8,128)}, u32[]{:S(2)}) copy-start(f32[8,64,512]{2,1,0:T(8,128)} %copy-done.9) | copy-start | bytes 3145732
  302.4 17.6 %copy-start.12 = (f32[8,64,512]{2,1,0:T(8,128)S(1)}, f32[8,64,512]{2,1,0:T(8,128)}, u32[]{:S(2)}) copy-start(f32[8,64,512]{2,1,0:T(8,128)} %copy-done.11) | copy-start | bytes 3145732
  302.4 17.6 %copy-start.14 = (f32[8,64,512]{2,1,0:T(8,128)S(1)}, f32[8,64,512]{2,1,0:T(8,128)}, u32[]{:S(2)}) copy-start(f32[8,64,512]{2,1,0:T(8,128)} %copy-done.13) | copy-start | bytes 3145732
  302.4 5.4 %collective-permute-start.10 = (f32[4,10,1,512]{3,0,2,1:T(4,128)S(1)}, f32[4,10,1,512]{3,0,2,1:T(4,128)S(1)}, u32[]{:S(2)}, u32[]{:S(2)}) collective-permute-start(f32[4,10,1,512]{3,0,2,1:T(4,128)S(1)} %get-tuple-element.23), channel_id=1, source_target_pairs={{1,0},{2,1},{3,2},{5,4},{6,5},{7,6},{9,8},{10,9},{11,10},{13,12},{... | collective-permute-start | bytes 245768 | tf_op jit(solution)/shard_map/ppermute | solution.py:19
  330.2 18.3 %copy-start.7 = (f32[4,8,64,512]{3,0,2,1:T(4,128)}, f32[4,8,64,512]{3,0,2,1:T(4,128)S(1)}, u32[]{:S(2)}) copy-start(f32[4,8,64,512]{3,0,2,1:T(4,128)S(1)} %fusion.2) | copy-start | bytes 12582916
  330.2 18.3 %copy-start.2 = (f32[4,8,64,512]{3,0,2,1:T(4,128)S(1)}, f32[4,8,64,512]{3,0,2,1:T(4,128)}, u32[]{:S(2)}) copy-start(f32[4,8,64,512]{3,0,2,1:T(4,128)} %scatter-add.4) | copy-start | bytes 12582916
  426.4 10.3 %copy-start.5 = (f32[4,8,64,512]{3,0,2,1:T(4,128)S(1)}, f32[4,8,64,512]{3,0,2,1:T(4,128)}, u32[]{:S(2)}) copy-start(f32[4,8,64,512]{3,0,2,1:T(4,128)} %copy-done.4) | copy-start | bytes 12582916
  426.4 10.3 %copy-start.8 = (f32[4,8,64,512]{3,0,2,1:T(4,128)S(1)}, f32[4,8,64,512]{3,0,2,1:T(4,128)}, u32[]{:S(2)}) copy-start(f32[4,8,64,512]{3,0,2,1:T(4,128)} %fusion.59) | copy-start | bytes 12582916
where the time goes:
time: 457 us; the launch traced here: 452 us
  blocking collectives  199 us (44%)
  matrix products  123 us (27%)
  other arithmetic  53.3 us (12%)
  starting transfers between devices  30.7 us (7%)
  local copies, waits for them, and re-layouts  29.3 us (6%)
  waiting for transfers between devices  15.1 us (3%)
    psum x2, blocking collectives, residual_norm(): return lax.psum(gram(residual, residual), ('gx', 'gy'))  133 us
    dot_general x4, matrix products, gram(): jnp.einsum('ixyz,jxyz->ij', left, right, precision=lax.Precision.HIGHEST)  73.7 us
    psum x1, blocking collectives, shards(): curvature = lax.psum(gram(direction, image), ('gx', 'gy'))  66.2 us
    dot_general x5, matrix products, combine(): jnp.einsum('ij,ixyz->jxyz', matrix, block, precision=lax.Precision.HIGHEST)  48.3 us
    concatenate x5, other arithmetic, with_halo(): block = jnp.concatenate([low, block, high], axis=dim)  24.7 us
    add x2, other arithmetic, apply_operator(): total = total + coeff[None] * (center - other)  20.2 us
    ppermute x6, starting transfers between devices, with_halo(): lax.ppermute(lax.slice_in_dim(block, block.shape[dim] - width, None, axis...  18.3 us
    unnamed x38, local copies, waits for them, and re-layouts  17.5 us
  transfers between devices with their start and end apart: 12, of which 4 were waited for; matrix products, arithmetic and copies ran while one was open for 8% of the time, Pallas kernels for 0%

commit v1 on v0

v1 whole, which is shorter than its diff:
```python
import functools
import math

import jax
import jax.numpy as jnp
from jax import lax
from jax.experimental import pallas as pl
from jax.experimental.pallas import tpu as pltpu
from jax.sharding import PartitionSpec as P

AXES = ("gx", "gy")
F = 4
NX = 8
NY = 64
NZ = 512
CHUNKS = NY // 8
PAIRS = [(i, j) for i in range(F) for j in range(i, F)]
L1_ROWS = (F + 1) * NY
L2_ROWS = F * NY + 16
IN_ROWS = L1_ROWS + L2_ROWS
G_ROWS = (F + 1) * 8 + F * 8
VMEM_LIMIT = 16 * 1024 * 1024

VM = pl.BlockSpec(memory_space=pltpu.VMEM)
SM = pl.BlockSpec(memory_space=pltpu.SMEM)
HBM = pl.BlockSpec(memory_space=pltpu.HBM)


def f32(*shape):
    return pltpu.VMEM(shape, jnp.float32)


def params():
    return pltpu.CompilerParams(vmem_limit_bytes=VMEM_LIMIT)


def cost(us):
    return pl.CostEstimate(flops=int(us * 4e6), bytes_accessed=int(us * 3.0e6), transcendentals=0)


def iota(dim):
    return lax.broadcasted_iota(jnp.int32, (8, NZ), dim)


def roll_z(v, shift):
    return pltpu.roll(v, shift % NZ, 1)


def row_up(load, i, halo):
    if i < CHUNKS - 1:
        return load(8 * i + 1)
    return jnp.where(iota(0) == 7, halo(), pltpu.roll(load(8 * i), 7, 0))


def row_down(load, i, halo):
    if i > 0:
        return load(8 * i - 1)
    return jnp.where(iota(0) == 0, halo(), pltpu.roll(load(8 * i), 1, 0))


def inside(h_other, h):
    return jnp.where(h_other > 0.0, h_other, h)


def z_coeffs(h):
    lane = iota(1)
    up = h + roll_z(h, -1)
    up_n = jnp.where(lane == NZ - 1, 0.0, up)
    down_n = roll_z(up_n, 1)
    total = jnp.where(lane == NZ - 1, 2.0 * h, up) + jnp.where(lane == 0, 2.0 * h, down_n)
    return up_n, down_n, total


def select_rows(ypar, r0, r1, start, count):
    a = r0[pl.ds(start, count), :]
    b = r1[pl.ds(start, count), :]
    return jnp.where(ypar == 0, b, a), jnp.where(ypar == 0, a, b)


def lanes_sum(p):
    return p[:, 0:128] + p[:, 128:256] + p[:, 256:384] + p[:, 384:512]


def add_gram(acc, base, left, right):
    for n, (i, j) in enumerate(PAIRS):
        acc[base + n] += lanes_sum(left[i] * right[j])


def add_spike(ref, index, row, current):
    tile = ref[(*index, slice(0, 128))]
    sub = lax.broadcasted_iota(jnp.int32, (8, 128), 0)
    lane = lax.broadcasted_iota(jnp.int32, (8, 128), 1)
    ref[(*index, slice(0, 128))] = tile + jnp.where((sub == row) & (lane == 0), current, 0.0)


def local_cell(elec, f):
    total_y = NY * lax.axis_size("gy")
    cell = elec[f]
    lx = cell // total_y - lax.axis_index("gx") * NX
    ly = cell % total_y - lax.axis_index("gy") * NY
    return lx, ly, (lx >= 0) & (lx < NX) & (ly >= 0) & (ly < NY)


def pack_kernel(current, adj, sigma, elec_in, l1_out, g0_out, g1_out, tiles, rows, elec, sems, esem):
    par = lax.axis_index("gx") % 2
    ypar = lax.axis_index("gy") % 2
    edge = par * (NX - 1)
    ecopy = pltpu.make_async_copy(elec_in, elec, esem)
    ecopy.start()
    copies = []
    for f in range(F + 1):
        src = adj.at[f] if f < F else sigma
        copies.append(
            pltpu.make_async_copy(src.at[edge], l1_out.at[pl.ds(f * NY, NY)], sems.at[0, f])
        )
        for side, y in ((0, 0), (1, NY - 8)):
            copies.append(
                pltpu.make_async_copy(
                    src.at[:, pl.ds(y, 8), :], tiles.at[f, side], sems.at[1 + side, f]
                )
            )
    for c in copies:
        c.start()
    ecopy.wait()
    for c in copies:
        c.wait()
    for f in range(F):
        lx, ly, here = local_cell(elec, f)

        @pl.when(here & (lx == edge))
        def _(f=f, ly=ly):
            r8 = pl.multiple_of((ly // 8) * 8, 8)
            add_spike(l1_out, (pl.ds(f * NY + r8, 8),), ly - r8, current)

        @pl.when(here & (ly < 8))
        def _(f=f, lx=lx, ly=ly):
            add_spike(tiles, (f, 0, lx, slice(0, 8)), ly, current)

        @pl.when(here & (ly >= NY - 8))
        def _(f=f, lx=lx, ly=ly):
            add_spike(tiles, (f, 1, lx, slice(0, 8)), ly - (NY - 8), current)

    h_rows = slice(F * NY, (F + 1) * NY)
    l1_out[h_rows, :] = 0.5 * l1_out[h_rows, :]
    for side, at in enumerate(((0, 1), (7, 6))):
        for depth, y in enumerate(at):
            for x in range(NX):
                for f in range(F + 1):
                    rows[side, depth, f * 8 + x : f * 8 + x + 1, :] = tiles[f, side, x, y : y + 1, :]
    h8 = slice(F * 8, F * 8 + 8)
    c_lo = 0.5 * (rows[0, 0, h8, :] + rows[0, 1, h8, :])
    c_hi = 0.5 * (rows[1, 0, h8, :] + rows[1, 1, h8, :])
    for f in range(F + 1):
        s = slice(f * 8, f * 8 + 8)
        k = 1.0 if f < F else 0.5
        lo, hi = k * rows[0, 0, s, :], k * rows[1, 0, s, :]
        g0_out[s, :] = jnp.where(ypar == 0, hi, lo)
        g1_out[s, :] = jnp.where(ypar == 0, lo, hi)
    for f in range(F):
        s = slice(f * 8, f * 8 + 8)
        lo = c_lo * (rows[0, 0, s, :] - rows[0, 1, s, :])
        hi = c_hi * (rows[1, 0, s, :] - rows[1, 1, s, :])
        d = slice((F + 1 + f) * 8, (F + 1 + f) * 8 + 8)
        g0_out[d, :] = jnp.where(ypar == 0, hi, lo)
        g1_out[d, :] = jnp.where(ypar == 0, lo, hi)


def pack(current, adj, sigma, electrodes):
    return pl.pallas_call(
        functools.partial(pack_kernel, current),
        out_shape=(f32(L1_ROWS, NZ), f32(G_ROWS, NZ), f32(G_ROWS, NZ)),
        in_specs=[HBM, HBM, HBM],
        out_specs=(VM,) * 3,
        scratch_shapes=[
            pltpu.VMEM((F + 1, 2, NX, 8, NZ), jnp.float32),
            pltpu.VMEM((2, 2, (F + 1) * 8, NZ), jnp.float32),
            pltpu.SMEM((F,), jnp.int32),
            pltpu.SemaphoreType.DMA((3, F + 1)),
            pltpu.SemaphoreType.DMA,
        ],
        compiler_params=params(),
        cost_estimate=cost(2),
        name="pack",
    )(adj, sigma, electrodes)


def load_kernel(current, adj, sigma, elec_in, b_out, h_out, acc, elec, sems, esem):
    ecopy = pltpu.make_async_copy(elec_in, elec, esem)
    ecopy.start()
    copies = [pltpu.make_async_copy(adj.at[f], b_out.at[f], sems.at[f]) for f in range(F)]
    copies.append(pltpu.make_async_copy(sigma, h_out, sems.at[F]))
    for c in copies:
        c.start()
    ecopy.wait()
    acc[...] = jnp.zeros(acc.shape, jnp.float32)
    for c in copies:
        c.wait()
    for f in range(F):
        lx, ly, here = local_cell(elec, f)

        @pl.when(here)
        def _(f=f, lx=lx, ly=ly):
            r8 = pl.multiple_of((ly // 8) * 8, 8)
            add_spike(b_out, (f, lx, pl.ds(r8, 8)), ly - r8, current)

    def plane(x, carry):
        for i in range(CHUNKS):
            r = slice(8 * i, 8 * i + 8)
            h_out[x, r, :] = 0.5 * h_out[x, r, :]
            vs = [b_out[f, x, r, :] for f in range(F)]
            add_gram(acc, 0, vs, vs)
        return carry

    lax.fori_loop(0, NX, plane, 0)


def load_fields(current, adj, sigma, electrodes):
    return pl.pallas_call(
        functools.partial(load_kernel, current),
        out_shape=(f32(F, NX, NY, NZ), f32(NX, NY, NZ), f32(10, 8, 128)),
        in_specs=[HBM, HBM, HBM],
        out_specs=(VM,) * 3,
        scratch_shapes=[
            pltpu.SMEM((F,), jnp.int32),
            pltpu.SemaphoreType.DMA((F + 1,)),
            pltpu.SemaphoreType.DMA,
        ],
        compiler_params=params(),
        cost_estimate=cost(3),
        name="load",
    )(adj, sigma, electrodes)


def chunk_coeffs(h_at, i, h_lo, h_hi, h_low=None, h_high=None):
    h = h_at(8 * i)
    up = h + row_up(h_at, i, lambda: inside(h_hi, h))
    down = h + row_down(h_at, i, lambda: inside(h_lo, h))
    zu, zd, total = z_coeffs(h)
    total = total + up + down
    xs = []
    for beside in (h_low, h_high):
        if beside is not None:
            xs.append(h + beside(8 * i))
            total = total + xs[-1]
        else:
            xs.append(None)
    return total, up, down, zu, zd, *xs


def chunk_apply(coeffs, load, low, high, i, lo_row, hi_row):
    total, up, down, zu, zd, xl, xh = coeffs
    v = load(8 * i)
    out = total * v - up * row_up(load, i, lambda: hi_row) - down * row_down(load, i, lambda: lo_row)
    out = out - zu * roll_z(v, -1) - zd * roll_z(v, 1)
    if xl is not None:
        out = out - xl * low(8 * i)
    if xh is not None:
        out = out - xh * high(8 * i)
    return v, out


def rows_of(ref, *index):
    return lambda r: ref[(*index, slice(r, r + 8), slice(None))]


def edge_kernel(b, h, r0, r1, y_out, l2_out, in_out):
    par = lax.axis_index("gx") % 2
    ypar = lax.axis_index("gy") % 2
    for n, x in enumerate((0, NX - 1)):
        beside = 1 if n == 0 else NX - 2
        h_lo, h_hi = select_rows(ypar, r0, r1, F * 8 + x, 1)
        rows = [select_rows(ypar, r0, r1, f * 8 + x, 1) for f in range(F)]
        for i in range(CHUNKS):
            side = {"h_high" if n == 0 else "h_low": rows_of(h, beside)}
            coeffs = chunk_coeffs(rows_of(h, x), i, h_lo, h_hi, **side)
            for f in range(F):
                other = rows_of(b, f, beside)
                _, out = chunk_apply(coeffs, rows_of(b, f, x), other, other, i, *rows[f])
                y_out[f, n, 8 * i : 8 * i + 8, :] = out
    far = par * (NX - 1)
    near = (NX - 1) - far
    in_out[F * NY : L1_ROWS, :] = h[near]
    for f in range(F):
        l2_out[f * NY : (f + 1) * NY, :] = y_out[f, par]
        in_out[f * NY : (f + 1) * NY, :] = b[f, near]
        in_out[L1_ROWS + f * NY : L1_ROWS + (f + 1) * NY, :] = y_out[f, 1 - par]
    l2_out[F * NY : L2_ROWS, :] = jnp.zeros((16, NZ), jnp.float32)
    in_out[L1_ROWS + F * NY : IN_ROWS, :] = jnp.zeros((16, NZ), jnp.float32)
    for f in range(F + 1):
        lo, hi = select_rows(ypar, r0, r1, f * 8 + far, 1)
        l2_out[F * NY + f : F * NY + f + 1, :] = lo
        l2_out[F * NY + 8 + f : F * NY + 8 + f + 1, :] = hi
        lo, hi = select_rows(ypar, r0, r1, f * 8 + near, 1)
        base = L1_ROWS + F * NY + f
        in_out[base : base + 1, :] = lo
        in_out[base + 8 : base + 9, :] = hi


def edge(b, h, r0, r1):
    return pl.pallas_call(
        edge_kernel,
        out_shape=(f32(F, 2, NY, NZ), f32(L2_ROWS, NZ), f32(IN_ROWS, NZ)),
        in_specs=[VM] * 4,
        out_specs=(VM,) * 3,
        compiler_params=params(),
        cost_estimate=cost(3),
        name="edge",
    )(b, h, r0, r1)


def row_halo(b, h, rh, side):
    y = 0 if side == 0 else NY - 1
    sub = iota(0)
    h_r = rh(F)
    h_own = jnp.concatenate([h[x, y : y + 1, :] for x in range(NX)], axis=0)
    zu, zd, total = z_coeffs(h_r)
    across = h_r + h_own
    up = jnp.where(sub == NX - 1, 0.0, h_r + pltpu.roll(h_r, 7, 0))
    down = jnp.where(sub == 0, 0.0, h_r + pltpu.roll(h_r, 1, 0))
    total = total + across + up + down
    outs = []
    for f in range(F):
        v = rh(f)
        own = jnp.concatenate([b[f, x, y : y + 1, :] for x in range(NX)], axis=0)
        out = total * v + rh(F + 1 + f) - across * own
        out = out - up * pltpu.roll(v, 7, 0) - down * pltpu.roll(v, 1, 0)
        out = out - zu * roll_z(v, -1) - zd * roll_z(v, 1)
        outs.append(jnp.where(h_r > 0.0, out, 0.0))
    return outs


def z_plane(h3, y3, h_rows, y_rows, store, acc):
    h_low, h_at, h_high = h3
    for i in range(CHUNKS):
        coeffs = chunk_coeffs(h_at, i, *h_rows, h_low, h_high)
        vs, outs = [], []
        for f in range(F):
            low, load, high = y3(f)
            v, out = chunk_apply(coeffs, load, low, high, i, *y_rows[f])
            store(f, 8 * i, out)
            vs.append(v)
            outs.append(out)
        add_gram(acc, 20, vs, outs)


def halo_of(x, yrows, hrows):
    h_rows = (hrows[0, pl.ds(x, 1), :], hrows[1, pl.ds(x, 1), :])
    y_rows = [(yrows[0, f, pl.ds(x, 1), :], yrows[1, f, pl.ds(x, 1), :]) for f in range(F)]
    return h_rows, y_rows


def inner_kernel(b, h, r0, r1, y, z, acc, yrows, hrows):
    ypar = lax.axis_index("gy") % 2
    acc[...] = jnp.zeros(acc.shape, jnp.float32)
    for side in range(2):
        rh = lambda f: select_rows(ypar, r0, r1, f * 8, 8)[side]
        hrows[side] = rh(F)
        for f, out in enumerate(row_halo(b, h, rh, side)):
            yrows[side, f] = out

    def y_plane(x, carry):
        h_lo, h_hi = select_rows(ypar, r0, r1, F * 8 + x, 1)
        rows = [select_rows(ypar, r0, r1, f * 8 + x, 1) for f in range(F)]
        for i in range(CHUNKS):
            coeffs = chunk_coeffs(
                rows_of(h, x), i, h_lo, h_hi, rows_of(h, x - 1), rows_of(h, x + 1)
            )
            vs, outs = [], []
            for f in range(F):
                low, load, high = (rows_of(b, f, x + d) for d in (-1, 0, 1))
                v, out = chunk_apply(coeffs, load, low, high, i, *rows[f])
                y[f, x - 1, 8 * i : 8 * i + 8, :] = out
                vs.append(v)
                outs.append(out)
            add_gram(acc, 0, vs, outs)
            add_gram(acc, 10, outs, outs)
        return carry

    lax.fori_loop(1, NX - 1, y_plane, 0)

    def z_loop(x, carry):
        def store(f, r, out):
            z[f, x - 2, r : r + 8, :] = out

        z_plane(
            [rows_of(h, x + d) for d in (-1, 0, 1)],
            lambda f: [rows_of(y, f, x - 1 + d) for d in (-1, 0, 1)],
            *halo_of(x, yrows, hrows),
            store,
            acc,
        )
        return carry

    lax.fori_loop(2, NX - 2, z_loop, 0)


def inner(b, h, r0, r1):
    return pl.pallas_call(
        inner_kernel,
        out_shape=(
            f32(F, NX - 2, NY, NZ),
            f32(F, NX - 4, NY, NZ),
            f32(30, 8, 128),
            f32(2, F, 8, NZ),
            f32(2, 8, NZ),
        ),
        in_specs=[VM] * 4,
        out_specs=(VM,) * 5,
        compiler_params=params(),
        cost_estimate=cost(8),
        name="inner",
    )(b, h, r0, r1)


def outer_kernel(
    b, h, rl1, rl2, rin, r0, r1, ye, yi, accb, acc_in, yr_in, hrows,
    yo, zo, msg,
    acc, yhalo, hhalo, yrows,
):
    par = lax.axis_index("gx") % 2
    ypar = lax.axis_index("gy") % 2
    acc[...] = acc_in[...]
    yrows[...] = yr_in[...]
    for n, first, second, s0 in ((par, rl1, rl2, 0), (1 - par, rin, rin, L1_ROWS)):
        x = n * (NX - 1)
        for i in range(CHUNKS):
            r = 8 * i
            own = h[x, r : r + 8, :]
            there = first[F * NY + r : F * NY + r + 8, :]
            beyond = inside(there, own)
            hhalo[n, r : r + 8, :] = beyond
            c = own + beyond
            vs, outs = [], []
            for f in range(F):
                v = b[f, x, r : r + 8, :]
                flux = c * (v - first[f * NY + r : f * NY + r + 8, :])
                out = ye[f, n, r : r + 8, :] + flux
                yo[f, n, r : r + 8, :] = out
                other = second[s0 + f * NY + r : s0 + f * NY + r + 8, :] - flux
                yhalo[f, n, r : r + 8, :] = jnp.where(there > 0.0, other, 0.0)
                vs.append(v)
                outs.append(out)
            add_gram(acc, 0, vs, outs)
            add_gram(acc, 10, outs, outs)
        for side in range(2):
            base = s0 + F * NY + 8 * side
            h_r = hrows[side, pl.ds(x, 1), :]
            h_c = second[base + F : base + F + 1, :]
            c = h_r + inside(h_c, h_r)
            for f in range(F):
                v = select_rows(ypar, r0, r1, f * 8 + x, 1)[side]
                add = jnp.where(h_r > 0.0, c * (v - second[base + f : base + f + 1, :]), 0.0)
                yrows[side, f, pl.ds(x, 1), :] = yrows[side, f, pl.ds(x, 1), :] + add
    h_of = lambda x: rows_of(hhalo, 0 if x < 0 else 1) if x in (-1, NX) else rows_of(h, x)

    def y_of(f, x):
        if x in (-1, NX):
            return rows_of(yhalo, f, 0 if x < 0 else 1)
        if x in (0, NX - 1):
            return rows_of(yo, f, 0 if x == 0 else 1)
        return rows_of(yi, f, x - 1)

    for n, x in enumerate((0, 1, NX - 2, NX - 1)):

        def store(f, r, out, n=n):
            zo[f, n, r : r + 8, :] = out

        z_plane(
            [h_of(x + d) for d in (-1, 0, 1)],
            lambda f: [y_of(f, x + d) for d in (-1, 0, 1)],
            *halo_of(x, yrows, hrows),
            store,
            acc,
        )
    sums = jnp.concatenate(
        [jnp.sum(accb[k], axis=0, keepdims=True) for k in range(10)]
        + [jnp.sum(acc[k], axis=0, keepdims=True) for k in range(30)]
        + [jnp.zeros((88, 128), jnp.float32)],
        axis=0,
    )
    msg[...] = lax.dot_general(
        jnp.ones((8, 128), jnp.float32),
        sums,
        (((1,), (1,)), ((), ())),
        precision=lax.Precision.HIGHEST,
        preferred_element_type=jnp.float32,
    )


def outer(b, h, rl1, rl2, rin, r0, r1, ye, yi, accb, acc, yrows, hrows):
    return pl.pallas_call(
        outer_kernel,
        out_shape=(f32(F, 2, NY, NZ), f32(F, 4, NY, NZ), f32(8, 128)),
        in_specs=[VM] * 13,
        out_specs=(VM,) * 3,
        scratch_shapes=[
            pltpu.VMEM((30, 8, 128), jnp.float32),
            pltpu.VMEM((F, 2, NY, NZ), jnp.float32),
            pltpu.VMEM((2, NY, NZ), jnp.float32),
            pltpu.VMEM((2, F, 8, NZ), jnp.float32),
        ],
        compiler_params=params(),
        cost_estimate=cost(5),
        name="outer",
    )(b, h, rl1, rl2, rin, r0, r1, ye, yi, accb, acc, yrows, hrows)


def mm(a, b, ta=False):
    at = (lambda i, k: a[k][i]) if ta else (lambda i, k: a[i][k])
    return [
        [sum((at(i, k) * b[k][j] for k in range(1, F)), at(i, 0) * b[0][j]) for j in range(F)]
        for i in range(F)
    ]


def add(a, b, s=1.0):
    return [[a[i][j] + s * b[i][j] for j in range(F)] for i in range(F)]


def symmetric(a):
    return [[a[i][j] if i == j else 0.5 * (a[i][j] + a[j][i]) for j in range(F)] for i in range(F)]


def spd_solve(a, b):
    low = [[None] * F for _ in range(F)]
    d, inv = [None] * F, [None] * F
    for j in range(F):
        t = a[j][j]
        for k in range(j):
            t = t - low[j][k] * low[j][k] * d[k]
        d[j] = t
        inv[j] = 1.0 / t
        for i in range(j + 1, F):
            t = a[i][j]
            for k in range(j):
                t = t - low[i][k] * low[j][k] * d[k]
            low[i][j] = t * inv[j]
    x = [list(row) for row in b]
    for i in range(F):
        for k in range(i):
            for j in range(F):
                x[i][j] = x[i][j] - low[i][k] * x[k][j]
    for i in range(F):
        x[i] = [e * inv[i] for e in x[i]]
    for i in reversed(range(F)):
        for k in range(i + 1, F):
            for j in range(F):
                x[i][j] = x[i][j] - low[k][i] * x[k][j]
    return x


def step_matrices(entry):
    grams = []
    for g in range(4):
        m = [[None] * F for _ in range(F)]
        for n, (i, j) in enumerate(PAIRS):
            m[i][j] = m[j][i] = entry(10 * g + n)
        grams.append(m)
    bb, by, yy, yz = grams
    alpha = spd_solve(by, bb)
    new = symmetric(add(mm(alpha, mm(yy, alpha), ta=True), bb, -1.0))
    beta = spd_solve(bb, new)
    e = [[beta[i][j] + 1.0 if i == j else beta[i][j] for j in range(F)] for i in range(F)]
    cross = mm(e, mm(yy, alpha), ta=True)
    curv = add(mm(e, mm(by, e), ta=True), mm(alpha, mm(yz, alpha), ta=True))
    curv = [[curv[i][j] - cross[i][j] - cross[j][i] for j in range(F)] for i in range(F)]
    alpha2 = spd_solve(symmetric(curv), new)
    m1 = add(alpha, mm(e, alpha2))
    m2 = mm(alpha, alpha2)
    return m1, m2


def final_kernel(w, b, yo, yi, zo, zi, xs_out, res_out, coef):
    x = pl.program_id(0)

    @pl.when(x == 0)
    def _():
        total = jnp.sum(w[...], axis=0, keepdims=True)
        sub = lax.broadcasted_iota(jnp.int32, (128, 128), 0)
        lane = lax.broadcasted_iota(jnp.int32, (128, 128), 1)
        spread = lax.dot_general(
            jnp.where(sub == lane, total, 0.0),
            jnp.ones((128, 128), jnp.float32),
            (((1,), (0,)), ((), ())),
            precision=lax.Precision.HIGHEST,
            preferred_element_type=jnp.float32,
        )
        m1, m2 = step_matrices(lambda k: spread[k : k + 1, :])
        for i in range(F):
            for j in range(F):
                coef[i * F + j] = jnp.broadcast_to(m1[i][j], (8, 128))
                coef[16 + i * F + j] = jnp.broadcast_to(m2[i][j], (8, 128))

    def planes(y_at, z_at):
        def body(i, carry):
            r = pl.ds(pl.multiple_of(i * 8, 8), 8)
            for q in range(NZ // 128):
                s = slice(q * 128, q * 128 + 128)
                bs = [b[f, x, r, s] for f in range(F)]
                ys = [y_at[0][f, y_at[1], r, s] for f in range(F)]
                zs = [z_at[0][f, z_at[1], r, s] for f in range(F)]
                for j in range(F):
                    xo, ro = None, bs[j]
                    for k in range(F):
                        c1 = coef[k * F + j]
                        c2 = coef[16 + k * F + j]
                        t = bs[k] * c1 - ys[k] * c2
                        xo = t if xo is None else xo + t
                        ro = ro - ys[k] * c1 + zs[k] * c2
                    xs_out[j, 0, r, s] = xo
                    res_out[j, 0, r, s] = ro
            return carry

        lax.fori_loop(0, CHUNKS, body, 0)

    high = x >= NX // 2

    @pl.when((x == 0) | (x == NX - 1))
    def _():
        n = jnp.where(high, 1, 0)
        planes((yo, n), (zo, 3 * n))

    @pl.when((x == 1) | (x == NX - 2))
    def _():
        planes((yi, x - 1), (zo, jnp.where(high, 2, 1)))

    @pl.when((x > 1) & (x < NX - 2))
    def _():
        planes((yi, x - 1), (zi, x - 2))


def final(w, b, yo, yi, zo, zi):
    block = pl.BlockSpec((F, 1, NY, NZ), lambda x: (0, x, 0, 0))
    return pl.pallas_call(
        final_kernel,
        grid=(NX,),
        out_shape=(
            jax.ShapeDtypeStruct((F, NX, NY, NZ), jnp.float32),
            jax.ShapeDtypeStruct((F, NX, NY, NZ), jnp.float32),
        ),
        in_specs=[VM] * 6,
        out_specs=(block, block),
        scratch_shapes=[pltpu.VMEM((32, 8, 128), jnp.float32)],
        compiler_params=params(),
        cost_estimate=cost(5),
        name="final",
    )(w, b, yo, yi, zo, zi)


def exchange(x, sizes, partner):
    nx, ny = sizes
    pairs = []
    for a in range(nx):
        for c in range(ny):
            ta, tc = partner(a, c)
            if 0 <= ta < nx and 0 <= tc < ny:
                pairs.append((a * ny + c, ta * ny + tc))
    return lax.ppermute(x, AXES, pairs)


def shards(sizes, adjoint_source, conductivity, electrodes):
    nx, ny = sizes
    current = math.sqrt(nx * NX * ny * NY * NZ)
    l1, g0, g1 = pack(current, adjoint_source, conductivity, electrodes)
    rl1 = exchange(l1, sizes, lambda a, c: (a + 1 if a % 2 else a - 1, c))
    r0 = exchange(g0, sizes, lambda a, c: (a, c ^ 1))
    r1 = exchange(g1, sizes, lambda a, c: (a, c + 1 if c % 2 else c - 1))
    b, h, accb = load_fields(current, adjoint_source, conductivity, electrodes)
    ye, l2, intra = edge(b, h, r0, r1)
    rl2 = exchange(l2, sizes, lambda a, c: (a + 1 if a % 2 else a - 1, c))
    rin = exchange(intra, sizes, lambda a, c: (a ^ 1, c))
    yi, zi, acc, yrows, hrows = inner(b, h, r0, r1)
    yo, zo, msg = outer(b, h, rl1, rl2, rin, r0, r1, ye, yi, accb, acc, yrows, hrows)
    sent = jnp.broadcast_to(msg[0:1][None], (nx * ny, 1, 128))
    w = lax.all_to_all(sent, AXES, 0, 0).reshape(nx * ny, 128)
    return final(w, b, yo, yi, zo, zi)


def solution(mesh):
    sizes = (mesh.shape["gx"], mesh.shape["gy"])
    placed = (P(None, "gx", "gy", None), P("gx", "gy", None), P())
    return jax.shard_map(
        functools.partial(shards, sizes),
        mesh=mesh,
        in_specs=placed,
        out_specs=(P(None, "gx", "gy", None), P(None, "gx", "gy", None)),
        check_vma=False,
    )
```

time: 457 us -> 69.6 us (0.15); the launches traced: 452 us -> 69.4 us
  blocking collectives: 199 us -> 24.3 us
  matrix products: 123 us -> 0 us
  other arithmetic: 53.3 us -> 0 us
  Pallas kernels: 0 us -> 25.8 us
  local copies, waits for them, and re-layouts: 29.3 us -> 4.12 us
  starting transfers between devices: 30.7 us -> 10.1 us
  waiting for transfers between devices: 15.1 us -> 4.32 us
    psum x3 -> x0, blocking collectives: 199 us -> none  [the longest x2 133 us: residual_norm(): return lax.psum(gram(residual, residual), ('gx', 'gy'))]
    dot_general x9 -> x0, matrix products: 122 us -> none  [the longest x4 73.7 us: gram(): jnp.einsum('ixyz,jxyz->ij', left, right, precision=lax.Precision.HIGHEST)]
    pallas_call x0 -> x6, Pallas kernels: none -> 25.8 us  [the longest x1 9.39 us: inner(): pl.pallas_call(inner_kernel, out_shape=(f32(F, NX - 2, NY, NZ), f32(F, NX...]
    concatenate x5 -> x0, other arithmetic: 24.7 us -> none  [with_halo(): block = jnp.concatenate([low, block, high], axis=dim)]
    all_to_all x0 -> x1, blocking collectives: none -> 24.3 us  [shards(): w = lax.all_to_all(sent, AXES, 0, 0).reshape(nx * ny, 128)]
    ppermute x12 -> x5, starting transfers between devices: 30.7 us -> 10.1 us  [exchange(): return lax.ppermute(x, AXES, pairs)]
    add x5 -> x0, other arithmetic: 20.5 us -> none  [the longest x2 20.2 us: apply_operator(): total = total + coeff[None] * (center - other)]
    unnamed x38 -> x6, local copies, waits for them, and re-layouts: 17.5 us -> 4.06 us
  transfers between devices with their start and end apart: 12 -> 5, of which waited for: 4 -> 2; matrix products, arithmetic and copies ran while one was open for 8% -> 0% of each run, Pallas kernels for 0% -> 16%
where the time goes in v1:
time: 69.6 us; the launch traced here: 69.4 us
  Pallas kernels  25.8 us (37%)
  blocking collectives  24.3 us (35%)
  starting transfers between devices  10.1 us (15%)
  waiting for transfers between devices  4.32 us (6%)
  local copies, waits for them, and re-layouts  4.12 us (6%)
  between operations  0.71 us (1%)
    all_to_all x1, blocking collectives, shards(): w = lax.all_to_all(sent, AXES, 0, 0).reshape(nx * ny, 128)  24.3 us
    ppermute x5, starting transfers between devices, exchange(): return lax.ppermute(x, AXES, pairs)  10.1 us
    pallas_call x1, Pallas kernels, inner(): pl.pallas_call(inner_kernel, out_shape=(f32(F, NX - 2, NY, NZ), f32(F, NX...  9.39 us
    pallas_call x1, Pallas kernels, final(): pl.pallas_call(final_kernel, grid=(NX,), out_shape=(jax.ShapeDtypeStruct(...  7.59 us
    ppermute x5, waiting for transfers between devices, exchange(): return lax.ppermute(x, AXES, pairs)  4.32 us
    pallas_call x1, Pallas kernels, outer(): pl.pallas_call(outer_kernel, out_shape=(f32(F, 2, NY, NZ), f32(F, 4, NY,...  4.21 us
    unnamed x6, local copies, waits for them, and re-layouts  4.06 us
    pallas_call x1, Pallas kernels, edge(): pl.pallas_call(edge_kernel, out_shape=(f32(F, 2, NY, NZ), f32(L2_ROWS, NZ...  1.76 us
  transfers between devices with their start and end apart: 5, of which 2 were waited for; matrix products, arithmetic and copies ran while one was open for 0% of the time, Pallas kernels for 16%

profile of v1, /device:TPU:1, one launch (start us, length us, event | category | flops | bytes accessed | tf_op | source)
XLA Modules:
  0.0 69.4 jit_solution(11434758530903677836)
XLA Ops:
  0.6 0.0 copy-start
  0.6 2.2 %copy-done = f32[4,8,64,512]{3,2,1,0:T(8,128)S(1)} copy-done((f32[4,8,64,512]{3,2,1,0:T(8,128)S(1)}, f32[4,8,64,512]{3,2,1,0:T(8,128)}, u32[]{:S(2)}) %copy-start) | copy-done | bytes 4194328
  2.8 0.0 copy-start.1
  2.8 1.2 %copy-done.1 = f32[8,64,512]{2,1,0:T(8,128)S(1)} copy-done((f32[8,64,512]{2,1,0:T(8,128)S(1)}, f32[8,64,512]{2,1,0:T(8,128)}, u32[]{:S(2)}) %copy-start.1) | copy-done | bytes 1048600
  4.0 0.0 copy-start.2
  4.0 0.7 copy-done.2
  4.7 1.5 %pack.1 = (f32[320,512]{1,0:T(8,128)S(1)}, f32[72,512]{1,0:T(8,128)S(1)}, f32[72,512]{1,0:T(8,128)S(1)}) custom-call(f32[4,8,64,512]{3,2,1,0:T(8,128)S(1)} %copy-done, f32[8,64,512]{2,1,0:T(8,128)S(1)} %copy-done.1, s32[4]{0:T(128)S(1)} %copy-done.2), custom_call_target="tpu_custom_call" | custom-call | flops 8000000 | bytes 6000000 | tf_op jit(solution)/shard_map/pack/pallas_call | solution.py:169
  6.2 2.5 %collective-permute-start.1 = (f32[72,512]{1,0:T(8,128)S(1)}, f32[72,512]{1,0:T(8,128)S(1)}, u32[]{:S(2)}, u32[]{:S(2)}) collective-permute-start(f32[72,512]{1,0:T(8,128)S(1)} %get-tuple-element.22), channel_id=1, source_target_pairs={{0,1},{1,0},{2,3},{3,2},{4,5},{5,4},{6,7},{7,6},{8,9},{9,8},{10,11... | collective-permute-start | bytes 442376 | tf_op jit(solution)/shard_map/ppermute | solution.py:658
  8.7 0.7 collective-permute-start.2
  9.4 1.4 %load.1 = (f32[4,8,64,512]{3,2,1,0:T(8,128)S(1)}, f32[8,64,512]{2,1,0:T(8,128)S(1)}, f32[10,8,128]{2,1,0:T(8,128)S(1)}) custom-call(f32[4,8,64,512]{3,2,1,0:T(8,128)S(1)} %copy-done, f32[8,64,512]{2,1,0:T(8,128)S(1)} %copy-done.1, s32[4]{0:T(128)S(1)} %copy-done.2), custom_call_target="tpu_custom_call" | custom-call | flops 12000000 | bytes 9000000 | tf_op jit(solution)/shard_map/load/pallas_call | solution.py:218
  10.8 1.4 %collective-permute-done.1.r0 = f32[72,512]{1,0:T(8,128)S(1)} collective-permute-done((f32[72,512]{1,0:T(8,128)S(1)}, f32[72,512]{1,0:T(8,128)S(1)}, u32[]{:S(2)}, u32[]{:S(2)}) %collective-permute-start.1) | collective-permute-done | bytes 147488 | tf_op jit(solution)/shard_map/ppermute | solution.py:658
  12.2 0.0 collective-permute-done.2.r1
  12.3 1.8 %edge.1 = (f32[4,2,64,512]{3,2,1,0:T(8,128)S(1)}, f32[272,512]{1,0:T(8,128)S(1)}, f32[592,512]{1,0:T(8,128)S(1)}) custom-call(f32[4,8,64,512]{3,2,1,0:T(8,128)S(1)} %get-tuple-element.19.b, f32[8,64,512]{2,1,0:T(8,128)S(1)} %get-tuple-element.20.h, f32[72,512]{1,0:T(8,128)S(1)} %collective-permute-done.1.r0, f32[72,512]{1,0:T(8,128)S(1)} %collective-permute-done.2.r1), custom_call_target="tpu_custom_call" | custom-call | flops 12000000 | bytes 9000000 | tf_op jit(solution)/shard_map/edge/pallas_call | solution.py:300
  14.0 1.4 %collective-permute-start.4 = (f32[592,512]{1,0:T(8,128)S(1)}, f32[592,512]{1,0:T(8,128)S(1)}, u32[]{:S(2)}, u32[]{:S(2)}) collective-permute-start(f32[592,512]{1,0:T(8,128)S(1)} %get-tuple-element.25), channel_id=1, source_target_pairs={{0,4},{1,5},{2,6},{3,7},{4,0},{5,1},{6,2},{7,3},{8,12},{9,13},{10,... | collective-permute-start | bytes 3637256 | tf_op jit(solution)/shard_map/ppermute | solution.py:658
  15.4 3.0 %collective-permute-start = (f32[320,512]{1,0:T(8,128)S(1)}, f32[320,512]{1,0:T(8,128)S(1)}, u32[]{:S(2)}, u32[]{:S(2)}) collective-permute-start(f32[320,512]{1,0:T(8,128)S(1)} %get-tuple-element.21), channel_id=1, source_target_pairs={{4,8},{5,9},{6,10},{7,11},{8,4},{9,5},{10,6},{11,7},{12,16},{13,17... | collective-permute-start | bytes 1966088 | tf_op jit(solution)/shard_map/ppermute | solution.py:658
  18.4 2.5 %collective-permute-start.3 = (f32[272,512]{1,0:T(8,128)S(1)}, f32[272,512]{1,0:T(8,128)S(1)}, u32[]{:S(2)}, u32[]{:S(2)}) collective-permute-start(f32[272,512]{1,0:T(8,128)S(1)} %get-tuple-element.24), channel_id=1, source_target_pairs={{4,8},{5,9},{6,10},{7,11},{8,4},{9,5},{10,6},{11,7},{12,16},{13,17... | collective-permute-start | bytes 1671176 | tf_op jit(solution)/shard_map/ppermute | solution.py:658
  20.9 9.4 %inner.1 = (f32[4,6,64,512]{3,2,1,0:T(8,128)S(1)}, f32[4,4,64,512]{3,2,1,0:T(8,128)S(1)}, f32[30,8,128]{2,1,0:T(8,128)S(1)}, f32[2,4,8,512]{3,2,1,0:T(8,128)S(1)}, f32[2,8,512]{2,1,0:T(8,128)S(1)}) custom-call(f32[4,8,64,512]{3,2,1,0:T(8,128)S(1)} %get-tuple-element.19.b, f32[8,64,512]{2,1,0:T(8,128)S(1)} %get-tuple-element.20.h, ...), custom_call_target="tpu_custom_call" | custom-call | flops 32000000 | bytes 24000000 | tf_op jit(solution)/shard_map/inner/pallas_call | solution.py:398
  30.3 0.0 collective-permute-done.rl1
  30.3 2.9 %collective-permute-done.3.rl2 = f32[272,512]{1,0:T(8,128)S(1)} collective-permute-done((f32[272,512]{1,0:T(8,128)S(1)}, f32[272,512]{1,0:T(8,128)S(1)}, u32[]{:S(2)}, u32[]{:S(2)}) %collective-permute-start.3) | collective-permute-done | bytes 557088 | tf_op jit(solution)/shard_map/ppermute | solution.py:658
  33.2 0.0 collective-permute-done.4.rin
  33.2 4.2 %outer.1 = (f32[4,2,64,512]{3,2,1,0:T(8,128)S(1)}, f32[4,4,64,512]{3,2,1,0:T(8,128)S(1)}, f32[8,128]{1,0:T(8,128)S(1)}) custom-call(f32[4,8,64,512]{3,2,1,0:T(8,128)S(1)} %get-tuple-element.19.b, f32[8,64,512]{2,1,0:T(8,128)S(1)} %get-tuple-element.20.h, f32[320,512]{1,0:T(8,128)S(1)} %collective-permute-done.rl1, ...), custom_call_target="tpu_custom_call" | custom-call | flops 20000000 | bytes 15000000 | tf_op jit(solution)/shard_map/outer/pallas_call | solution.py:491
  37.5 0.1 broadcast_in_dim.9
  37.5 24.3 %all_to_all.5 = f32[128,1,128]{2,1,0:T(1,128)S(1)} all-to-all(f32[128,1,128]{2,1,0:T(1,128)S(1)} %broadcast_in_dim.9), channel_id=1, replica_groups=mesh['gx'=32,'gy'=4] {'gx','gy'}, dimensions={0} | all-to-all | bytes 131072 | tf_op jit(solution)/shard_map/all_to_all | solution.py:675
  61.8 7.6 %final.1 = (f32[4,8,64,512]{3,2,1,0:T(8,128)}, f32[4,8,64,512]{3,2,1,0:T(8,128)}) custom-call(f32[128,128]{1,0:T(8,128)S(1)} %bitcast.3, f32[4,8,64,512]{3,2,1,0:T(8,128)S(1)} %get-tuple-element.19.b, f32[4,2,64,512]{3,2,1,0:T(8,128)S(1)} %get-tuple-element.33.yo, f32[4,6,64,512]{3,2,1,0:T(8,128)S(1)} %get-tuple-element.27.yi, ...), custom_call_target="tpu_custom_call" | custom-call | flops 20000000 | bytes 15000000 | tf_op jit(solution)/shard_map/final/pallas_call | solution.py:634
  (1 shorter events, 0.0 us)
Async XLA Ops:
  0.6 2.2 %copy-start = (f32[4,8,64,512]{3,2,1,0:T(8,128)S(1)}, f32[4,8,64,512]{3,2,1,0:T(8,128)}, u32[]{:S(2)}) copy-start(f32[4,8,64,512]{3,2,1,0:T(8,128)} %adj.3) | copy-start | bytes 12582916
  2.8 1.2 %copy-start.1 = (f32[8,64,512]{2,1,0:T(8,128)S(1)}, f32[8,64,512]{2,1,0:T(8,128)}, u32[]{:S(2)}) copy-start(f32[8,64,512]{2,1,0:T(8,128)} %sigma.3) | copy-start | bytes 3145732
  4.0 0.7 copy-start.2
  6.2 6.1 %collective-permute-start.1 = (f32[72,512]{1,0:T(8,128)S(1)}, f32[72,512]{1,0:T(8,128)S(1)}, u32[]{:S(2)}, u32[]{:S(2)}) collective-permute-start(f32[72,512]{1,0:T(8,128)S(1)} %get-tuple-element.22), channel_id=1, source_target_pairs={{0,1},{1,0},{2,3},{3,2},{4,5},{5,4},{6,7},{7,6},{8,9},{9,8},{10,11... | collective-permute-start | bytes 442376 | tf_op jit(solution)/shard_map/ppermute | solution.py:658
  8.7 3.5 %collective-permute-start.2 = (f32[72,512]{1,0:T(8,128)S(1)}, f32[72,512]{1,0:T(8,128)S(1)}, u32[]{:S(2)}, u32[]{:S(2)}) collective-permute-start(f32[72,512]{1,0:T(8,128)S(1)} %get-tuple-element.23), channel_id=1, source_target_pairs={{1,2},{2,1},{5,6},{6,5},{9,10},{10,9},{13,14},{14,13},{17,18},{18,... | collective-permute-start | bytes 442376 | tf_op jit(solution)/shard_map/ppermute | solution.py:658
  14.0 19.2 %collective-permute-start.4 = (f32[592,512]{1,0:T(8,128)S(1)}, f32[592,512]{1,0:T(8,128)S(1)}, u32[]{:S(2)}, u32[]{:S(2)}) collective-permute-start(f32[592,512]{1,0:T(8,128)S(1)} %get-tuple-element.25), channel_id=1, source_target_pairs={{0,4},{1,5},{2,6},{3,7},{4,0},{5,1},{6,2},{7,3},{8,12},{9,13},{10,... | collective-permute-start | bytes 3637256 | tf_op jit(solution)/shard_map/ppermute | solution.py:658
  15.4 15.0 %collective-permute-start = (f32[320,512]{1,0:T(8,128)S(1)}, f32[320,512]{1,0:T(8,128)S(1)}, u32[]{:S(2)}, u32[]{:S(2)}) collective-permute-start(f32[320,512]{1,0:T(8,128)S(1)} %get-tuple-element.21), channel_id=1, source_target_pairs={{4,8},{5,9},{6,10},{7,11},{8,4},{9,5},{10,6},{11,7},{12,16},{13,17... | collective-permute-start | bytes 1966088 | tf_op jit(solution)/shard_map/ppermute | solution.py:658
  18.4 14.8 %collective-permute-start.3 = (f32[272,512]{1,0:T(8,128)S(1)}, f32[272,512]{1,0:T(8,128)S(1)}, u32[]{:S(2)}, u32[]{:S(2)}) collective-permute-start(f32[272,512]{1,0:T(8,128)S(1)} %get-tuple-element.24), channel_id=1, source_target_pairs={{4,8},{5,9},{6,10},{7,11},{8,4},{9,5},{10,6},{11,7},{12,16},{13,17... | collective-permute-start | bytes 1671176 | tf_op jit(solution)/shard_map/ppermute | solution.py:658

commit v2 on v1

v2 whole, which is shorter than its diff:
```python
import functools
import math

import jax
import jax.numpy as jnp
from jax import lax
from jax.experimental import pallas as pl
from jax.experimental.pallas import tpu as pltpu
from jax.sharding import PartitionSpec as P

AXES = ("gx", "gy")
F = 4
NX = 8
NY = 64
NZ = 512
Q = NZ // 128
CHUNKS = NY // 8
UNROLL = 2
PAIRS = [(i, j) for i in range(F) for j in range(i, F)]
TOP = 8
ROWS = NY + 2 * TOP
PLANE = Q * NY
L1_ROWS = (F + 1) * PLANE
CORNER = 24
L2_ROWS = F * PLANE + 2 * CORNER
IN_ROWS = L1_ROWS + L2_ROWS
TILE_ROWS = (F + 1) * Q * 8
G_ROWS = TILE_ROWS + F * Q * 8
VMEM_LIMIT = 16 * 1024 * 1024

VM = pl.BlockSpec(memory_space=pltpu.VMEM)
HBM = pl.BlockSpec(memory_space=pltpu.HBM)


def f32(*shape):
    return pltpu.VMEM(shape, jnp.float32)


def params():
    return pltpu.CompilerParams(vmem_limit_bytes=VMEM_LIMIT)


def cost(us):
    return pl.CostEstimate(flops=int(us * 4e6), bytes_accessed=int(us * 3.0e6), transcendentals=0)


def in_hbm(*arrays):
    return tuple(pltpu.with_memory_space_constraint(a, pltpu.HBM) for a in arrays)


def iota(dim):
    return lax.broadcasted_iota(jnp.int32, (8, 128), dim)


def inside(h_other, h):
    return jnp.where(h_other > 0.0, h_other, h)


def above_z(v):
    t = [pltpu.roll(a, 127, 1) for a in v]
    last = iota(1) == 127
    return [jnp.where(last, t[q + 1], t[q]) if q < Q - 1 else t[q] for q in range(Q)]


def below_z(v):
    t = [pltpu.roll(a, 1, 1) for a in v]
    first = iota(1) == 0
    return [jnp.where(first, t[q - 1], t[q]) if q > 0 else t[q] for q in range(Q)]


def z_coeffs(h):
    up = [a + b for a, b in zip(h, above_z(h))]
    edge = iota(1) == 127
    total = up[:-1] + [jnp.where(edge, 2.0 * h[-1], up[-1])]
    up[-1] = jnp.where(edge, 0.0, up[-1])
    down = below_z(up)
    first = jnp.where(iota(1) == 0, 2.0 * h[0], down[0])
    total = [t + d for t, d in zip(total, [first] + down[1:])]
    down[0] = jnp.where(iota(1) == 0, 0.0, down[0])
    return up, down, total


def add_gram(acc, base, left, right):
    for n, (i, j) in enumerate(PAIRS):
        t = left[i][0] * right[j][0]
        for q in range(1, Q):
            t = t + left[i][q] * right[j][q]
        acc[base + n] += t


def chunk_loop(body):
    def step(i, carry):
        for u in range(UNROLL):
            body(pl.multiple_of(i * (8 * UNROLL), 8) + 8 * u)
        return carry

    lax.fori_loop(0, CHUNKS // UNROLL, step, 0)


def tiles_of(ref, index, row):
    return [ref[(*index, q, pl.ds(row, 8), slice(None))] for q in range(Q)]


def add_spike(ref, index, row, current):
    tile = ref[(*index, slice(0, 128))]
    ref[(*index, slice(0, 128))] = tile + jnp.where(
        (iota(0) == row) & (iota(1) == 0), current, 0.0
    )


def local_cell(elec, f):
    total_y = NY * lax.axis_size("gy")
    cell = elec[f]
    lx = cell // total_y - lax.axis_index("gx") * NX
    ly = cell % total_y - lax.axis_index("gy") * NY
    return lx, ly, (lx >= 0) & (lx < NX) & (ly >= 0) & (ly < NY)


def pack_kernel(
    current, adj, sigma, elec_in, l1_out, g0_out, g1_out, own_out, plane, tiles, far_rows, elec, sems, esem
):
    par = lax.axis_index("gx") % 2
    ypar = lax.axis_index("gy") % 2
    edge = par * (NX - 1)
    ecopy = pltpu.make_async_copy(elec_in, elec, esem)
    ecopy.start()
    copies = []
    for f in range(F + 1):
        src = adj.at[f] if f < F else sigma
        copies.append(pltpu.make_async_copy(src.at[edge], plane.at[f], sems.at[0, f]))
        for side, y in ((0, 0), (1, NY - 8)):
            copies.append(
                pltpu.make_async_copy(
                    src.at[:, pl.ds(y, 8), :], tiles.at[f, side], sems.at[1 + side, f]
                )
            )
    for c in copies:
        c.start()
    ecopy.wait()
    for c in copies:
        c.wait()
    for f in range(F):
        lx, ly, here = local_cell(elec, f)

        @pl.when(here & (lx == edge))
        def _(f=f, ly=ly):
            r8 = pl.multiple_of((ly // 8) * 8, 8)
            add_spike(plane, (f, pl.ds(r8, 8)), ly - r8, current)

        @pl.when(here & (ly < 8))
        def _(f=f, lx=lx, ly=ly):
            add_spike(tiles, (f, 0, lx, slice(0, 8)), ly, current)

        @pl.when(here & (ly >= NY - 8))
        def _(f=f, lx=lx, ly=ly):
            add_spike(tiles, (f, 1, lx, slice(0, 8)), ly - (NY - 8), current)

    for f in range(F + 1):
        k = 1.0 if f < F else 0.5
        for q in range(Q):
            s = slice(q * 128, q * 128 + 128)
            a = (f * Q + q) * NY
            l1_out[a : a + NY, :] = k * plane[f, :, s]
            for x in range(NX):
                a = (f * Q + q) * 8 + x
                for side, (near, far) in enumerate(((0, 1), (7, 6))):
                    own_out[side, a : a + 1, :] = k * tiles[f, side, x, near : near + 1, s]
                    far_rows[side, a : a + 1, :] = k * tiles[f, side, x, far : far + 1, s]
    for f in range(F + 1):
        for q in range(Q):
            t = slice((f * Q + q) * 8, (f * Q + q) * 8 + 8)
            lo, hi = own_out[0, t, :], own_out[1, t, :]
            g0_out[t, :] = jnp.where(ypar == 0, hi, lo)
            g1_out[t, :] = jnp.where(ypar == 0, lo, hi)
            if f < F:
                ht = slice((F * Q + q) * 8, (F * Q + q) * 8 + 8)
                lo = (own_out[0, ht, :] + far_rows[0, ht, :]) * (lo - far_rows[0, t, :])
                hi = (own_out[1, ht, :] + far_rows[1, ht, :]) * (hi - far_rows[1, t, :])
                d = slice(TILE_ROWS + (f * Q + q) * 8, TILE_ROWS + (f * Q + q) * 8 + 8)
                g0_out[d, :] = jnp.where(ypar == 0, hi, lo)
                g1_out[d, :] = jnp.where(ypar == 0, lo, hi)


def pack(current, adj, sigma, electrodes):
    return pl.pallas_call(
        functools.partial(pack_kernel, current),
        out_shape=(
            f32(L1_ROWS, 128),
            f32(G_ROWS, 128),
            f32(G_ROWS, 128),
            f32(2, TILE_ROWS, 128),
        ),
        in_specs=[HBM] * 3,
        out_specs=(VM,) * 4,
        scratch_shapes=[
            pltpu.VMEM((F + 1, NY, NZ), jnp.float32),
            pltpu.VMEM((F + 1, 2, NX, 8, NZ), jnp.float32),
            pltpu.VMEM((2, TILE_ROWS, 128), jnp.float32),
            pltpu.SMEM((F,), jnp.int32),
            pltpu.SemaphoreType.DMA((3, F + 1)),
            pltpu.SemaphoreType.DMA,
        ],
        compiler_params=params(),
        cost_estimate=cost(2),
        name="pack",
    )(*in_hbm(adj, sigma, electrodes))


def load_kernel(current, adj, sigma, elec_in, b_out, h_out, acc, fields, cond, elec, sems, esem):
    ecopy = pltpu.make_async_copy(elec_in, elec, esem)
    ecopy.start()
    copies = [pltpu.make_async_copy(adj.at[f], fields.at[f], sems.at[f]) for f in range(F)]
    copies.append(pltpu.make_async_copy(sigma, cond, sems.at[F]))
    for c in copies:
        c.start()
    ecopy.wait()
    acc[...] = jnp.zeros(acc.shape, jnp.float32)
    for c in copies:
        c.wait()
    for f in range(F):
        lx, ly, here = local_cell(elec, f)

        @pl.when(here)
        def _(f=f, lx=lx, ly=ly):
            r8 = pl.multiple_of((ly // 8) * 8, 8)
            add_spike(fields, (f, lx, pl.ds(r8, 8)), ly - r8, current)

    def plane(x, carry):
        def chunk(r):
            vs = []
            for f in range(F):
                v = [fields[f, x, pl.ds(r, 8), q * 128 : q * 128 + 128] for q in range(Q)]
                for q in range(Q):
                    b_out[f, x, q, pl.ds(r + TOP, 8), :] = v[q]
                vs.append(v)
            for q in range(Q):
                h_out[x + 1, q, pl.ds(r + TOP, 8), :] = (
                    0.5 * cond[x, pl.ds(r, 8), q * 128 : q * 128 + 128]
                )
            add_gram(acc, 0, vs, vs)

        chunk_loop(chunk)
        return carry

    lax.fori_loop(0, NX, plane, 0)


def load_fields(current, adj, sigma, electrodes):
    return pl.pallas_call(
        functools.partial(load_kernel, current),
        out_shape=(f32(F, NX, Q, ROWS, 128), f32(NX + 2, Q, ROWS, 128), f32(10, 8, 128)),
        in_specs=[HBM] * 3,
        out_specs=(VM,) * 3,
        scratch_shapes=[
            pltpu.VMEM((F, NX, NY, NZ), jnp.float32),
            pltpu.VMEM((NX, NY, NZ), jnp.float32),
            pltpu.SMEM((F,), jnp.int32),
            pltpu.SemaphoreType.DMA((F + 1,)),
            pltpu.SemaphoreType.DMA,
        ],
        compiler_params=params(),
        cost_estimate=cost(3),
        name="load",
    )(*in_hbm(adj, sigma, electrodes))


def chunk_coeffs(h, k, r, low=True, high=True):
    at = r + TOP
    own = tiles_of(h, (k,), at)
    up, down, total = z_coeffs(own)
    faces = [(None, up), (None, down)]
    others = [((0, 1), tiles_of(h, (k,), at + 1)), ((0, -1), tiles_of(h, (k,), at - 1))]
    if low:
        others.append(((-1, 0), tiles_of(h, (k - 1,), at)))
    if high:
        others.append(((1, 0), tiles_of(h, (k + 1,), at)))
    for step, other in others:
        c = [a + b for a, b in zip(own, other)]
        total = [a + b for a, b in zip(total, c)]
        faces.append((step, c))
    return total, faces


def chunk_apply(coeffs, v, f, k, r):
    total, faces = coeffs
    at = r + TOP
    own = tiles_of(v, (f, k), at)
    beside = [above_z(own), below_z(own)]
    beside += [tiles_of(v, (f, k + s[0]), at + s[1]) for s, _ in faces[2:]]
    out = []
    for q in range(Q):
        t = total[q] * own[q]
        for (_, c), n in zip(faces, beside):
            t = t - c[q] * n[q]
        out.append(t)
    return own, out


def side_planes(par):
    far = par * (NX - 1)
    near = (NX - 1) - far
    return far, near, par * (NX + 1), (1 - par) * (NX + 1)


def halo_select(ypar, r0, r1, item):
    a = r0[item * 8 : item * 8 + 8, :]
    b = r1[item * 8 : item * 8 + 8, :]
    return jnp.where(ypar == 0, b, a), jnp.where(ypar == 0, a, b)


def edge_kernel(b_in, h_in, own, r0, r1, rl1, b, h, y, l2_out, in_out, g):
    del b_in, h_in
    par = lax.axis_index("gx") % 2
    ypar = lax.axis_index("gy") % 2
    far, near, far_halo, _ = side_planes(par)
    for item in range((F + 1) * Q):
        f, q = divmod(item, Q)
        for side, t in enumerate(halo_select(ypar, r0, r1, item)):
            row = TOP - 1 if side == 0 else TOP + NY
            g[side, item * 8 : item * 8 + 8, :] = t
            if f < F:
                for x in range(NX):
                    b[f, x, q, row : row + 1, :] = g[side, item * 8 + x : item * 8 + x + 1, :]
            else:
                t = inside(t, own[side, item * 8 : item * 8 + 8, :])
                g[2 + side, q * 8 : q * 8 + 8, :] = t
                for x in range(NX):
                    h[x + 1, q, row : row + 1, :] = g[2 + side, q * 8 + x : q * 8 + x + 1, :]
    for x in (0, NX - 1):

        def chunk(r, x=x):
            coeffs = chunk_coeffs(h, x + 1, r, low=x > 0, high=x == 0)
            for f in range(F):
                _, out = chunk_apply(coeffs, b, f, x, r)
                for q in range(Q):
                    y[f, x + 1, q, pl.ds(r + TOP, 8), :] = out[q]

        chunk_loop(chunk)
    data = slice(TOP, TOP + NY)
    for q in range(Q):
        for f in range(F):
            a = (f * Q + q) * NY
            l2_out[a : a + NY, :] = y[f, far + 1, q, data, :]
            in_out[a : a + NY, :] = b[f, near, q, data, :]
            in_out[L1_ROWS + a : L1_ROWS + a + NY, :] = y[f, near + 1, q, data, :]
        a = (F * Q + q) * NY
        in_out[a : a + NY, :] = h[near + 1, q, data, :]
    base = F * PLANE
    l2_out[base:L2_ROWS, :] = jnp.zeros((2 * CORNER, 128), jnp.float32)
    in_out[L1_ROWS + base : IN_ROWS, :] = jnp.zeros((2 * CORNER, 128), jnp.float32)
    for side in range(2):
        for item in range((F + 1) * Q):
            a = base + side * CORNER + item
            l2_out[a : a + 1, :] = g[side, pl.ds(item * 8 + far, 1), :]
            in_out[L1_ROWS + a : L1_ROWS + a + 1, :] = g[side, pl.ds(item * 8 + near, 1), :]
    border(b, h, y, rl1, far, far_halo)


def border(b, h, y, first, x, halo):
    def chunk(r):
        for q in range(Q):
            own = h[x + 1, q, pl.ds(r + TOP, 8), :]
            beyond = inside(first[pl.ds((F * Q + q) * NY + r, 8), :], own)
            h[halo, q, pl.ds(r + TOP, 8), :] = beyond
            c = own + beyond
            for f in range(F):
                v = b[f, x, q, pl.ds(r + TOP, 8), :]
                flux = c * (v - first[pl.ds((f * Q + q) * NY + r, 8), :])
                at = (f, x + 1, q, pl.ds(r + TOP, 8), slice(None))
                y[at] = y[at] + flux

    chunk_loop(chunk)


def edge(b, h, own, r0, r1, rl1):
    return pl.pallas_call(
        edge_kernel,
        out_shape=(
            f32(F, NX, Q, ROWS, 128),
            f32(NX + 2, Q, ROWS, 128),
            f32(F, NX + 2, Q, ROWS, 128),
            f32(L2_ROWS, 128),
            f32(IN_ROWS, 128),
        ),
        in_specs=[VM] * 6,
        out_specs=(VM,) * 5,
        input_output_aliases={0: 0, 1: 1},
        scratch_shapes=[pltpu.VMEM((4, TILE_ROWS, 128), jnp.float32)],
        compiler_params=params(),
        cost_estimate=cost(10),
        name="edge",
    )(b, h, own, r0, r1, rl1)


def row_halo(own, rh, side, y, tmp):
    count = lax.axis_size("gy")
    ay = lax.axis_index("gy")
    valid = ay > 0 if side == 0 else ay < count - 1
    row = TOP - 1 if side == 0 else TOP + NY
    sub = iota(0)
    own_at = lambda f, q: own[side, (f * Q + q) * 8 : (f * Q + q) * 8 + 8, :]
    h_r = [rh(F * Q + q) for q in range(Q)]
    zu, zd, total = z_coeffs(h_r)
    across = [h_r[q] + own_at(F, q) for q in range(Q)]
    up = [jnp.where(sub == NX - 1, 0.0, a + pltpu.roll(a, 7, 0)) for a in h_r]
    down = [jnp.where(sub == 0, 0.0, a + pltpu.roll(a, 1, 0)) for a in h_r]
    total = [sum(t) for t in zip(total, across, up, down)]
    for f in range(F):
        v = [rh(f * Q + q) for q in range(Q)]
        zp, zm = above_z(v), below_z(v)
        for q in range(Q):
            out = total[q] * v[q] + rh((F + 1 + f) * Q + q) - across[q] * own_at(f, q)
            out = out - up[q] * pltpu.roll(v[q], 7, 0) - down[q] * pltpu.roll(v[q], 1, 0)
            out = out - zu[q] * zp[q] - zd[q] * zm[q]
            tmp[side, f, q] = jnp.where(valid, out, 0.0)
            for x in range(NX):
                y[f, x + 1, q, row : row + 1, :] = tmp[side, f, q, x : x + 1, :]


def z_plane(h, y, z, acc, x):
    def chunk(r):
        coeffs = chunk_coeffs(h, x + 1, r)
        vs, outs = [], []
        for f in range(F):
            v, out = chunk_apply(coeffs, y, f, x + 1, r)
            for q in range(Q):
                z[f, x, q, pl.ds(r, 8), :] = out[q] - v[q]
            vs.append(v)
            outs.append(out)
        add_gram(acc, 20, vs, outs)

    chunk_loop(chunk)


def edge_grams(b, y, acc, x):
    def chunk(r):
        vs = [tiles_of(b, (f, x), r + TOP) for f in range(F)]
        outs = [tiles_of(y, (f, x + 1), r + TOP) for f in range(F)]
        add_gram(acc, 0, vs, outs)
        add_gram(acc, 10, outs, outs)

    chunk_loop(chunk)


def inner_kernel(b, h, own, r0, r1, y_in, y, z, acc, tmp):
    del y_in
    par = lax.axis_index("gx") % 2
    ypar = lax.axis_index("gy") % 2
    far = side_planes(par)[0]
    acc[...] = jnp.zeros(acc.shape, jnp.float32)
    for side in range(2):
        row_halo(own, lambda item: halo_select(ypar, r0, r1, item)[side], side, y, tmp)

    def y_plane(x, carry):
        def chunk(r):
            coeffs = chunk_coeffs(h, x + 1, r)
            vs, outs = [], []
            for f in range(F):
                v, out = chunk_apply(coeffs, b, f, x, r)
                for q in range(Q):
                    y[f, x + 1, q, pl.ds(r + TOP, 8), :] = out[q]
                vs.append(v)
                outs.append(out)
            add_gram(acc, 0, vs, outs)
            add_gram(acc, 10, outs, outs)

        chunk_loop(chunk)
        return carry

    lax.fori_loop(1, NX - 1, y_plane, 0)
    edge_grams(b, y, acc, far)

    def z_loop(n, carry):
        z_plane(h, y, z, acc, jnp.where(par == 0, n, NX - 1 - n))
        return carry

    lax.fori_loop(1, NX - 2, z_loop, 0)


def inner(b, h, own, r0, r1, y):
    return pl.pallas_call(
        inner_kernel,
        out_shape=(
            f32(F, NX + 2, Q, ROWS, 128),
            f32(F, NX, Q, NY, 128),
            f32(30, 8, 128),
        ),
        in_specs=[VM] * 6,
        out_specs=(VM,) * 3,
        input_output_aliases={5: 0},
        scratch_shapes=[pltpu.VMEM((2, F, Q, 8, 128), jnp.float32)],
        compiler_params=params(),
        cost_estimate=cost(6),
        name="inner",
    )(b, h, own, r0, r1, y)


def halo_image(b, h, y, first, second, s0, x, halo):
    count_x, count_y = lax.axis_size("gx"), lax.axis_size("gy")
    ax, ay = lax.axis_index("gx"), lax.axis_index("gy")
    valid = jnp.where(x == 0, ax > 0, ax < count_x - 1)

    def chunk(r):
        for q in range(Q):
            c = h[x + 1, q, pl.ds(r + TOP, 8), :] + h[halo, q, pl.ds(r + TOP, 8), :]
            for f in range(F):
                a = (f * Q + q) * NY + r
                flux = c * (b[f, x, q, pl.ds(r + TOP, 8), :] - first[pl.ds(a, 8), :])
                other = second[pl.ds(s0 + a, 8), :] - flux
                y[f, halo, q, pl.ds(r + TOP, 8), :] = jnp.where(valid, other, 0.0)

    chunk_loop(chunk)
    for side in range(2):
        row = TOP - 1 if side == 0 else TOP + NY
        valid_row = ay > 0 if side == 0 else ay < count_y - 1
        base = s0 + F * PLANE + side * CORNER
        for q in range(Q):
            h_r = h[x + 1, q, row : row + 1, :]
            a = base + F * Q + q
            c = h_r + inside(second[a : a + 1, :], h_r)
            for f in range(F):
                v = b[f, x, q, row : row + 1, :]
                a = base + f * Q + q
                flux = jnp.where(valid_row, c * (v - second[a : a + 1, :]), 0.0)
                y[f, x + 1, q, row : row + 1, :] = y[f, x + 1, q, row : row + 1, :] + flux


def near_kernel(b, h_in, rin, y_in, z_in, acc_in, h, y, z, acc):
    del h_in, y_in, z_in
    par = lax.axis_index("gx") % 2
    _, near, _, halo = side_planes(par)
    acc[...] = acc_in[...]
    border(b, h, y, rin, near, halo)
    halo_image(b, h, y, rin, rin, L1_ROWS, near, halo)
    edge_grams(b, y, acc, near)

    def z_loop(n, carry):
        z_plane(h, y, z, acc, jnp.where(par == 0, n, NX - 1 - n))
        return carry

    lax.fori_loop(NX - 2, NX, z_loop, 0)


def near_side(b, h, rin, y, z, acc):
    return pl.pallas_call(
        near_kernel,
        out_shape=(
            f32(NX + 2, Q, ROWS, 128),
            f32(F, NX + 2, Q, ROWS, 128),
            f32(F, NX, Q, NY, 128),
            f32(30, 8, 128),
        ),
        in_specs=[VM] * 6,
        out_specs=(VM,) * 4,
        input_output_aliases={1: 0, 3: 1, 4: 2},
        compiler_params=params(),
        cost_estimate=cost(3),
        name="near",
    )(b, h, rin, y, z, acc)


def far_kernel(b, h, rl1, rl2, y_in, z_in, accb, acc_in, y, z, msg, acc):
    del y_in, z_in
    par = lax.axis_index("gx") % 2
    far, _, halo, _ = side_planes(par)
    acc[...] = acc_in[...]
    halo_image(b, h, y, rl1, rl2, 0, far, halo)
    z_plane(h, y, z, acc, far)
    sums = jnp.concatenate(
        [jnp.sum(accb[k], axis=0, keepdims=True) for k in range(10)]
        + [jnp.sum(acc[k], axis=0, keepdims=True) for k in range(30)]
        + [jnp.zeros((88, 128), jnp.float32)],
        axis=0,
    )
    msg[...] = lax.dot_general(
        jnp.ones((8, 128), jnp.float32),
        sums,
        (((1,), (1,)), ((), ())),
        precision=lax.Precision.HIGHEST,
        preferred_element_type=jnp.float32,
    )


def far_side(b, h, rl1, rl2, y, z, accb, acc):
    return pl.pallas_call(
        far_kernel,
        out_shape=(f32(F, NX + 2, Q, ROWS, 128), f32(F, NX, Q, NY, 128), f32(8, 128)),
        in_specs=[VM] * 8,
        out_specs=(VM,) * 3,
        input_output_aliases={4: 0, 5: 1},
        scratch_shapes=[pltpu.VMEM((30, 8, 128), jnp.float32)],
        compiler_params=params(),
        cost_estimate=cost(3),
        name="far",
    )(b, h, rl1, rl2, y, z, accb, acc)


def mm(a, b, ta=False):
    at = (lambda i, k: a[k][i]) if ta else (lambda i, k: a[i][k])
    return [
        [sum((at(i, k) * b[k][j] for k in range(1, F)), at(i, 0) * b[0][j]) for j in range(F)]
        for i in range(F)
    ]


def add(a, b, s=1.0):
    return [[a[i][j] + s * b[i][j] for j in range(F)] for i in range(F)]


def symmetric(a):
    return [[a[i][j] if i == j else 0.5 * (a[i][j] + a[j][i]) for j in range(F)] for i in range(F)]


def spd_solve(a, b):
    low = [[None] * F for _ in range(F)]
    d, inv = [None] * F, [None] * F
    for j in range(F):
        t = a[j][j]
        for k in range(j):
            t = t - low[j][k] * low[j][k] * d[k]
        d[j] = t
        inv[j] = 1.0 / t
        for i in range(j + 1, F):
            t = a[i][j]
            for k in range(j):
                t = t - low[i][k] * low[j][k] * d[k]
            low[i][j] = t * inv[j]
    x = [list(row) for row in b]
    for i in range(F):
        for k in range(i):
            for j in range(F):
                x[i][j] = x[i][j] - low[i][k] * x[k][j]
    for i in range(F):
        x[i] = [e * inv[i] for e in x[i]]
    for i in reversed(range(F)):
        for k in range(i + 1, F):
            for j in range(F):
                x[i][j] = x[i][j] - low[k][i] * x[k][j]
    return x


def step_matrices(entry):
    grams = []
    for g in range(4):
        m = [[None] * F for _ in range(F)]
        for n, (i, j) in enumerate(PAIRS):
            m[i][j] = m[j][i] = entry(10 * g + n)
        grams.append(m)
    bb, by, yy, yz = grams
    alpha = spd_solve(by, bb)
    new = symmetric(add(mm(alpha, mm(yy, alpha), ta=True), bb, -1.0))
    beta = spd_solve(bb, new)
    e = [[beta[i][j] + 1.0 if i == j else beta[i][j] for j in range(F)] for i in range(F)]
    cross = mm(e, mm(yy, alpha), ta=True)
    curv = add(mm(e, mm(by, e), ta=True), mm(alpha, mm(yz, alpha), ta=True))
    curv = [[curv[i][j] - cross[i][j] - cross[j][i] for j in range(F)] for i in range(F)]
    alpha2 = spd_solve(symmetric(curv), new)
    m1 = add(alpha, mm(e, alpha2))
    m2 = mm(alpha, alpha2)
    return m1, m2


def final_kernel(w, b, y, d, xs_out, res_out, coef):
    x = pl.program_id(0)

    @pl.when(x == 0)
    def _():
        total = jnp.sum(w[...], axis=0, keepdims=True)
        sub = lax.broadcasted_iota(jnp.int32, (128, 128), 0)
        lane = lax.broadcasted_iota(jnp.int32, (128, 128), 1)
        spread = lax.dot_general(
            jnp.where(sub == lane, total, 0.0),
            jnp.ones((128, 128), jnp.float32),
            (((1,), (0,)), ((), ())),
            precision=lax.Precision.HIGHEST,
            preferred_element_type=jnp.float32,
        )
        m1, m2 = step_matrices(lambda k: spread[k : k + 1, :])
        for i in range(F):
            for j in range(F):
                n = i * F + j
                coef[n] = jnp.broadcast_to(m1[i][j], (8, 128))
                coef[16 + n] = jnp.broadcast_to(m2[i][j], (8, 128))
                coef[32 + n] = jnp.broadcast_to(m1[i][j] - m2[i][j], (8, 128))

    def body(i, carry):
        r = pl.multiple_of(i * 8, 8)
        for q in range(Q):
            bs = [b[f, x, q, pl.ds(r + TOP, 8), :] for f in range(F)]
            ys = [y[f, x + 1, q, pl.ds(r + TOP, 8), :] for f in range(F)]
            ds = [d[f, x, q, pl.ds(r, 8), :] for f in range(F)]
            es = [bs[f] - ys[f] for f in range(F)]
            for j in range(F):
                p = ys[0] * coef[32 + j]
                for k in range(1, F):
                    p = p + ys[k] * coef[32 + k * F + j]
                ro = bs[j] - p
                for k in range(F):
                    p = p + es[k] * coef[k * F + j]
                    ro = ro + ds[k] * coef[16 + k * F + j]
                s = slice(q * 128, q * 128 + 128)
                xs_out[j, 0, pl.ds(r, 8), s] = p
                res_out[j, 0, pl.ds(r, 8), s] = ro
        return carry

    lax.fori_loop(0, CHUNKS, body, 0)


def final(w, b, y, d):
    block = pl.BlockSpec((F, 1, NY, NZ), lambda x: (0, x, 0, 0))
    out = jax.ShapeDtypeStruct((F, NX, NY, NZ), jnp.float32)
    return pl.pallas_call(
        final_kernel,
        grid=(NX,),
        out_shape=(out, out),
        in_specs=[VM] * 4,
        out_specs=(block, block),
        scratch_shapes=[pltpu.VMEM((48, 8, 128), jnp.float32)],
        compiler_params=params(),
        cost_estimate=cost(5),
        name="final",
    )(w, b, y, d)


def exchange(x, sizes, partner):
    nx, ny = sizes
    pairs = []
    for a in range(nx):
        for c in range(ny):
            ta, tc = partner(a, c)
            if 0 <= ta < nx and 0 <= tc < ny:
                pairs.append((a * ny + c, ta * ny + tc))
    return lax.ppermute(x, AXES, pairs)


def shards(sizes, adjoint_source, conductivity, electrodes):
    nx, ny = sizes
    current = math.sqrt(nx * NX * ny * NY * NZ)
    border_pair = lambda a, c: (a + 1 if a % 2 else a - 1, c)
    inputs = (current, adjoint_source, conductivity, electrodes)
    l1, g0, g1, own = pack(*inputs)
    rl1 = exchange(l1, sizes, border_pair)
    r0 = exchange(g0, sizes, lambda a, c: (a, c ^ 1))
    r1 = exchange(g1, sizes, lambda a, c: (a, c + 1 if c % 2 else c - 1))
    b, h, accb = load_fields(*inputs)
    b, h, y, l2, intra = edge(b, h, own, r0, r1, rl1)
    rl2 = exchange(l2, sizes, border_pair)
    rin = exchange(intra, sizes, lambda a, c: (a ^ 1, c))
    y, z, acc = inner(b, h, own, r0, r1, y)
    h, y, z, acc = near_side(b, h, rin, y, z, acc)
    y, z, msg = far_side(b, h, rl1, rl2, y, z, accb, acc)
    sent = jnp.broadcast_to(msg[0:1][None], (nx * ny, 1, 128))
    w = lax.all_to_all(sent, AXES, 0, 0).reshape(nx * ny, 128)
    return final(w, b, y, z)


def solution(mesh):
    sizes = (mesh.shape["gx"], mesh.shape["gy"])
    placed = (P(None, "gx", "gy", None), P("gx", "gy", None), P())
    return jax.shard_map(
        functools.partial(shards, sizes),
        mesh=mesh,
        in_specs=placed,
        out_specs=(P(None, "gx", "gy", None), P(None, "gx", "gy", None)),
        check_vma=False,
    )
```

time: 69.6 us -> 65.4 us (0.940)
  Pallas kernels: 25.8 us -> 30.3 us
  local copies, waits for them, and re-layouts: 4.12 us -> 0.06 us
  blocking collectives: 24.3 us -> 21.1 us
  waiting for transfers between devices: 4.32 us -> 2.27 us
    unnamed x6 -> x0, local copies, waits for them, and re-layouts: 4.06 us -> none
    all_to_all x1, blocking collectives: 24.3 us -> 21.1 us  [shards(): w = lax.all_to_all(sent, AXES, 0, 0).reshape(nx * ny, 128)]
    pallas_call x1, Pallas kernels: 1.44 us -> 3.58 us  [load_fields(): pl.pallas_call(functools.partial(load_kernel, current), out_shape=(f32(F,...]
    ppermute x5, waiting for transfers between devices: 4.32 us -> 2.27 us  [exchange(): return lax.ppermute(x, AXES, pairs)]
    pallas_call x4 -> x5, Pallas kernels: 22.9 us -> 24.7 us  [the longest x1 11.7 us: inner(): pl.pallas_call(inner_kernel, out_shape=(f32(F, NX + 2, Q, ROWS, 128), f32...]
  transfers between devices with their start and end apart: 5 -> 5, of which waited for: 2 -> 1; matrix products, arithmetic and copies ran while one was open for 0% -> 0% of each run, Pallas kernels for 16% -> 27%
where the time goes in v2:
time: 65.4 us; the launch traced here: 65.2 us
  Pallas kernels  30.3 us (46%)
  blocking collectives  21.1 us (32%)
  starting transfers between devices  10.7 us (16%)
  waiting for transfers between devices  2.27 us (3%)
  between operations  0.74 us (1%)
    all_to_all x1, blocking collectives, shards(): w = lax.all_to_all(sent, AXES, 0, 0).reshape(nx * ny, 128)  21.1 us
    pallas_call x1, Pallas kernels, inner(): pl.pallas_call(inner_kernel, out_shape=(f32(F, NX + 2, Q, ROWS, 128), f32...  11.7 us
    ppermute x5, starting transfers between devices, exchange(): return lax.ppermute(x, AXES, pairs)  10.7 us
    pallas_call x1, Pallas kernels, final(): pl.pallas_call(final_kernel, grid=(NX,), out_shape=(out, out), in_specs=[...  7.14 us
    pallas_call x1, Pallas kernels, load_fields(): pl.pallas_call(functools.partial(load_kernel, current), out_shape=(f32(F,...  3.58 us
    pallas_call x1, Pallas kernels, near_side(): pl.pallas_call(near_kernel, out_shape=(f32(NX + 2, Q, ROWS, 128), f32(F,...  2.5 us
    ppermute x5, waiting for transfers between devices, exchange(): return lax.ppermute(x, AXES, pairs)  2.27 us
    pallas_call x1, Pallas kernels, edge(): pl.pallas_call(edge_kernel, out_shape=(f32(F, NX, Q, ROWS, 128), f32(NX +...  2.06 us
  transfers between devices with their start and end apart: 5, of which 1 were waited for; matrix products, arithmetic and copies ran while one was open for 0% of the time, Pallas kernels for 27%

profile of v2, /device:TPU:1, one launch (start us, length us, event | category | flops | bytes accessed | tf_op | source)
XLA Modules:
  0.0 65.2 jit_solution(12535271206521937838)
XLA Ops:
  0.6 2.0 %pack.1 = (f32[1280,128]{1,0:T(8,128)S(1)}, f32[288,128]{1,0:T(8,128)S(1)}, f32[288,128]{1,0:T(8,128)S(1)}, f32[2,160,128]{2,1,0:T(8,128)S(1)}) custom-call(f32[4,8,64,512]{3,2,1,0:T(8,128)} %adj.3, f32[8,64,512]{2,1,0:T(8,128)} %sigma.3, s32[4]{0:T(128)} %elec_in.3), custom_call_target="tpu_custom_call" | custom-call | flops 8000000 | bytes 6000000 | tf_op jit(solution)/shard_map/pack/pallas_call | solution.py:185
  2.7 4.5 %collective-permute-start.2 = (f32[1280,128]{1,0:T(8,128)S(1)}, f32[1280,128]{1,0:T(8,128)S(1)}, u32[]{:S(2)}, u32[]{:S(2)}) collective-permute-start(f32[1280,128]{1,0:T(8,128)S(1)} %get-tuple-element.29), channel_id=1, source_target_pairs={{4,8},{5,9},{6,10},{7,11},{8,4},{9,5},{10,6},{11,7},{12,16},{13,17... | collective-permute-start | bytes 1966088 | tf_op jit(solution)/shard_map/ppermute | solution.py:733
  7.2 1.7 %collective-permute-start = (f32[288,128]{1,0:T(8,128)S(1)}, f32[288,128]{1,0:T(8,128)S(1)}, u32[]{:S(2)}, u32[]{:S(2)}) collective-permute-start(f32[288,128]{1,0:T(8,128)S(1)} %get-tuple-element.27), channel_id=1, source_target_pairs={{0,1},{1,0},{2,3},{3,2},{4,5},{5,4},{6,7},{7,6},{8,9},{9,8},{10,11... | collective-permute-start | bytes 442376 | tf_op jit(solution)/shard_map/ppermute | solution.py:733
  8.9 0.7 %collective-permute-start.1 = (f32[288,128]{1,0:T(8,128)S(1)}, f32[288,128]{1,0:T(8,128)S(1)}, u32[]{:S(2)}, u32[]{:S(2)}) collective-permute-start(f32[288,128]{1,0:T(8,128)S(1)} %get-tuple-element.28), channel_id=1, source_target_pairs={{1,2},{2,1},{5,6},{6,5},{9,10},{10,9},{13,14},{14,13},{17,18},{18,... | collective-permute-start | bytes 442376 | tf_op jit(solution)/shard_map/ppermute | solution.py:733
  9.6 3.6 %load.1 = (f32[4,8,4,80,128]{4,3,2,1,0:T(8,128)S(1)}, f32[10,4,80,128]{3,2,1,0:T(8,128)S(1)}, f32[10,8,128]{2,1,0:T(8,128)S(1)}) custom-call(f32[4,8,64,512]{3,2,1,0:T(8,128)} %adj.3, f32[8,64,512]{2,1,0:T(8,128)} %sigma.3, s32[4]{0:T(128)} %elec_in.3), custom_call_target="tpu_custom_call" | custom-call | flops 12000000 | bytes 9000000 | tf_op jit(solution)/shard_map/load/pallas_call | solution.py:249
  13.1 0.0 collective-permute-done.r0
  13.2 0.0 collective-permute-done.1.r1
  13.2 2.3 %collective-permute-done.2.rl1 = f32[1280,128]{1,0:T(8,128)S(1)} collective-permute-done((f32[1280,128]{1,0:T(8,128)S(1)}, f32[1280,128]{1,0:T(8,128)S(1)}, u32[]{:S(2)}, u32[]{:S(2)}) %collective-permute-start.2) | collective-permute-done | bytes 655392 | tf_op jit(solution)/shard_map/ppermute | solution.py:733
  15.4 2.1 %edge.1 = (f32[4,8,4,80,128]{4,3,2,1,0:T(8,128)S(1)}, f32[10,4,80,128]{3,2,1,0:T(8,128)S(1)}, f32[4,10,4,80,128]{4,3,2,1,0:T(8,128)S(1)}, f32[1072,128]{1,0:T(8,128)S(1)}, f32[2352,128]{1,0:T(8,128)S(1)}) custom-call(f32[4,8,4,80,128]{4,3,2,1,0:T(8,128)S(1)} %get-tuple-element.24.b_in, ...), custom_call_target="tpu_custom_call", output_to_operand_aliasing={{0}: (0, {}), {1}: (1, {})} | custom-call | flops 40000000 | bytes 30000000 | tf_op jit(solution)/shard_map/edge/pallas_call | solution.py:376
  17.5 0.1 collective-permute-start.3
  17.6 3.7 %collective-permute-start.4 = (f32[1072,128]{1,0:T(8,128)S(1)}, f32[1072,128]{1,0:T(8,128)S(1)}, u32[]{:S(2)}, u32[]{:S(2)}) collective-permute-start(f32[1072,128]{1,0:T(8,128)S(1)} %get-tuple-element.38), channel_id=1, source_target_pairs={{4,8},{5,9},{6,10},{7,11},{8,4},{9,5},{10,6},{11,7},{12,16},{13,17... | collective-permute-start | bytes 1646600 | tf_op jit(solution)/shard_map/ppermute | solution.py:733
  21.3 11.7 %inner.1 = (f32[4,10,4,80,128]{4,3,2,1,0:T(8,128)S(1)}, f32[4,8,4,64,128]{4,3,2,1,0:T(8,128)S(1)}, f32[30,8,128]{2,1,0:T(8,128)S(1)}) custom-call(f32[4,8,4,80,128]{4,3,2,1,0:T(8,128)S(1)} %get-tuple-element.30.b, f32[10,4,80,128]{3,2,1,0:T(8,128)S(1)} %get-tuple-element.31.h.h_in, ...), custom_call_target="tpu_custom_call", output_to_operand_aliasing={{0}: (5, {})} | custom-call | flops 24000000 | bytes 18000000 | tf_op jit(solution)/shard_map/inner/pallas_call | solution.py:481
  33.0 0.0 collective-permute-done.3.rin
  33.1 2.5 %near.1 = (f32[10,4,80,128]{3,2,1,0:T(8,128)S(1)}, f32[4,10,4,80,128]{4,3,2,1,0:T(8,128)S(1)}, f32[4,8,4,64,128]{4,3,2,1,0:T(8,128)S(1)}, f32[30,8,128]{2,1,0:T(8,128)S(1)}) custom-call(f32[4,8,4,80,128]{4,3,2,1,0:T(8,128)S(1)} %get-tuple-element.30.b, ...), custom_call_target="tpu_custom_call", output_to_operand_aliasing={{0}: (1, {}), {1}: (3, {}), {2}: (4, {})} | custom-call | flops 12000000 | bytes 9000000 | tf_op jit(solution)/shard_map/near/pallas_call | solution.py:545
  35.6 0.0 collective-permute-done.4.rl2
  35.6 1.3 %far.1 = (f32[4,10,4,80,128]{4,3,2,1,0:T(8,128)S(1)}, f32[4,8,4,64,128]{4,3,2,1,0:T(8,128)S(1)}, f32[8,128]{1,0:T(8,128)S(1)}) custom-call(f32[4,8,4,80,128]{4,3,2,1,0:T(8,128)S(1)} %get-tuple-element.30.b, f32[10,4,80,128]{3,2,1,0:T(8,128)S(1)} %get-tuple-element.37.h, ...), custom_call_target="tpu_custom_call", output_to_operand_aliasing={{0}: (4, {}), {1}: (5, {})} | custom-call | flops 12000000 | bytes 9000000 | tf_op jit(solution)/shard_map/far/pallas_call | solution.py:585
  36.9 0.1 broadcast_in_dim.9
  37.0 21.1 %all_to_all.5 = f32[128,1,128]{2,1,0:T(1,128)S(1)} all-to-all(f32[128,1,128]{2,1,0:T(1,128)S(1)} %broadcast_in_dim.9), channel_id=1, replica_groups=mesh['gx'=32,'gy'=4] {'gx','gy'}, dimensions={0} | all-to-all | bytes 131072 | tf_op jit(solution)/shard_map/all_to_all | solution.py:753
  58.0 7.1 %final.1 = (f32[4,8,64,512]{3,2,1,0:T(8,128)}, f32[4,8,64,512]{3,2,1,0:T(8,128)}) custom-call(f32[128,128]{1,0:T(8,128)S(1)} %bitcast.3, f32[4,8,4,80,128]{4,3,2,1,0:T(8,128)S(1)} %get-tuple-element.30.b, f32[4,10,4,80,128]{4,3,2,1,0:T(8,128)S(1)} %get-tuple-element.44.y, f32[4,8,4,64,128]{4,3,2,1,0:T(8,128)S(1)} %get-tuple-element.45.d), custom_call_target="tpu_custom_call" | custom-call | flops 20000000 | bytes 15000000 | tf_op jit(solution)/shard_map/final/pallas_call | solution.py:712
  (1 shorter events, 0.0 us)
Async XLA Ops:
  2.7 12.8 %collective-permute-start.2 = (f32[1280,128]{1,0:T(8,128)S(1)}, f32[1280,128]{1,0:T(8,128)S(1)}, u32[]{:S(2)}, u32[]{:S(2)}) collective-permute-start(f32[1280,128]{1,0:T(8,128)S(1)} %get-tuple-element.29), channel_id=1, source_target_pairs={{4,8},{5,9},{6,10},{7,11},{8,4},{9,5},{10,6},{11,7},{12,16},{13,17... | collective-permute-start | bytes 1966088 | tf_op jit(solution)/shard_map/ppermute | solution.py:733
  7.2 6.0 %collective-permute-start = (f32[288,128]{1,0:T(8,128)S(1)}, f32[288,128]{1,0:T(8,128)S(1)}, u32[]{:S(2)}, u32[]{:S(2)}) collective-permute-start(f32[288,128]{1,0:T(8,128)S(1)} %get-tuple-element.27), channel_id=1, source_target_pairs={{0,1},{1,0},{2,3},{3,2},{4,5},{5,4},{6,7},{7,6},{8,9},{9,8},{10,11... | collective-permute-start | bytes 442376 | tf_op jit(solution)/shard_map/ppermute | solution.py:733
  8.9 4.3 %collective-permute-start.1 = (f32[288,128]{1,0:T(8,128)S(1)}, f32[288,128]{1,0:T(8,128)S(1)}, u32[]{:S(2)}, u32[]{:S(2)}) collective-permute-start(f32[288,128]{1,0:T(8,128)S(1)} %get-tuple-element.28), channel_id=1, source_target_pairs={{1,2},{2,1},{5,6},{6,5},{9,10},{10,9},{13,14},{14,13},{17,18},{18,... | collective-permute-start | bytes 442376 | tf_op jit(solution)/shard_map/ppermute | solution.py:733
  17.5 15.6 %collective-permute-start.3 = (f32[2352,128]{1,0:T(8,128)S(1)}, f32[2352,128]{1,0:T(8,128)S(1)}, u32[]{:S(2)}, u32[]{:S(2)}) collective-permute-start(f32[2352,128]{1,0:T(8,128)S(1)} %get-tuple-element.32), channel_id=1, source_target_pairs={{0,4},{1,5},{2,6},{3,7},{4,0},{5,1},{6,2},{7,3},{8,12},{9,13},{10,... | collective-permute-start | bytes 3612680 | tf_op jit(solution)/shard_map/ppermute | solution.py:733
  17.6 18.0 %collective-permute-start.4 = (f32[1072,128]{1,0:T(8,128)S(1)}, f32[1072,128]{1,0:T(8,128)S(1)}, u32[]{:S(2)}, u32[]{:S(2)}) collective-permute-start(f32[1072,128]{1,0:T(8,128)S(1)} %get-tuple-element.38), channel_id=1, source_target_pairs={{4,8},{5,9},{6,10},{7,11},{8,4},{9,5},{10,6},{11,7},{12,16},{13,17... | collective-permute-start | bytes 1646600 | tf_op jit(solution)/shard_map/ppermute | solution.py:733

commit v3 on v2

--- a/solution.py
+++ b/solution.py
@@ -15,7 +15,7 @@
 NZ = 512
 Q = NZ // 128
 CHUNKS = NY // 8
-UNROLL = 2
+UNROLL = 4
 PAIRS = [(i, j) for i in range(F) for j in range(i, F)]
 TOP = 8
 ROWS = NY + 2 * TOP
@@ -70,13 +70,13 @@
 
 def z_coeffs(h):
     up = [a + b for a, b in zip(h, above_z(h))]
-    edge = iota(1) == 127
-    total = up[:-1] + [jnp.where(edge, 2.0 * h[-1], up[-1])]
-    up[-1] = jnp.where(edge, 0.0, up[-1])
-    down = below_z(up)
-    first = jnp.where(iota(1) == 0, 2.0 * h[0], down[0])
-    total = [t + d for t, d in zip(total, [first] + down[1:])]
-    down[0] = jnp.where(iota(1) == 0, 0.0, down[0])
+    down = [a + b for a, b in zip(h, below_z(h))]
+    first, last = iota(1) == 0, iota(1) == 127
+    total = [a + b for a, b in zip(up, down)]
+    total[0] = up[0] + jnp.where(first, 2.0 * h[0], down[0])
+    total[-1] = jnp.where(last, 2.0 * h[-1], up[-1]) + down[-1]
+    down[0] = jnp.where(first, 0.0, down[0])
+    up[-1] = jnp.where(last, 0.0, up[-1])
     return up, down, total
 
 
@@ -285,14 +285,15 @@
     total, faces = coeffs
     at = r + TOP
     own = tiles_of(v, (f, k), at)
-    beside = [above_z(own), below_z(own)]
-    beside += [tiles_of(v, (f, k + s[0]), at + s[1]) for s, _ in faces[2:]]
     out = []
+    up, down = above_z(own), below_z(own)
     for q in range(Q):
-        t = total[q] * own[q]
-        for (_, c), n in zip(faces, beside):
-            t = t - c[q] * n[q]
-        out.append(t)
+        t = total[q] * own[q] - faces[0][1][q] * up[q] - faces[1][1][q] * down[q]
+        u = None
+        for s, c in faces[2:]:
+            n = c[q] * v[f, k + s[0], q, pl.ds(at + s[1], 8), :]
+            u = n if u is None else u + n
+        out.append(t - u)
     return own, out
 
 
@@ -417,22 +418,23 @@
                 y[f, x + 1, q, row : row + 1, :] = tmp[side, f, q, x : x + 1, :]
 
 
-def z_plane(h, y, z, acc, x):
+def z_plane(h, y, d, acc, x):
     def chunk(r):
         coeffs = chunk_coeffs(h, x + 1, r)
-        vs, outs = [], []
         for f in range(F):
             v, out = chunk_apply(coeffs, y, f, x + 1, r)
             for q in range(Q):
-                z[f, x, q, pl.ds(r, 8), :] = out[q] - v[q]
-            vs.append(v)
-            outs.append(out)
-        add_gram(acc, 20, vs, outs)
+                d[f, x, q, pl.ds(r, 8), :] = out[q] - v[q]
+
+    def grams(r):
+        ys = [tiles_of(y, (f, x + 1), r + TOP) for f in range(F)]
+        add_gram(acc, 20, ys, [tiles_of(d, (f, x), r) for f in range(F)])
 
     chunk_loop(chunk)
-
-
-def edge_grams(b, y, acc, x):
+    chunk_loop(grams)
+
+
+def plane_grams(b, y, acc, x):
     def chunk(r):
         vs = [tiles_of(b, (f, x), r + TOP) for f in range(F)]
         outs = [tiles_of(y, (f, x + 1), r + TOP) for f in range(F)]
@@ -454,21 +456,17 @@
     def y_plane(x, carry):
         def chunk(r):
             coeffs = chunk_coeffs(h, x + 1, r)
-            vs, outs = [], []
             for f in range(F):
-                v, out = chunk_apply(coeffs, b, f, x, r)
+                _, out = chunk_apply(coeffs, b, f, x, r)
                 for q in range(Q):
                     y[f, x + 1, q, pl.ds(r + TOP, 8), :] = out[q]
-                vs.append(v)
-                outs.append(out)
-            add_gram(acc, 0, vs, outs)
-            add_gram(acc, 10, outs, outs)
 
         chunk_loop(chunk)
+        plane_grams(b, y, acc, x)
         return carry
 
     lax.fori_loop(1, NX - 1, y_plane, 0)
-    edge_grams(b, y, acc, far)
+    plane_grams(b, y, acc, far)
 
     def z_loop(n, carry):
         z_plane(h, y, z, acc, jnp.where(par == 0, n, NX - 1 - n))
@@ -532,7 +530,7 @@
     acc[...] = acc_in[...]
     border(b, h, y, rin, near, halo)
     halo_image(b, h, y, rin, rin, L1_ROWS, near, halo)
-    edge_grams(b, y, acc, near)
+    plane_grams(b, y, acc, near)
 
     def z_loop(n, carry):
         z_plane(h, y, z, acc, jnp.where(par == 0, n, NX - 1 - n))
@@ -646,7 +644,8 @@
         for n, (i, j) in enumerate(PAIRS):
             m[i][j] = m[j][i] = entry(10 * g + n)
         grams.append(m)
-    bb, by, yy, yz = grams
+    bb, by, yy, yd = grams
+    yz = add(yd, yy)
     alpha = spd_solve(by, bb)
     new = symmetric(add(mm(alpha, mm(yy, alpha), ta=True), bb, -1.0))
     beta = spd_solve(bb, new)

time: 65.4 us -> 59.5 us (0.910)
  Pallas kernels: 30.3 us -> 24.4 us
    pallas_call x1, Pallas kernels: 11.7 us -> 7.61 us  [inner(): pl.pallas_call(inner_kernel, out_shape=(f32(F, NX + 2, Q, ROWS, 128), f32...]
    pallas_call x1, Pallas kernels: 2.5 us -> 1.71 us  [near_side(): pl.pallas_call(near_kernel, out_shape=(f32(NX + 2, Q, ROWS, 128), f32(F,...]
  transfers between devices with their start and end apart: 5 -> 5, of which waited for: 1 -> 1; matrix products, arithmetic and copies ran while one was open for 0% -> 0% of each run, Pallas kernels for 27% -> 22%
where the time goes in v3:
time: 59.5 us; the launch traced here: 59.3 us
  Pallas kernels  24.4 us (41%)
  blocking collectives  21.1 us (35%)
  starting transfers between devices  10.7 us (18%)
  waiting for transfers between devices  2.32 us (4%)
  between operations  0.74 us (1%)
    all_to_all x1, blocking collectives, shards(): w = lax.all_to_all(sent, AXES, 0, 0).reshape(nx * ny, 128)  21.1 us
    ppermute x5, starting transfers between devices, exchange(): return lax.ppermute(x, AXES, pairs)  10.7 us
    pallas_call x1, Pallas kernels, inner(): pl.pallas_call(inner_kernel, out_shape=(f32(F, NX + 2, Q, ROWS, 128), f32...  7.61 us
    pallas_call x1, Pallas kernels, final(): pl.pallas_call(final_kernel, grid=(NX,), out_shape=(out, out), in_specs=[...  7.14 us
    pallas_call x1, Pallas kernels, load_fields(): pl.pallas_call(functools.partial(load_kernel, current), out_shape=(f32(F,...  3.53 us
    ppermute x5, waiting for transfers between devices, exchange(): return lax.ppermute(x, AXES, pairs)  2.32 us
    pallas_call x1, Pallas kernels, pack(): pl.pallas_call(functools.partial(pack_kernel, current), out_shape=(f32(L1...  2.02 us
    pallas_call x1, Pallas kernels, near_side(): pl.pallas_call(near_kernel, out_shape=(f32(NX + 2, Q, ROWS, 128), f32(F,...  1.71 us
  transfers between devices with their start and end apart: 5, of which 1 were waited for; matrix products, arithmetic and copies ran while one was open for 0% of the time, Pallas kernels for 22%

profile of v3, /device:TPU:1, one launch (start us, length us, event | category | flops | bytes accessed | tf_op | source)
XLA Modules:
  0.0 59.3 jit_solution(14999322083820390449)
XLA Ops:
  0.6 2.0 %pack.1 = (f32[1280,128]{1,0:T(8,128)S(1)}, f32[288,128]{1,0:T(8,128)S(1)}, f32[288,128]{1,0:T(8,128)S(1)}, f32[2,160,128]{2,1,0:T(8,128)S(1)}) custom-call(f32[4,8,64,512]{3,2,1,0:T(8,128)} %adj.3, f32[8,64,512]{2,1,0:T(8,128)} %sigma.3, s32[4]{0:T(128)} %elec_in.3), custom_call_target="tpu_custom_call" | custom-call | flops 8000000 | bytes 6000000 | tf_op jit(solution)/shard_map/pack/pallas_call | solution.py:185
  2.7 4.5 %collective-permute-start.2 = (f32[1280,128]{1,0:T(8,128)S(1)}, f32[1280,128]{1,0:T(8,128)S(1)}, u32[]{:S(2)}, u32[]{:S(2)}) collective-permute-start(f32[1280,128]{1,0:T(8,128)S(1)} %get-tuple-element.29), channel_id=1, source_target_pairs={{4,8},{5,9},{6,10},{7,11},{8,4},{9,5},{10,6},{11,7},{12,16},{13,17... | collective-permute-start | bytes 1966088 | tf_op jit(solution)/shard_map/ppermute | solution.py:732
  7.2 1.7 %collective-permute-start = (f32[288,128]{1,0:T(8,128)S(1)}, f32[288,128]{1,0:T(8,128)S(1)}, u32[]{:S(2)}, u32[]{:S(2)}) collective-permute-start(f32[288,128]{1,0:T(8,128)S(1)} %get-tuple-element.27), channel_id=1, source_target_pairs={{0,1},{1,0},{2,3},{3,2},{4,5},{5,4},{6,7},{7,6},{8,9},{9,8},{10,11... | collective-permute-start | bytes 442376 | tf_op jit(solution)/shard_map/ppermute | solution.py:732
  8.9 0.7 %collective-permute-start.1 = (f32[288,128]{1,0:T(8,128)S(1)}, f32[288,128]{1,0:T(8,128)S(1)}, u32[]{:S(2)}, u32[]{:S(2)}) collective-permute-start(f32[288,128]{1,0:T(8,128)S(1)} %get-tuple-element.28), channel_id=1, source_target_pairs={{1,2},{2,1},{5,6},{6,5},{9,10},{10,9},{13,14},{14,13},{17,18},{18,... | collective-permute-start | bytes 442376 | tf_op jit(solution)/shard_map/ppermute | solution.py:732
  9.6 3.5 %load.1 = (f32[4,8,4,80,128]{4,3,2,1,0:T(8,128)S(1)}, f32[10,4,80,128]{3,2,1,0:T(8,128)S(1)}, f32[10,8,128]{2,1,0:T(8,128)S(1)}) custom-call(f32[4,8,64,512]{3,2,1,0:T(8,128)} %adj.3, f32[8,64,512]{2,1,0:T(8,128)} %sigma.3, s32[4]{0:T(128)} %elec_in.3), custom_call_target="tpu_custom_call" | custom-call | flops 12000000 | bytes 9000000 | tf_op jit(solution)/shard_map/load/pallas_call | solution.py:249
  13.1 0.0 collective-permute-done.r0
  13.1 0.0 collective-permute-done.1.r1
  13.1 2.3 %collective-permute-done.2.rl1 = f32[1280,128]{1,0:T(8,128)S(1)} collective-permute-done((f32[1280,128]{1,0:T(8,128)S(1)}, f32[1280,128]{1,0:T(8,128)S(1)}, u32[]{:S(2)}, u32[]{:S(2)}) %collective-permute-start.2) | collective-permute-done | bytes 655392 | tf_op jit(solution)/shard_map/ppermute | solution.py:732
  15.4 1.4 %edge.1 = (f32[4,8,4,80,128]{4,3,2,1,0:T(8,128)S(1)}, f32[10,4,80,128]{3,2,1,0:T(8,128)S(1)}, f32[4,10,4,80,128]{4,3,2,1,0:T(8,128)S(1)}, f32[1072,128]{1,0:T(8,128)S(1)}, f32[2352,128]{1,0:T(8,128)S(1)}) custom-call(f32[4,8,4,80,128]{4,3,2,1,0:T(8,128)S(1)} %get-tuple-element.24.b_in, ...), custom_call_target="tpu_custom_call", output_to_operand_aliasing={{0}: (0, {}), {1}: (1, {})} | custom-call | flops 40000000 | bytes 30000000 | tf_op jit(solution)/shard_map/edge/pallas_call | solution.py:377
  16.8 0.1 collective-permute-start.3
  16.9 3.7 %collective-permute-start.4 = (f32[1072,128]{1,0:T(8,128)S(1)}, f32[1072,128]{1,0:T(8,128)S(1)}, u32[]{:S(2)}, u32[]{:S(2)}) collective-permute-start(f32[1072,128]{1,0:T(8,128)S(1)} %get-tuple-element.38), channel_id=1, source_target_pairs={{4,8},{5,9},{6,10},{7,11},{8,4},{9,5},{10,6},{11,7},{12,16},{13,17... | collective-permute-start | bytes 1646600 | tf_op jit(solution)/shard_map/ppermute | solution.py:732
  20.7 7.6 %inner.1 = (f32[4,10,4,80,128]{4,3,2,1,0:T(8,128)S(1)}, f32[4,8,4,64,128]{4,3,2,1,0:T(8,128)S(1)}, f32[30,8,128]{2,1,0:T(8,128)S(1)}) custom-call(f32[4,8,4,80,128]{4,3,2,1,0:T(8,128)S(1)} %get-tuple-element.30.b, f32[10,4,80,128]{3,2,1,0:T(8,128)S(1)} %get-tuple-element.31.h.h_in, ...), custom_call_target="tpu_custom_call", output_to_operand_aliasing={{0}: (5, {})} | custom-call | flops 24000000 | bytes 18000000 | tf_op jit(solution)/shard_map/inner/pallas_call | solution.py:479
  28.3 0.0 collective-permute-done.3.rin
  28.3 1.7 %near.1 = (f32[10,4,80,128]{3,2,1,0:T(8,128)S(1)}, f32[4,10,4,80,128]{4,3,2,1,0:T(8,128)S(1)}, f32[4,8,4,64,128]{4,3,2,1,0:T(8,128)S(1)}, f32[30,8,128]{2,1,0:T(8,128)S(1)}) custom-call(f32[4,8,4,80,128]{4,3,2,1,0:T(8,128)S(1)} %get-tuple-element.30.b, ...), custom_call_target="tpu_custom_call", output_to_operand_aliasing={{0}: (1, {}), {1}: (3, {}), {2}: (4, {})} | custom-call | flops 12000000 | bytes 9000000 | tf_op jit(solution)/shard_map/near/pallas_call | solution.py:543
  30.0 0.0 collective-permute-done.4.rl2
  30.0 0.9 %far.1 = (f32[4,10,4,80,128]{4,3,2,1,0:T(8,128)S(1)}, f32[4,8,4,64,128]{4,3,2,1,0:T(8,128)S(1)}, f32[8,128]{1,0:T(8,128)S(1)}) custom-call(f32[4,8,4,80,128]{4,3,2,1,0:T(8,128)S(1)} %get-tuple-element.30.b, f32[10,4,80,128]{3,2,1,0:T(8,128)S(1)} %get-tuple-element.37.h, ...), custom_call_target="tpu_custom_call", output_to_operand_aliasing={{0}: (4, {}), {1}: (5, {})} | custom-call | flops 12000000 | bytes 9000000 | tf_op jit(solution)/shard_map/far/pallas_call | solution.py:583
  31.0 0.1 broadcast_in_dim.9
  31.0 21.1 %all_to_all.5 = f32[128,1,128]{2,1,0:T(1,128)S(1)} all-to-all(f32[128,1,128]{2,1,0:T(1,128)S(1)} %broadcast_in_dim.9), channel_id=1, replica_groups=mesh['gx'=32,'gy'=4] {'gx','gy'}, dimensions={0} | all-to-all | bytes 131072 | tf_op jit(solution)/shard_map/all_to_all | solution.py:752
  52.2 7.1 %final.1 = (f32[4,8,64,512]{3,2,1,0:T(8,128)}, f32[4,8,64,512]{3,2,1,0:T(8,128)}) custom-call(f32[128,128]{1,0:T(8,128)S(1)} %bitcast.3, f32[4,8,4,80,128]{4,3,2,1,0:T(8,128)S(1)} %get-tuple-element.30.b, f32[4,10,4,80,128]{4,3,2,1,0:T(8,128)S(1)} %get-tuple-element.44.y, f32[4,8,4,64,128]{4,3,2,1,0:T(8,128)S(1)} %get-tuple-element.45.d), custom_call_target="tpu_custom_call" | custom-call | flops 20000000 | bytes 15000000 | tf_op jit(solution)/shard_map/final/pallas_call | solution.py:711
  (1 shorter events, 0.0 us)
Async XLA Ops:
  2.7 12.8 %collective-permute-start.2 = (f32[1280,128]{1,0:T(8,128)S(1)}, f32[1280,128]{1,0:T(8,128)S(1)}, u32[]{:S(2)}, u32[]{:S(2)}) collective-permute-start(f32[1280,128]{1,0:T(8,128)S(1)} %get-tuple-element.29), channel_id=1, source_target_pairs={{4,8},{5,9},{6,10},{7,11},{8,4},{9,5},{10,6},{11,7},{12,16},{13,17... | collective-permute-start | bytes 1966088 | tf_op jit(solution)/shard_map/ppermute | solution.py:732
  7.2 5.9 %collective-permute-start = (f32[288,128]{1,0:T(8,128)S(1)}, f32[288,128]{1,0:T(8,128)S(1)}, u32[]{:S(2)}, u32[]{:S(2)}) collective-permute-start(f32[288,128]{1,0:T(8,128)S(1)} %get-tuple-element.27), channel_id=1, source_target_pairs={{0,1},{1,0},{2,3},{3,2},{4,5},{5,4},{6,7},{7,6},{8,9},{9,8},{10,11... | collective-permute-start | bytes 442376 | tf_op jit(solution)/shard_map/ppermute | solution.py:732
  8.9 4.2 %collective-permute-start.1 = (f32[288,128]{1,0:T(8,128)S(1)}, f32[288,128]{1,0:T(8,128)S(1)}, u32[]{:S(2)}, u32[]{:S(2)}) collective-permute-start(f32[288,128]{1,0:T(8,128)S(1)} %get-tuple-element.28), channel_id=1, source_target_pairs={{1,2},{2,1},{5,6},{6,5},{9,10},{10,9},{13,14},{14,13},{17,18},{18,... | collective-permute-start | bytes 442376 | tf_op jit(solution)/shard_map/ppermute | solution.py:732
  16.8 11.5 %collective-permute-start.3 = (f32[2352,128]{1,0:T(8,128)S(1)}, f32[2352,128]{1,0:T(8,128)S(1)}, u32[]{:S(2)}, u32[]{:S(2)}) collective-permute-start(f32[2352,128]{1,0:T(8,128)S(1)} %get-tuple-element.32), channel_id=1, source_target_pairs={{0,4},{1,5},{2,6},{3,7},{4,0},{5,1},{6,2},{7,3},{8,12},{9,13},{10,... | collective-permute-start | bytes 3612680 | tf_op jit(solution)/shard_map/ppermute | solution.py:732
  16.9 13.1 %collective-permute-start.4 = (f32[1072,128]{1,0:T(8,128)S(1)}, f32[1072,128]{1,0:T(8,128)S(1)}, u32[]{:S(2)}, u32[]{:S(2)}) collective-permute-start(f32[1072,128]{1,0:T(8,128)S(1)} %get-tuple-element.38), channel_id=1, source_target_pairs={{4,8},{5,9},{6,10},{7,11},{8,4},{9,5},{10,6},{11,7},{12,16},{13,17... | collective-permute-start | bytes 1646600 | tf_op jit(solution)/shard_map/ppermute | solution.py:732

commit v4 on v3

--- a/solution.py
+++ b/solution.py
@@ -206,37 +206,32 @@
     )(*in_hbm(adj, sigma, electrodes))
 
 
-def load_kernel(current, adj, sigma, elec_in, b_out, h_out, acc, fields, cond, elec, sems, esem):
+def load_kernel(current, adj, sigma, elec_in, b_out, h_out, acc, elec, esem):
     ecopy = pltpu.make_async_copy(elec_in, elec, esem)
     ecopy.start()
-    copies = [pltpu.make_async_copy(adj.at[f], fields.at[f], sems.at[f]) for f in range(F)]
-    copies.append(pltpu.make_async_copy(sigma, cond, sems.at[F]))
-    for c in copies:
-        c.start()
+    acc[...] = jnp.zeros(acc.shape, jnp.float32)
+
+    def place(x, carry):
+        for q in range(Q):
+            s = slice(q * 128, q * 128 + 128)
+            for f in range(F):
+                b_out[f, x, q, TOP : TOP + NY, :] = adj[f, x, :, s]
+            h_out[x + 1, q, TOP : TOP + NY, :] = 0.5 * sigma[x, :, s]
+        return carry
+
+    lax.fori_loop(0, NX, place, 0)
     ecopy.wait()
-    acc[...] = jnp.zeros(acc.shape, jnp.float32)
-    for c in copies:
-        c.wait()
     for f in range(F):
         lx, ly, here = local_cell(elec, f)
 
         @pl.when(here)
         def _(f=f, lx=lx, ly=ly):
             r8 = pl.multiple_of((ly // 8) * 8, 8)
-            add_spike(fields, (f, lx, pl.ds(r8, 8)), ly - r8, current)
+            add_spike(b_out, (f, lx, 0, pl.ds(r8 + TOP, 8)), ly - r8, current)
 
     def plane(x, carry):
         def chunk(r):
-            vs = []
-            for f in range(F):
-                v = [fields[f, x, pl.ds(r, 8), q * 128 : q * 128 + 128] for q in range(Q)]
-                for q in range(Q):
-                    b_out[f, x, q, pl.ds(r + TOP, 8), :] = v[q]
-                vs.append(v)
-            for q in range(Q):
-                h_out[x + 1, q, pl.ds(r + TOP, 8), :] = (
-                    0.5 * cond[x, pl.ds(r, 8), q * 128 : q * 128 + 128]
-                )
+            vs = [tiles_of(b_out, (f, x), r + TOP) for f in range(F)]
             add_gram(acc, 0, vs, vs)
 
         chunk_loop(chunk)
@@ -249,31 +244,22 @@
     return pl.pallas_call(
         functools.partial(load_kernel, current),
         out_shape=(f32(F, NX, Q, ROWS, 128), f32(NX + 2, Q, ROWS, 128), f32(10, 8, 128)),
-        in_specs=[HBM] * 3,
+        in_specs=[VM, VM, HBM],
         out_specs=(VM,) * 3,
-        scratch_shapes=[
-            pltpu.VMEM((F, NX, NY, NZ), jnp.float32),
-            pltpu.VMEM((NX, NY, NZ), jnp.float32),
-            pltpu.SMEM((F,), jnp.int32),
-            pltpu.SemaphoreType.DMA((F + 1,)),
-            pltpu.SemaphoreType.DMA,
-        ],
+        scratch_shapes=[pltpu.SMEM((F,), jnp.int32), pltpu.SemaphoreType.DMA],
         compiler_params=params(),
-        cost_estimate=cost(3),
+        cost_estimate=cost(2),
         name="load",
-    )(*in_hbm(adj, sigma, electrodes))
-
-
-def chunk_coeffs(h, k, r, low=True, high=True):
+    )(adj, sigma, *in_hbm(electrodes))
+
+
+def chunk_coeffs(h, k, r, x_steps=(-1, 1)):
     at = r + TOP
     own = tiles_of(h, (k,), at)
     up, down, total = z_coeffs(own)
     faces = [(None, up), (None, down)]
     others = [((0, 1), tiles_of(h, (k,), at + 1)), ((0, -1), tiles_of(h, (k,), at - 1))]
-    if low:
-        others.append(((-1, 0), tiles_of(h, (k - 1,), at)))
-    if high:
-        others.append(((1, 0), tiles_of(h, (k + 1,), at)))
+    others += [((s, 0), tiles_of(h, (k + s,), at)) for s in x_steps]
     for step, other in others:
         c = [a + b for a, b in zip(own, other)]
         total = [a + b for a, b in zip(total, c)]
@@ -309,11 +295,34 @@
     return jnp.where(ypar == 0, b, a), jnp.where(ypar == 0, a, b)
 
 
-def edge_kernel(b_in, h_in, own, r0, r1, rl1, b, h, y, l2_out, in_out, g):
+def edge_plane(b, h, y, x, step):
+    def chunk(r):
+        coeffs = chunk_coeffs(h, x + 1, r, (step,))
+        for f in range(F):
+            _, out = chunk_apply(coeffs, b, f, x, r)
+            for q in range(Q):
+                y[f, x + 1, q, pl.ds(r + TOP, 8), :] = out[q]
+
+    chunk_loop(chunk)
+
+
+def put_image(y, g, out, base, x):
+    for item in range(F * Q):
+        f, q = divmod(item, Q)
+        a = base + item * NY
+        out[a : a + NY, :] = y[f, x + 1, q, TOP : TOP + NY, :]
+    base = base + F * PLANE
+    out[base : base + 2 * CORNER, :] = jnp.zeros((2 * CORNER, 128), jnp.float32)
+    for side in range(2):
+        for item in range((F + 1) * Q):
+            a = base + side * CORNER + item
+            out[a : a + 1, :] = g[side, pl.ds(item * 8 + x, 1), :]
+
+
+def far_edge_kernel(b_in, h_in, own, r0, r1, b, h, y, g, out, clamped):
     del b_in, h_in
     par = lax.axis_index("gx") % 2
     ypar = lax.axis_index("gy") % 2
-    far, near, far_halo, _ = side_planes(par)
     for item in range((F + 1) * Q):
         f, q = divmod(item, Q)
         for side, t in enumerate(halo_select(ypar, r0, r1, item)):
@@ -323,37 +332,26 @@
                 for x in range(NX):
                     b[f, x, q, row : row + 1, :] = g[side, item * 8 + x : item * 8 + x + 1, :]
             else:
-                t = inside(t, own[side, item * 8 : item * 8 + 8, :])
-                g[2 + side, q * 8 : q * 8 + 8, :] = t
+                clamped[side, q] = inside(t, own[side, item * 8 : item * 8 + 8, :])
                 for x in range(NX):
-                    h[x + 1, q, row : row + 1, :] = g[2 + side, q * 8 + x : q * 8 + x + 1, :]
-    for x in (0, NX - 1):
-
-        def chunk(r, x=x):
-            coeffs = chunk_coeffs(h, x + 1, r, low=x > 0, high=x == 0)
-            for f in range(F):
-                _, out = chunk_apply(coeffs, b, f, x, r)
-                for q in range(Q):
-                    y[f, x + 1, q, pl.ds(r + TOP, 8), :] = out[q]
-
-        chunk_loop(chunk)
-    data = slice(TOP, TOP + NY)
+                    h[x + 1, q, row : row + 1, :] = clamped[side, q, x : x + 1, :]
+    far = side_planes(par)[0]
+    edge_plane(b, h, y, far, 1 - 2 * par)
+    put_image(y, g, out, 0, far)
+
+
+def near_edge_kernel(b, h_in, y_in, g, rl1, h, y, out):
+    del h_in, y_in
+    par = lax.axis_index("gx") % 2
+    far, near, far_halo, _ = side_planes(par)
+    edge_plane(b, h, y, near, 2 * par - 1)
     for q in range(Q):
         for f in range(F):
             a = (f * Q + q) * NY
-            l2_out[a : a + NY, :] = y[f, far + 1, q, data, :]
-            in_out[a : a + NY, :] = b[f, near, q, data, :]
-            in_out[L1_ROWS + a : L1_ROWS + a + NY, :] = y[f, near + 1, q, data, :]
+            out[a : a + NY, :] = b[f, near, q, TOP : TOP + NY, :]
         a = (F * Q + q) * NY
-        in_out[a : a + NY, :] = h[near + 1, q, data, :]
-    base = F * PLANE
-    l2_out[base:L2_ROWS, :] = jnp.zeros((2 * CORNER, 128), jnp.float32)
-    in_out[L1_ROWS + base : IN_ROWS, :] = jnp.zeros((2 * CORNER, 128), jnp.float32)
-    for side in range(2):
-        for item in range((F + 1) * Q):
-            a = base + side * CORNER + item
-            l2_out[a : a + 1, :] = g[side, pl.ds(item * 8 + far, 1), :]
-            in_out[L1_ROWS + a : L1_ROWS + a + 1, :] = g[side, pl.ds(item * 8 + near, 1), :]
+        out[a : a + NY, :] = h[near + 1, q, TOP : TOP + NY, :]
+    put_image(y, g, out, L1_ROWS, near)
     border(b, h, y, rl1, far, far_halo)
 
 
@@ -373,24 +371,41 @@
     chunk_loop(chunk)
 
 
-def edge(b, h, own, r0, r1, rl1):
+def far_edge(b, h, own, r0, r1):
     return pl.pallas_call(
-        edge_kernel,
+        far_edge_kernel,
         out_shape=(
             f32(F, NX, Q, ROWS, 128),
             f32(NX + 2, Q, ROWS, 128),
             f32(F, NX + 2, Q, ROWS, 128),
+            f32(2, TILE_ROWS, 128),
             f32(L2_ROWS, 128),
+        ),
+        in_specs=[VM] * 5,
+        out_specs=(VM,) * 5,
+        input_output_aliases={0: 0, 1: 1},
+        scratch_shapes=[pltpu.VMEM((2, Q, 8, 128), jnp.float32)],
+        compiler_params=params(),
+        cost_estimate=cost(10),
+        name="far_edge",
+    )(b, h, own, r0, r1)
+
+
+def near_edge(b, h, y, g, rl1):
+    return pl.pallas_call(
+        near_edge_kernel,
+        out_shape=(
+            f32(NX + 2, Q, ROWS, 128),
+            f32(F, NX + 2, Q, ROWS, 128),
             f32(IN_ROWS, 128),
         ),
-        in_specs=[VM] * 6,
-        out_specs=(VM,) * 5,
-        input_output_aliases={0: 0, 1: 1},
-        scratch_shapes=[pltpu.VMEM((4, TILE_ROWS, 128), jnp.float32)],
+        in_specs=[VM] * 5,
+        out_specs=(VM,) * 3,
+        input_output_aliases={1: 0, 2: 1},
         compiler_params=params(),
-        cost_estimate=cost(10),
-        name="edge",
-    )(b, h, own, r0, r1, rl1)
+        cost_estimate=cost(20),
+        name="near_edge",
+    )(b, h, y, g, rl1)
 
 
 def row_halo(own, rh, side, y, tmp):
@@ -488,7 +503,7 @@
         input_output_aliases={5: 0},
         scratch_shapes=[pltpu.VMEM((2, F, Q, 8, 128), jnp.float32)],
         compiler_params=params(),
-        cost_estimate=cost(6),
+        cost_estimate=cost(0),
         name="inner",
     )(b, h, own, r0, r1, y)
 
@@ -552,7 +567,7 @@
         out_specs=(VM,) * 4,
         input_output_aliases={1: 0, 3: 1, 4: 2},
         compiler_params=params(),
-        cost_estimate=cost(3),
+        cost_estimate=cost(0),
         name="near",
     )(b, h, rin, y, z, acc)
 
@@ -659,62 +674,76 @@
     return m1, m2
 
 
-def final_kernel(w, b, y, d, xs_out, res_out, coef):
-    x = pl.program_id(0)
-
-    @pl.when(x == 0)
-    def _():
-        total = jnp.sum(w[...], axis=0, keepdims=True)
-        sub = lax.broadcasted_iota(jnp.int32, (128, 128), 0)
-        lane = lax.broadcasted_iota(jnp.int32, (128, 128), 1)
-        spread = lax.dot_general(
-            jnp.where(sub == lane, total, 0.0),
-            jnp.ones((128, 128), jnp.float32),
-            (((1,), (0,)), ((), ())),
-            precision=lax.Precision.HIGHEST,
-            preferred_element_type=jnp.float32,
+def final_kernel(w, b, y, d, xs_hbm, res_hbm, coef, xs_out, res_out, sems):
+    total = jnp.sum(w[...], axis=0, keepdims=True)
+    sub = lax.broadcasted_iota(jnp.int32, (128, 128), 0)
+    lane = lax.broadcasted_iota(jnp.int32, (128, 128), 1)
+    spread = lax.dot_general(
+        jnp.where(sub == lane, total, 0.0),
+        jnp.ones((128, 128), jnp.float32),
+        (((1,), (0,)), ((), ())),
+        precision=lax.Precision.HIGHEST,
+        preferred_element_type=jnp.float32,
+    )
+    m1, m2 = step_matrices(lambda k: spread[k : k + 1, :])
+    for i in range(F):
+        for j in range(F):
+            n = i * F + j
+            coef[n] = jnp.broadcast_to(m1[i][j], (8, 128))
+            coef[16 + n] = jnp.broadcast_to(m2[i][j], (8, 128))
+            coef[32 + n] = jnp.broadcast_to(m1[i][j] - m2[i][j], (8, 128))
+
+    def copies(x):
+        return (
+            pltpu.make_async_copy(xs_out.at[:, x], xs_hbm.at[:, x], sems.at[0, x]),
+            pltpu.make_async_copy(res_out.at[:, x], res_hbm.at[:, x], sems.at[1, x]),
         )
-        m1, m2 = step_matrices(lambda k: spread[k : k + 1, :])
-        for i in range(F):
-            for j in range(F):
-                n = i * F + j
-                coef[n] = jnp.broadcast_to(m1[i][j], (8, 128))
-                coef[16 + n] = jnp.broadcast_to(m2[i][j], (8, 128))
-                coef[32 + n] = jnp.broadcast_to(m1[i][j] - m2[i][j], (8, 128))
-
-    def body(i, carry):
-        r = pl.multiple_of(i * 8, 8)
-        for q in range(Q):
-            bs = [b[f, x, q, pl.ds(r + TOP, 8), :] for f in range(F)]
-            ys = [y[f, x + 1, q, pl.ds(r + TOP, 8), :] for f in range(F)]
-            ds = [d[f, x, q, pl.ds(r, 8), :] for f in range(F)]
-            es = [bs[f] - ys[f] for f in range(F)]
-            for j in range(F):
-                p = ys[0] * coef[32 + j]
-                for k in range(1, F):
-                    p = p + ys[k] * coef[32 + k * F + j]
-                ro = bs[j] - p
-                for k in range(F):
-                    p = p + es[k] * coef[k * F + j]
-                    ro = ro + ds[k] * coef[16 + k * F + j]
-                s = slice(q * 128, q * 128 + 128)
-                xs_out[j, 0, pl.ds(r, 8), s] = p
-                res_out[j, 0, pl.ds(r, 8), s] = ro
+
+    def plane(x, carry):
+        def body(i, inner):
+            r = pl.multiple_of(i * 8, 8)
+            for q in range(Q):
+                bs = [b[f, x, q, pl.ds(r + TOP, 8), :] for f in range(F)]
+                ys = [y[f, x + 1, q, pl.ds(r + TOP, 8), :] for f in range(F)]
+                ds = [d[f, x, q, pl.ds(r, 8), :] for f in range(F)]
+                es = [bs[f] - ys[f] for f in range(F)]
+                for j in range(F):
+                    p = ys[0] * coef[32 + j]
+                    for k in range(1, F):
+                        p = p + ys[k] * coef[32 + k * F + j]
+                    ro = bs[j] - p
+                    for k in range(F):
+                        p = p + es[k] * coef[k * F + j]
+                        ro = ro + ds[k] * coef[16 + k * F + j]
+                    s = slice(q * 128, q * 128 + 128)
+                    xs_out[j, x, pl.ds(r, 8), s] = p
+                    res_out[j, x, pl.ds(r, 8), s] = ro
+            return inner
+
+        lax.fori_loop(0, CHUNKS, body, 0)
+        for c in copies(x):
+            c.start()
         return carry
 
-    lax.fori_loop(0, CHUNKS, body, 0)
+    lax.fori_loop(0, NX, plane, 0)
+    for x in range(NX):
+        for c in copies(x):
+            c.wait()
 
 
 def final(w, b, y, d):
-    block = pl.BlockSpec((F, 1, NY, NZ), lambda x: (0, x, 0, 0))
     out = jax.ShapeDtypeStruct((F, NX, NY, NZ), jnp.float32)
     return pl.pallas_call(
         final_kernel,
-        grid=(NX,),
         out_shape=(out, out),
         in_specs=[VM] * 4,
-        out_specs=(block, block),
-        scratch_shapes=[pltpu.VMEM((48, 8, 128), jnp.float32)],
+        out_specs=(HBM, HBM),
+        scratch_shapes=[
+            pltpu.VMEM((48, 8, 128), jnp.float32),
+            pltpu.VMEM((F, NX, NY, NZ), jnp.float32),
+            pltpu.VMEM((F, NX, NY, NZ), jnp.float32),
+            pltpu.SemaphoreType.DMA((2, NX)),
+        ],
         compiler_params=params(),
         cost_estimate=cost(5),
         name="final",
@@ -742,9 +771,10 @@
     r0 = exchange(g0, sizes, lambda a, c: (a, c ^ 1))
     r1 = exchange(g1, sizes, lambda a, c: (a, c + 1 if c % 2 else c - 1))
     b, h, accb = load_fields(*inputs)
-    b, h, y, l2, intra = edge(b, h, own, r0, r1, rl1)
+    b, h, y, g, l2 = far_edge(b, h, own, r0, r1)
     rl2 = exchange(l2, sizes, border_pair)
-    rin = exchange(intra, sizes, lambda a, c: (a ^ 1, c))
+    h, y, core = near_edge(b, h, y, g, rl1)
+    rin = exchange(core, sizes, lambda a, c: (a ^ 1, c))
     y, z, acc = inner(b, h, own, r0, r1, y)
     h, y, z, acc = near_side(b, h, rin, y, z, acc)
     y, z, msg = far_side(b, h, rl1, rl2, y, z, accb, acc)

time: 59.5 us -> 58.4 us (0.982)
  Pallas kernels: 24.4 us -> 21.9 us
  waiting for transfers between devices: 2.32 us -> 3.58 us
    pallas_call x1, Pallas kernels: 3.53 us -> 1.57 us  [load_fields(): pl.pallas_call(functools.partial(load_kernel, current), out_shape=(f32(F,...]
    ppermute x5, waiting for transfers between devices: 2.32 us -> 3.58 us  [exchange(): return lax.ppermute(x, AXES, pairs)]
    pallas_call x2 -> x3, Pallas kernels: 8.55 us -> 7.5 us  [the longest x1 6.06 us: final(): pl.pallas_call(final_kernel, out_shape=(out, out), in_specs=[VM] * 4, out...]
  transfers between devices with their start and end apart: 5 -> 5, of which waited for: 1 -> 2; matrix products, arithmetic and copies ran while one was open for 0% -> 0% of each run, Pallas kernels for 22% -> 21%
where the time goes in v4:
time: 58.4 us; the launch traced here: 58.2 us
  Pallas kernels  21.9 us (38%)
  blocking collectives  21.1 us (36%)
  starting transfers between devices  10.8 us (18%)
  waiting for transfers between devices  3.58 us (6%)
  between operations  0.76 us (1%)
    all_to_all x1, blocking collectives, shards(): w = lax.all_to_all(sent, AXES, 0, 0).reshape(nx * ny, 128)  21.1 us
    ppermute x5, starting transfers between devices, exchange(): return lax.ppermute(x, AXES, pairs)  10.8 us
    pallas_call x1, Pallas kernels, inner(): pl.pallas_call(inner_kernel, out_shape=(f32(F, NX + 2, Q, ROWS, 128), f32...  7.92 us
    pallas_call x1, Pallas kernels, final(): pl.pallas_call(final_kernel, out_shape=(out, out), in_specs=[VM] * 4, out...  6.06 us
    ppermute x5, waiting for transfers between devices, exchange(): return lax.ppermute(x, AXES, pairs)  3.58 us
    pallas_call x1, Pallas kernels, pack(): pl.pallas_call(functools.partial(pack_kernel, current), out_shape=(f32(L1...  2.17 us
    pallas_call x1, Pallas kernels, near_side(): pl.pallas_call(near_kernel, out_shape=(f32(NX + 2, Q, ROWS, 128), f32(F,...  1.79 us
    pallas_call x1, Pallas kernels, load_fields(): pl.pallas_call(functools.partial(load_kernel, current), out_shape=(f32(F,...  1.57 us
  transfers between devices with their start and end apart: 5, of which 2 were waited for; matrix products, arithmetic and copies ran while one was open for 0% of the time, Pallas kernels for 21%

profile of v4, /device:TPU:1, one launch (start us, length us, event | category | flops | bytes accessed | tf_op | source)
XLA Modules:
  0.0 58.2 jit_solution(2327941644846309525)
XLA Ops:
  0.6 0.0 copy-start.1
  0.6 0.0 copy-start
  0.6 2.2 %pack.1 = (f32[1280,128]{1,0:T(8,128)S(1)}, f32[288,128]{1,0:T(8,128)S(1)}, f32[288,128]{1,0:T(8,128)S(1)}, f32[2,160,128]{2,1,0:T(8,128)S(1)}) custom-call(f32[4,8,64,512]{3,2,1,0:T(8,128)} %adj.3, f32[8,64,512]{2,1,0:T(8,128)} %sigma.3, s32[4]{0:T(128)} %elec_in.3), custom_call_target="tpu_custom_call" | custom-call | flops 8000000 | bytes 6000000 | tf_op jit(solution)/shard_map/pack/pallas_call | solution.py:185
  2.8 4.6 %collective-permute-start.2 = (f32[1280,128]{1,0:T(8,128)S(1)}, f32[1280,128]{1,0:T(8,128)S(1)}, u32[]{:S(2)}, u32[]{:S(2)}) collective-permute-start(f32[1280,128]{1,0:T(8,128)S(1)} %get-tuple-element.36), channel_id=1, source_target_pairs={{4,8},{5,9},{6,10},{7,11},{8,4},{9,5},{10,6},{11,7},{12,16},{13,17... | collective-permute-start | bytes 1966088 | tf_op jit(solution)/shard_map/ppermute | solution.py:761
  7.5 1.7 %collective-permute-start = (f32[288,128]{1,0:T(8,128)S(1)}, f32[288,128]{1,0:T(8,128)S(1)}, u32[]{:S(2)}, u32[]{:S(2)}) collective-permute-start(f32[288,128]{1,0:T(8,128)S(1)} %get-tuple-element.30), channel_id=1, source_target_pairs={{0,1},{1,0},{2,3},{3,2},{4,5},{5,4},{6,7},{7,6},{8,9},{9,8},{10,11... | collective-permute-start | bytes 442376 | tf_op jit(solution)/shard_map/ppermute | solution.py:761
  9.2 0.7 %collective-permute-start.1 = (f32[288,128]{1,0:T(8,128)S(1)}, f32[288,128]{1,0:T(8,128)S(1)}, u32[]{:S(2)}, u32[]{:S(2)}) collective-permute-start(f32[288,128]{1,0:T(8,128)S(1)} %get-tuple-element.31), channel_id=1, source_target_pairs={{1,2},{2,1},{5,6},{6,5},{9,10},{10,9},{13,14},{14,13},{17,18},{18,... | collective-permute-start | bytes 442376 | tf_op jit(solution)/shard_map/ppermute | solution.py:761
  9.9 0.0 copy-done.1
  9.9 0.0 copy-done
  9.9 1.6 %load.1 = (f32[4,8,4,80,128]{4,3,2,1,0:T(8,128)S(1)}, f32[10,4,80,128]{3,2,1,0:T(8,128)S(1)}, f32[10,8,128]{2,1,0:T(8,128)S(1)}) custom-call(f32[4,8,64,512]{3,2,1,0:T(8,128)S(1)} %copy-done, f32[8,64,512]{2,1,0:T(8,128)S(1)} %copy-done.1, s32[4]{0:T(128)} %elec_in.3), custom_call_target="tpu_custom_call" | custom-call | flops 8000000 | bytes 6000000 | tf_op jit(solution)/shard_map/load/pallas_call | solution.py:244
  11.5 0.3 collective-permute-done.r0
  11.7 0.0 collective-permute-done.1.r1
  11.7 0.7 %far_edge.1 = (f32[4,8,4,80,128]{4,3,2,1,0:T(8,128)S(1)}, f32[10,4,80,128]{3,2,1,0:T(8,128)S(1)}, f32[4,10,4,80,128]{4,3,2,1,0:T(8,128)S(1)}, f32[2,160,128]{2,1,0:T(8,128)S(1)}, f32[1072,128]{1,0:T(8,128)S(1)}) custom-call(f32[4,8,4,80,128]{4,3,2,1,0:T(8,128)S(1)} %get-tuple-element.27.b_in, ...), custom_call_target="tpu_custom_call", output_to_operand_aliasing={{0}: (0, {}), {1}: (1, {})} | custom-call | flops 40000000 | bytes 30000000 | tf_op jit(solution)/shard_map/far_edge/pallas_call | solution.py:375
  12.4 3.3 %collective-permute-done.2.rl1 = f32[1280,128]{1,0:T(8,128)S(1)} collective-permute-done((f32[1280,128]{1,0:T(8,128)S(1)}, f32[1280,128]{1,0:T(8,128)S(1)}, u32[]{:S(2)}, u32[]{:S(2)}) %collective-permute-start.2) | collective-permute-done | bytes 655392 | tf_op jit(solution)/shard_map/ppermute | solution.py:761
  15.7 0.7 %near_edge.1 = (f32[10,4,80,128]{3,2,1,0:T(8,128)S(1)}, f32[4,10,4,80,128]{4,3,2,1,0:T(8,128)S(1)}, f32[2352,128]{1,0:T(8,128)S(1)}) custom-call(f32[4,8,4,80,128]{4,3,2,1,0:T(8,128)S(1)} %get-tuple-element.32.b, f32[10,4,80,128]{3,2,1,0:T(8,128)S(1)} %get-tuple-element.33.h_in, ...), custom_call_target="tpu_custom_call", output_to_operand_aliasing={{0}: (1, {}), {1}: (2, {})} | custom-call | flops 80000000 | bytes 60000000 | tf_op jit(solution)/shard_map/near_edge/pallas_call | solution.py:395
  16.5 0.1 collective-permute-start.3
  16.6 3.7 %collective-permute-start.4 = (f32[1072,128]{1,0:T(8,128)S(1)}, f32[1072,128]{1,0:T(8,128)S(1)}, u32[]{:S(2)}, u32[]{:S(2)}) collective-permute-start(f32[1072,128]{1,0:T(8,128)S(1)} %get-tuple-element.44), channel_id=1, source_target_pairs={{4,8},{5,9},{6,10},{7,11},{8,4},{9,5},{10,6},{11,7},{12,16},{13,17... | collective-permute-start | bytes 1646600 | tf_op jit(solution)/shard_map/ppermute | solution.py:761
  20.3 7.9 %inner.1 = (f32[4,10,4,80,128]{4,3,2,1,0:T(8,128)S(1)}, f32[4,8,4,64,128]{4,3,2,1,0:T(8,128)S(1)}, f32[30,8,128]{2,1,0:T(8,128)S(1)}) custom-call(f32[4,8,4,80,128]{4,3,2,1,0:T(8,128)S(1)} %get-tuple-element.32.b, f32[10,4,80,128]{3,2,1,0:T(8,128)S(1)} %get-tuple-element.37.h.h_in, ...), custom_call_target="tpu_custom_call", output_to_operand_aliasing={{0}: (5, {})} | custom-call | tf_op jit(solution)/shard_map/inner/pallas_call | solution.py:494
  28.2 0.0 collective-permute-done.3.rin
  28.2 1.8 %near.1 = (f32[10,4,80,128]{3,2,1,0:T(8,128)S(1)}, f32[4,10,4,80,128]{4,3,2,1,0:T(8,128)S(1)}, f32[4,8,4,64,128]{4,3,2,1,0:T(8,128)S(1)}, f32[30,8,128]{2,1,0:T(8,128)S(1)}) custom-call(f32[4,8,4,80,128]{4,3,2,1,0:T(8,128)S(1)} %get-tuple-element.32.b, ...), custom_call_target="tpu_custom_call", output_to_operand_aliasing={{0}: (1, {}), {1}: (3, {}), {2}: (4, {})} | custom-call | tf_op jit(solution)/shard_map/near/pallas_call | solution.py:558
  30.0 0.0 collective-permute-done.4.rl2
  30.1 1.0 %far.1 = (f32[4,10,4,80,128]{4,3,2,1,0:T(8,128)S(1)}, f32[4,8,4,64,128]{4,3,2,1,0:T(8,128)S(1)}, f32[8,128]{1,0:T(8,128)S(1)}) custom-call(f32[4,8,4,80,128]{4,3,2,1,0:T(8,128)S(1)} %get-tuple-element.32.b, f32[10,4,80,128]{3,2,1,0:T(8,128)S(1)} %get-tuple-element.43.h, ...), custom_call_target="tpu_custom_call", output_to_operand_aliasing={{0}: (4, {}), {1}: (5, {})} | custom-call | flops 12000000 | bytes 9000000 | tf_op jit(solution)/shard_map/far/pallas_call | solution.py:598
  31.0 0.1 broadcast_in_dim.9
  31.1 21.1 %all_to_all.5 = f32[128,1,128]{2,1,0:T(1,128)S(1)} all-to-all(f32[128,1,128]{2,1,0:T(1,128)S(1)} %broadcast_in_dim.9), channel_id=1, replica_groups=mesh['gx'=32,'gy'=4] {'gx','gy'}, dimensions={0} | all-to-all | bytes 131072 | tf_op jit(solution)/shard_map/all_to_all | solution.py:782
  52.2 6.1 %final.1 = (f32[4,8,64,512]{3,2,1,0:T(8,128)}, f32[4,8,64,512]{3,2,1,0:T(8,128)}) custom-call(f32[128,128]{1,0:T(8,128)S(1)} %bitcast.3, f32[4,8,4,80,128]{4,3,2,1,0:T(8,128)S(1)} %get-tuple-element.32.b, f32[4,10,4,80,128]{4,3,2,1,0:T(8,128)S(1)} %get-tuple-element.50.y, f32[4,8,4,64,128]{4,3,2,1,0:T(8,128)S(1)} %get-tuple-element.51.d), custom_call_target="tpu_custom_call" | custom-call | flops 20000000 | bytes 15000000 | tf_op jit(solution)/shard_map/final/pallas_call | solution.py:736
  (1 shorter events, 0.0 us)
Async XLA Ops:
  0.6 9.2 %copy-start.1 = (f32[8,64,512]{2,1,0:T(8,128)S(1)}, f32[8,64,512]{2,1,0:T(8,128)}, u32[]{:S(2)}) copy-start(f32[8,64,512]{2,1,0:T(8,128)} %sigma.3) | copy-start | bytes 3145732
  0.6 9.2 %copy-start = (f32[4,8,64,512]{3,2,1,0:T(8,128)S(1)}, f32[4,8,64,512]{3,2,1,0:T(8,128)}, u32[]{:S(2)}) copy-start(f32[4,8,64,512]{3,2,1,0:T(8,128)} %adj.3) | copy-start | bytes 12582916
  2.8 12.9 %collective-permute-start.2 = (f32[1280,128]{1,0:T(8,128)S(1)}, f32[1280,128]{1,0:T(8,128)S(1)}, u32[]{:S(2)}, u32[]{:S(2)}) collective-permute-start(f32[1280,128]{1,0:T(8,128)S(1)} %get-tuple-element.36), channel_id=1, source_target_pairs={{4,8},{5,9},{6,10},{7,11},{8,4},{9,5},{10,6},{11,7},{12,16},{13,17... | collective-permute-start | bytes 1966088 | tf_op jit(solution)/shard_map/ppermute | solution.py:761
  7.5 4.3 %collective-permute-start = (f32[288,128]{1,0:T(8,128)S(1)}, f32[288,128]{1,0:T(8,128)S(1)}, u32[]{:S(2)}, u32[]{:S(2)}) collective-permute-start(f32[288,128]{1,0:T(8,128)S(1)} %get-tuple-element.30), channel_id=1, source_target_pairs={{0,1},{1,0},{2,3},{3,2},{4,5},{5,4},{6,7},{7,6},{8,9},{9,8},{10,11... | collective-permute-start | bytes 442376 | tf_op jit(solution)/shard_map/ppermute | solution.py:761
  9.2 2.5 %collective-permute-start.1 = (f32[288,128]{1,0:T(8,128)S(1)}, f32[288,128]{1,0:T(8,128)S(1)}, u32[]{:S(2)}, u32[]{:S(2)}) collective-permute-start(f32[288,128]{1,0:T(8,128)S(1)} %get-tuple-element.31), channel_id=1, source_target_pairs={{1,2},{2,1},{5,6},{6,5},{9,10},{10,9},{13,14},{14,13},{17,18},{18,... | collective-permute-start | bytes 442376 | tf_op jit(solution)/shard_map/ppermute | solution.py:761
  16.5 11.8 %collective-permute-start.3 = (f32[2352,128]{1,0:T(8,128)S(1)}, f32[2352,128]{1,0:T(8,128)S(1)}, u32[]{:S(2)}, u32[]{:S(2)}) collective-permute-start(f32[2352,128]{1,0:T(8,128)S(1)} %get-tuple-element.38), channel_id=1, source_target_pairs={{0,4},{1,5},{2,6},{3,7},{4,0},{5,1},{6,2},{7,3},{8,12},{9,13},{10,... | collective-permute-start | bytes 3612680 | tf_op jit(solution)/shard_map/ppermute | solution.py:761
  16.6 13.5 %collective-permute-start.4 = (f32[1072,128]{1,0:T(8,128)S(1)}, f32[1072,128]{1,0:T(8,128)S(1)}, u32[]{:S(2)}, u32[]{:S(2)}) collective-permute-start(f32[1072,128]{1,0:T(8,128)S(1)} %get-tuple-element.44), channel_id=1, source_target_pairs={{4,8},{5,9},{6,10},{7,11},{8,4},{9,5},{10,6},{11,7},{12,16},{13,17... | collective-permute-start | bytes 1646600 | tf_op jit(solution)/shard_map/ppermute | solution.py:761

commit v5 on v4

--- a/solution.py
+++ b/solution.py
@@ -206,7 +206,7 @@
     )(*in_hbm(adj, sigma, electrodes))
 
 
-def load_kernel(current, adj, sigma, elec_in, b_out, h_out, acc, elec, esem):
+def load_kernel(current, adj, sigma, elec_in, b_out, h_out, y, acc, elec, esem):
     ecopy = pltpu.make_async_copy(elec_in, elec, esem)
     ecopy.start()
     acc[...] = jnp.zeros(acc.shape, jnp.float32)
@@ -217,6 +217,10 @@
             for f in range(F):
                 b_out[f, x, q, TOP : TOP + NY, :] = adj[f, x, :, s]
             h_out[x + 1, q, TOP : TOP + NY, :] = 0.5 * sigma[x, :, s]
+            for row, edge in ((TOP - 1, TOP), (TOP + NY, TOP + NY - 1)):
+                h_out[x + 1, q, row : row + 1, :] = -h_out[x + 1, q, edge : edge + 1, :]
+                for f in range(F):
+                    b_out[f, x, q, row : row + 1, :] = jnp.zeros((1, 128), jnp.float32)
         return carry
 
     lax.fori_loop(0, NX, place, 0)
@@ -239,13 +243,31 @@
 
     lax.fori_loop(0, NX, plane, 0)
 
+    def image(x, carry):
+        def chunk(r):
+            coeffs = chunk_coeffs(h_out, x + 1, r)
+            for f in range(F):
+                _, out = chunk_apply(coeffs, b_out, f, x, r)
+                for q in range(Q):
+                    y[f, x + 1, q, pl.ds(r + TOP, 8), :] = out[q]
+
+        chunk_loop(chunk)
+        return carry
+
+    lax.fori_loop(1, NX - 1, image, 0)
+
 
 def load_fields(current, adj, sigma, electrodes):
     return pl.pallas_call(
         functools.partial(load_kernel, current),
-        out_shape=(f32(F, NX, Q, ROWS, 128), f32(NX + 2, Q, ROWS, 128), f32(10, 8, 128)),
+        out_shape=(
+            f32(F, NX, Q, ROWS, 128),
+            f32(NX + 2, Q, ROWS, 128),
+            f32(F, NX + 2, Q, ROWS, 128),
+            f32(10, 8, 128),
+        ),
         in_specs=[VM, VM, HBM],
-        out_specs=(VM,) * 3,
+        out_specs=(VM,) * 4,
         scratch_shapes=[pltpu.SMEM((F,), jnp.int32), pltpu.SemaphoreType.DMA],
         compiler_params=params(),
         cost_estimate=cost(2),
@@ -319,8 +341,8 @@
             out[a : a + 1, :] = g[side, pl.ds(item * 8 + x, 1), :]
 
 
-def far_edge_kernel(b_in, h_in, own, r0, r1, b, h, y, g, out, clamped):
-    del b_in, h_in
+def far_edge_kernel(b_in, h_in, y_in, own, r0, r1, b, h, y, g, out, clamped):
+    del b_in, h_in, y_in
     par = lax.axis_index("gx") % 2
     ypar = lax.axis_index("gy") % 2
     for item in range((F + 1) * Q):
@@ -371,7 +393,7 @@
     chunk_loop(chunk)
 
 
-def far_edge(b, h, own, r0, r1):
+def far_edge(b, h, y, own, r0, r1):
     return pl.pallas_call(
         far_edge_kernel,
         out_shape=(
@@ -381,14 +403,14 @@
             f32(2, TILE_ROWS, 128),
             f32(L2_ROWS, 128),
         ),
-        in_specs=[VM] * 5,
+        in_specs=[VM] * 6,
         out_specs=(VM,) * 5,
-        input_output_aliases={0: 0, 1: 1},
+        input_output_aliases={0: 0, 1: 1, 2: 2},
         scratch_shapes=[pltpu.VMEM((2, Q, 8, 128), jnp.float32)],
         compiler_params=params(),
         cost_estimate=cost(10),
         name="far_edge",
-    )(b, h, own, r0, r1)
+    )(b, h, y, own, r0, r1)
 
 
 def near_edge(b, h, y, g, rl1):
@@ -433,6 +455,19 @@
                 y[f, x + 1, q, row : row + 1, :] = tmp[side, f, q, x : x + 1, :]
 
 
+def halo_rows(own, rh, y, tmp):
+    for side in range(2):
+        row = TOP if side == 0 else TOP + NY - 1
+        for q in range(Q):
+            h_own = own[side, (F * Q + q) * 8 : (F * Q + q) * 8 + 8, :]
+            c = h_own + inside(rh(F * Q + q)[side], h_own)
+            for f in range(F):
+                item = f * Q + q
+                tmp[2 + side, f, q] = c * (own[side, item * 8 : item * 8 + 8, :] - rh(item)[side])
+                for x in range(1, NX - 1):
+                    y[f, x + 1, q, row : row + 1, :] += tmp[2 + side, f, q, x : x + 1, :]
+
+
 def z_plane(h, y, d, acc, x):
     def chunk(r):
         coeffs = chunk_coeffs(h, x + 1, r)
@@ -468,15 +503,9 @@
     for side in range(2):
         row_halo(own, lambda item: halo_select(ypar, r0, r1, item)[side], side, y, tmp)
 
+    halo_rows(own, lambda item: halo_select(ypar, r0, r1, item), y, tmp)
+
     def y_plane(x, carry):
-        def chunk(r):
-            coeffs = chunk_coeffs(h, x + 1, r)
-            for f in range(F):
-                _, out = chunk_apply(coeffs, b, f, x, r)
-                for q in range(Q):
-                    y[f, x + 1, q, pl.ds(r + TOP, 8), :] = out[q]
-
-        chunk_loop(chunk)
         plane_grams(b, y, acc, x)
         return carry
 
@@ -501,7 +530,7 @@
         in_specs=[VM] * 6,
         out_specs=(VM,) * 3,
         input_output_aliases={5: 0},
-        scratch_shapes=[pltpu.VMEM((2, F, Q, 8, 128), jnp.float32)],
+        scratch_shapes=[pltpu.VMEM((4, F, Q, 8, 128), jnp.float32)],
         compiler_params=params(),
         cost_estimate=cost(0),
         name="inner",
@@ -770,8 +799,8 @@
     rl1 = exchange(l1, sizes, border_pair)
     r0 = exchange(g0, sizes, lambda a, c: (a, c ^ 1))
     r1 = exchange(g1, sizes, lambda a, c: (a, c + 1 if c % 2 else c - 1))
-    b, h, accb = load_fields(*inputs)
-    b, h, y, g, l2 = far_edge(b, h, own, r0, r1)
+    b, h, y, accb = load_fields(*inputs)
+    b, h, y, g, l2 = far_edge(b, h, y, own, r0, r1)
     rl2 = exchange(l2, sizes, border_pair)
     h, y, core = near_edge(b, h, y, g, rl1)
     rin = exchange(core, sizes, lambda a, c: (a ^ 1, c))

time: 58.4 us -> 58.1 us (level)
  waiting for transfers between devices: 3.58 us -> 0.78 us
  blocking collectives: 21.1 us -> 23.4 us
    pallas_call x1, Pallas kernels: 1.57 us -> 4.71 us  [load_fields(): pl.pallas_call(functools.partial(load_kernel, current), out_shape=(f32(F,...]
    pallas_call x1, Pallas kernels: 7.92 us -> 4.93 us  [inner(): pl.pallas_call(inner_kernel, out_shape=(f32(F, NX + 2, Q, ROWS, 128), f32...]
    ppermute x5, waiting for transfers between devices: 3.58 us -> 0.78 us  [exchange(): return lax.ppermute(x, AXES, pairs)]
    all_to_all x1, blocking collectives: 21.1 us -> 23.4 us  [shards(): w = lax.all_to_all(sent, AXES, 0, 0).reshape(nx * ny, 128)]
where the time goes in v5:
time: 58.1 us; the launch traced here: 57.9 us
  blocking collectives  23.4 us (40%)
  Pallas kernels  22.1 us (38%)
  starting transfers between devices  10.8 us (19%)
  waiting for transfers between devices  0.78 us (1%)
  between operations  0.77 us (1%)
    all_to_all x1, blocking collectives, shards(): w = lax.all_to_all(sent, AXES, 0, 0).reshape(nx * ny, 128)  23.4 us
    ppermute x5, starting transfers between devices, exchange(): return lax.ppermute(x, AXES, pairs)  10.8 us
    pallas_call x1, Pallas kernels, final(): pl.pallas_call(final_kernel, out_shape=(out, out), in_specs=[VM] * 4, out...  6.06 us
    pallas_call x1, Pallas kernels, inner(): pl.pallas_call(inner_kernel, out_shape=(f32(F, NX + 2, Q, ROWS, 128), f32...  4.93 us
    pallas_call x1, Pallas kernels, load_fields(): pl.pallas_call(functools.partial(load_kernel, current), out_shape=(f32(F,...  4.71 us
    pallas_call x1, Pallas kernels, pack(): pl.pallas_call(functools.partial(pack_kernel, current), out_shape=(f32(L1...  2.17 us
    pallas_call x1, Pallas kernels, near_side(): pl.pallas_call(near_kernel, out_shape=(f32(NX + 2, Q, ROWS, 128), f32(F,...  1.79 us
  transfers between devices with their start and end apart: 5, of which 2 were waited for; matrix products, arithmetic and copies ran while one was open for 0% of the time, Pallas kernels for 21%

profile of v5, /device:TPU:1, one launch (start us, length us, event | category | flops | bytes accessed | tf_op | source)
XLA Modules:
  0.0 57.9 jit_solution(3366843945123103926)
XLA Ops:
  0.6 0.0 copy-start.1
  0.6 0.0 copy-start
  0.6 2.2 %pack.1 = (f32[1280,128]{1,0:T(8,128)S(1)}, f32[288,128]{1,0:T(8,128)S(1)}, f32[288,128]{1,0:T(8,128)S(1)}, f32[2,160,128]{2,1,0:T(8,128)S(1)}) custom-call(f32[4,8,64,512]{3,2,1,0:T(8,128)} %adj.3, f32[8,64,512]{2,1,0:T(8,128)} %sigma.3, s32[4]{0:T(128)} %elec_in.3), custom_call_target="tpu_custom_call" | custom-call | flops 8000000 | bytes 6000000 | tf_op jit(solution)/shard_map/pack/pallas_call | solution.py:185
  2.8 4.6 %collective-permute-start.2 = (f32[1280,128]{1,0:T(8,128)S(1)}, f32[1280,128]{1,0:T(8,128)S(1)}, u32[]{:S(2)}, u32[]{:S(2)}) collective-permute-start(f32[1280,128]{1,0:T(8,128)S(1)} %get-tuple-element.38), channel_id=1, source_target_pairs={{4,8},{5,9},{6,10},{7,11},{8,4},{9,5},{10,6},{11,7},{12,16},{13,17... | collective-permute-start | bytes 1966088 | tf_op jit(solution)/shard_map/ppermute | solution.py:790
  7.5 1.7 %collective-permute-start = (f32[288,128]{1,0:T(8,128)S(1)}, f32[288,128]{1,0:T(8,128)S(1)}, u32[]{:S(2)}, u32[]{:S(2)}) collective-permute-start(f32[288,128]{1,0:T(8,128)S(1)} %get-tuple-element.32), channel_id=1, source_target_pairs={{0,1},{1,0},{2,3},{3,2},{4,5},{5,4},{6,7},{7,6},{8,9},{9,8},{10,11... | collective-permute-start | bytes 442376 | tf_op jit(solution)/shard_map/ppermute | solution.py:790
  9.2 0.7 %collective-permute-start.1 = (f32[288,128]{1,0:T(8,128)S(1)}, f32[288,128]{1,0:T(8,128)S(1)}, u32[]{:S(2)}, u32[]{:S(2)}) collective-permute-start(f32[288,128]{1,0:T(8,128)S(1)} %get-tuple-element.33), channel_id=1, source_target_pairs={{1,2},{2,1},{5,6},{6,5},{9,10},{10,9},{13,14},{14,13},{17,18},{18,... | collective-permute-start | bytes 442376 | tf_op jit(solution)/shard_map/ppermute | solution.py:790
  9.9 0.0 copy-done.1
  9.9 0.0 copy-done
  9.9 4.7 %load.1 = (f32[4,8,4,80,128]{4,3,2,1,0:T(8,128)S(1)}, f32[10,4,80,128]{3,2,1,0:T(8,128)S(1)}, f32[4,10,4,80,128]{4,3,2,1,0:T(8,128)S(1)}, f32[10,8,128]{2,1,0:T(8,128)S(1)}) custom-call(f32[4,8,64,512]{3,2,1,0:T(8,128)S(1)} %copy-done, f32[8,64,512]{2,1,0:T(8,128)S(1)} %copy-done.1, s32[4]{0:T(128)} %elec_in.3), custom_call_target="tpu_custom_call" | custom-call | flops 8000000 | bytes 6000000 | tf_op jit(solution)/shard_map/load/pallas_call | solution.py:261
  14.6 0.0 collective-permute-done.r0
  14.6 0.0 collective-permute-done.1.r1
  14.6 0.7 %far_edge.1 = (f32[4,8,4,80,128]{4,3,2,1,0:T(8,128)S(1)}, f32[10,4,80,128]{3,2,1,0:T(8,128)S(1)}, f32[4,10,4,80,128]{4,3,2,1,0:T(8,128)S(1)}, f32[2,160,128]{2,1,0:T(8,128)S(1)}, f32[1072,128]{1,0:T(8,128)S(1)}) custom-call(f32[4,8,4,80,128]{4,3,2,1,0:T(8,128)S(1)} %get-tuple-element.28.b_in, ...), custom_call_target="tpu_custom_call", output_to_operand_aliasing={{0}: (0, {}), {1}: (1, {}), {2}: (2, {})} | custom-call | flops 40000000 | bytes 30000000 | tf_op jit(solution)/shard_map/far_edge/pallas_call | solution.py:397
  15.3 0.4 collective-permute-done.2.rl1
  15.7 0.7 %near_edge.1 = (f32[10,4,80,128]{3,2,1,0:T(8,128)S(1)}, f32[4,10,4,80,128]{4,3,2,1,0:T(8,128)S(1)}, f32[2352,128]{1,0:T(8,128)S(1)}) custom-call(f32[4,8,4,80,128]{4,3,2,1,0:T(8,128)S(1)} %get-tuple-element.34.b, f32[10,4,80,128]{3,2,1,0:T(8,128)S(1)} %get-tuple-element.35.h_in, ...), custom_call_target="tpu_custom_call", output_to_operand_aliasing={{0}: (1, {}), {1}: (2, {})} | custom-call | flops 80000000 | bytes 60000000 | tf_op jit(solution)/shard_map/near_edge/pallas_call | solution.py:417
  16.5 0.1 collective-permute-start.3
  16.6 3.7 %collective-permute-start.4 = (f32[1072,128]{1,0:T(8,128)S(1)}, f32[1072,128]{1,0:T(8,128)S(1)}, u32[]{:S(2)}, u32[]{:S(2)}) collective-permute-start(f32[1072,128]{1,0:T(8,128)S(1)} %get-tuple-element.46), channel_id=1, source_target_pairs={{4,8},{5,9},{6,10},{7,11},{8,4},{9,5},{10,6},{11,7},{12,16},{13,17... | collective-permute-start | bytes 1646600 | tf_op jit(solution)/shard_map/ppermute | solution.py:790
  20.3 4.9 %inner.1 = (f32[4,10,4,80,128]{4,3,2,1,0:T(8,128)S(1)}, f32[4,8,4,64,128]{4,3,2,1,0:T(8,128)S(1)}, f32[30,8,128]{2,1,0:T(8,128)S(1)}) custom-call(f32[4,8,4,80,128]{4,3,2,1,0:T(8,128)S(1)} %get-tuple-element.34.b, f32[10,4,80,128]{3,2,1,0:T(8,128)S(1)} %get-tuple-element.39.h.h_in, ...), custom_call_target="tpu_custom_call", output_to_operand_aliasing={{0}: (5, {})} | custom-call | tf_op jit(solution)/shard_map/inner/pallas_call | solution.py:523
  25.2 0.0 collective-permute-done.3.rin
  25.3 1.8 %near.1 = (f32[10,4,80,128]{3,2,1,0:T(8,128)S(1)}, f32[4,10,4,80,128]{4,3,2,1,0:T(8,128)S(1)}, f32[4,8,4,64,128]{4,3,2,1,0:T(8,128)S(1)}, f32[30,8,128]{2,1,0:T(8,128)S(1)}) custom-call(f32[4,8,4,80,128]{4,3,2,1,0:T(8,128)S(1)} %get-tuple-element.34.b, ...), custom_call_target="tpu_custom_call", output_to_operand_aliasing={{0}: (1, {}), {1}: (3, {}), {2}: (4, {})} | custom-call | tf_op jit(solution)/shard_map/near/pallas_call | solution.py:587
  27.1 0.4 collective-permute-done.4.rl2
  27.4 1.0 %far.1 = (f32[4,10,4,80,128]{4,3,2,1,0:T(8,128)S(1)}, f32[4,8,4,64,128]{4,3,2,1,0:T(8,128)S(1)}, f32[8,128]{1,0:T(8,128)S(1)}) custom-call(f32[4,8,4,80,128]{4,3,2,1,0:T(8,128)S(1)} %get-tuple-element.34.b, f32[10,4,80,128]{3,2,1,0:T(8,128)S(1)} %get-tuple-element.45.h, ...), custom_call_target="tpu_custom_call", output_to_operand_aliasing={{0}: (4, {}), {1}: (5, {})} | custom-call | flops 12000000 | bytes 9000000 | tf_op jit(solution)/shard_map/far/pallas_call | solution.py:627
  28.4 0.1 broadcast_in_dim.9
  28.4 23.4 %all_to_all.5 = f32[128,1,128]{2,1,0:T(1,128)S(1)} all-to-all(f32[128,1,128]{2,1,0:T(1,128)S(1)} %broadcast_in_dim.9), channel_id=1, replica_groups=mesh['gx'=32,'gy'=4] {'gx','gy'}, dimensions={0} | all-to-all | bytes 131072 | tf_op jit(solution)/shard_map/all_to_all | solution.py:811
  51.8 6.1 %final.1 = (f32[4,8,64,512]{3,2,1,0:T(8,128)}, f32[4,8,64,512]{3,2,1,0:T(8,128)}) custom-call(f32[128,128]{1,0:T(8,128)S(1)} %bitcast.3, f32[4,8,4,80,128]{4,3,2,1,0:T(8,128)S(1)} %get-tuple-element.34.b, f32[4,10,4,80,128]{4,3,2,1,0:T(8,128)S(1)} %get-tuple-element.52.y, f32[4,8,4,64,128]{4,3,2,1,0:T(8,128)S(1)} %get-tuple-element.53.d), custom_call_target="tpu_custom_call" | custom-call | flops 20000000 | bytes 15000000 | tf_op jit(solution)/shard_map/final/pallas_call | solution.py:765
  (1 shorter events, 0.0 us)
Async XLA Ops:
  0.6 9.2 %copy-start.1 = (f32[8,64,512]{2,1,0:T(8,128)S(1)}, f32[8,64,512]{2,1,0:T(8,128)}, u32[]{:S(2)}) copy-start(f32[8,64,512]{2,1,0:T(8,128)} %sigma.3) | copy-start | bytes 3145732
  0.6 9.2 %copy-start = (f32[4,8,64,512]{3,2,1,0:T(8,128)S(1)}, f32[4,8,64,512]{3,2,1,0:T(8,128)}, u32[]{:S(2)}) copy-start(f32[4,8,64,512]{3,2,1,0:T(8,128)} %adj.3) | copy-start | bytes 12582916
  2.8 12.9 %collective-permute-start.2 = (f32[1280,128]{1,0:T(8,128)S(1)}, f32[1280,128]{1,0:T(8,128)S(1)}, u32[]{:S(2)}, u32[]{:S(2)}) collective-permute-start(f32[1280,128]{1,0:T(8,128)S(1)} %get-tuple-element.38), channel_id=1, source_target_pairs={{4,8},{5,9},{6,10},{7,11},{8,4},{9,5},{10,6},{11,7},{12,16},{13,17... | collective-permute-start | bytes 1966088 | tf_op jit(solution)/shard_map/ppermute | solution.py:790
  7.5 7.1 %collective-permute-start = (f32[288,128]{1,0:T(8,128)S(1)}, f32[288,128]{1,0:T(8,128)S(1)}, u32[]{:S(2)}, u32[]{:S(2)}) collective-permute-start(f32[288,128]{1,0:T(8,128)S(1)} %get-tuple-element.32), channel_id=1, source_target_pairs={{0,1},{1,0},{2,3},{3,2},{4,5},{5,4},{6,7},{7,6},{8,9},{9,8},{10,11... | collective-permute-start | bytes 442376 | tf_op jit(solution)/shard_map/ppermute | solution.py:790
  9.2 5.4 %collective-permute-start.1 = (f32[288,128]{1,0:T(8,128)S(1)}, f32[288,128]{1,0:T(8,128)S(1)}, u32[]{:S(2)}, u32[]{:S(2)}) collective-permute-start(f32[288,128]{1,0:T(8,128)S(1)} %get-tuple-element.33), channel_id=1, source_target_pairs={{1,2},{2,1},{5,6},{6,5},{9,10},{10,9},{13,14},{14,13},{17,18},{18,... | collective-permute-start | bytes 442376 | tf_op jit(solution)/shard_map/ppermute | solution.py:790
  16.5 8.8 %collective-permute-start.3 = (f32[2352,128]{1,0:T(8,128)S(1)}, f32[2352,128]{1,0:T(8,128)S(1)}, u32[]{:S(2)}, u32[]{:S(2)}) collective-permute-start(f32[2352,128]{1,0:T(8,128)S(1)} %get-tuple-element.40), channel_id=1, source_target_pairs={{0,4},{1,5},{2,6},{3,7},{4,0},{5,1},{6,2},{7,3},{8,12},{9,13},{10,... | collective-permute-start | bytes 3612680 | tf_op jit(solution)/shard_map/ppermute | solution.py:790
  16.6 10.9 %collective-permute-start.4 = (f32[1072,128]{1,0:T(8,128)S(1)}, f32[1072,128]{1,0:T(8,128)S(1)}, u32[]{:S(2)}, u32[]{:S(2)}) collective-permute-start(f32[1072,128]{1,0:T(8,128)S(1)} %get-tuple-element.46), channel_id=1, source_target_pairs={{4,8},{5,9},{6,10},{7,11},{8,4},{9,5},{10,6},{11,7},{12,16},{13,17... | collective-permute-start | bytes 1646600 | tf_op jit(solution)/shard_map/ppermute | solution.py:790

commit v6 on v5

--- a/solution.py
+++ b/solution.py
@@ -341,7 +341,7 @@
             out[a : a + 1, :] = g[side, pl.ds(item * 8 + x, 1), :]
 
 
-def far_edge_kernel(b_in, h_in, y_in, own, r0, r1, b, h, y, g, out, clamped):
+def far_edge_kernel(b_in, h_in, y_in, own, r0, r1, b, h, y, out, core, g, clamped):
     del b_in, h_in, y_in
     par = lax.axis_index("gx") % 2
     ypar = lax.axis_index("gy") % 2
@@ -357,23 +357,23 @@
                 clamped[side, q] = inside(t, own[side, item * 8 : item * 8 + 8, :])
                 for x in range(NX):
                     h[x + 1, q, row : row + 1, :] = clamped[side, q, x : x + 1, :]
-    far = side_planes(par)[0]
+    far, near, _, _ = side_planes(par)
     edge_plane(b, h, y, far, 1 - 2 * par)
     put_image(y, g, out, 0, far)
-
-
-def near_edge_kernel(b, h_in, y_in, g, rl1, h, y, out):
-    del h_in, y_in
-    par = lax.axis_index("gx") % 2
-    far, near, far_halo, _ = side_planes(par)
     edge_plane(b, h, y, near, 2 * par - 1)
     for q in range(Q):
         for f in range(F):
             a = (f * Q + q) * NY
-            out[a : a + NY, :] = b[f, near, q, TOP : TOP + NY, :]
+            core[a : a + NY, :] = b[f, near, q, TOP : TOP + NY, :]
         a = (F * Q + q) * NY
-        out[a : a + NY, :] = h[near + 1, q, TOP : TOP + NY, :]
-    put_image(y, g, out, L1_ROWS, near)
+        core[a : a + NY, :] = h[near + 1, q, TOP : TOP + NY, :]
+    put_image(y, g, core, L1_ROWS, near)
+
+
+def border_kernel(b, h_in, y_in, core_in, rl1, h, y, core):
+    del h_in, y_in, core_in, core
+    par = lax.axis_index("gx") % 2
+    far, _, far_halo, _ = side_planes(par)
     border(b, h, y, rl1, far, far_halo)
 
 
@@ -400,34 +400,33 @@
             f32(F, NX, Q, ROWS, 128),
             f32(NX + 2, Q, ROWS, 128),
             f32(F, NX + 2, Q, ROWS, 128),
-            f32(2, TILE_ROWS, 128),
             f32(L2_ROWS, 128),
+            f32(IN_ROWS, 128),
         ),
         in_specs=[VM] * 6,
         out_specs=(VM,) * 5,
         input_output_aliases={0: 0, 1: 1, 2: 2},
-        scratch_shapes=[pltpu.VMEM((2, Q, 8, 128), jnp.float32)],
+        scratch_shapes=[
+            pltpu.VMEM((2, TILE_ROWS, 128), jnp.float32),
+            pltpu.VMEM((2, Q, 8, 128), jnp.float32),
+        ],
         compiler_params=params(),
         cost_estimate=cost(10),
         name="far_edge",
     )(b, h, y, own, r0, r1)
 
 
-def near_edge(b, h, y, g, rl1):
+def border_faces(b, h, y, core, rl1):
     return pl.pallas_call(
-        near_edge_kernel,
-        out_shape=(
-            f32(NX + 2, Q, ROWS, 128),
-            f32(F, NX + 2, Q, ROWS, 128),
-            f32(IN_ROWS, 128),
-        ),
+        border_kernel,
+        out_shape=(f32(NX + 2, Q, ROWS, 128), f32(F, NX + 2, Q, ROWS, 128), f32(IN_ROWS, 128)),
         in_specs=[VM] * 5,
         out_specs=(VM,) * 3,
-        input_output_aliases={1: 0, 2: 1},
+        input_output_aliases={1: 0, 2: 1, 3: 2},
         compiler_params=params(),
         cost_estimate=cost(20),
-        name="near_edge",
-    )(b, h, y, g, rl1)
+        name="border",
+    )(b, h, y, core, rl1)
 
 
 def row_halo(own, rh, side, y, tmp):
@@ -800,9 +799,9 @@
     r0 = exchange(g0, sizes, lambda a, c: (a, c ^ 1))
     r1 = exchange(g1, sizes, lambda a, c: (a, c + 1 if c % 2 else c - 1))
     b, h, y, accb = load_fields(*inputs)
-    b, h, y, g, l2 = far_edge(b, h, y, own, r0, r1)
+    b, h, y, l2, core = far_edge(b, h, y, own, r0, r1)
     rl2 = exchange(l2, sizes, border_pair)
-    h, y, core = near_edge(b, h, y, g, rl1)
+    h, y, core = border_faces(b, h, y, core, rl1)
     rin = exchange(core, sizes, lambda a, c: (a ^ 1, c))
     y, z, acc = inner(b, h, own, r0, r1, y)
     h, y, z, acc = near_side(b, h, rin, y, z, acc)

time: 58.1 us -> 57.6 us (level)
    pallas_call x1, Pallas kernels: 0.7 us -> 1.29 us  [far_edge(): pl.pallas_call(far_edge_kernel, out_shape=(f32(F, NX, Q, ROWS, 128), f32(...]
  transfers between devices with their start and end apart: 5 -> 5, of which waited for: 2 -> 1; matrix products, arithmetic and copies ran while one was open for 0% -> 0% of each run, Pallas kernels for 21% -> 22%
where the time goes in v6:
time: 57.6 us; the launch traced here: 57.4 us
  blocking collectives  23.3 us (40%)
  Pallas kernels  22.1 us (38%)
  starting transfers between devices  10.6 us (18%)
  between operations  0.78 us (1%)
    all_to_all x1, blocking collectives, shards(): w = lax.all_to_all(sent, AXES, 0, 0).reshape(nx * ny, 128)  23.3 us
    ppermute x5, starting transfers between devices, exchange(): return lax.ppermute(x, AXES, pairs)  10.6 us
    pallas_call x1, Pallas kernels, final(): pl.pallas_call(final_kernel, out_shape=(out, out), in_specs=[VM] * 4, out...  6.06 us
    pallas_call x1, Pallas kernels, inner(): pl.pallas_call(inner_kernel, out_shape=(f32(F, NX + 2, Q, ROWS, 128), f32...  4.92 us
    pallas_call x1, Pallas kernels, load_fields(): pl.pallas_call(functools.partial(load_kernel, current), out_shape=(f32(F,...  4.71 us
    pallas_call x1, Pallas kernels, pack(): pl.pallas_call(functools.partial(pack_kernel, current), out_shape=(f32(L1...  2.16 us
    pallas_call x1, Pallas kernels, near_side(): pl.pallas_call(near_kernel, out_shape=(f32(NX + 2, Q, ROWS, 128), f32(F,...  1.79 us
    pallas_call x1, Pallas kernels, far_edge(): pl.pallas_call(far_edge_kernel, out_shape=(f32(F, NX, Q, ROWS, 128), f32(...  1.29 us
  transfers between devices with their start and end apart: 5, of which 1 were waited for; matrix products, arithmetic and copies ran while one was open for 0% of the time, Pallas kernels for 22%

profile of v6, /device:TPU:1, one launch (start us, length us, event | category | flops | bytes accessed | tf_op | source)
XLA Modules:
  0.0 57.4 jit_solution(13217301954087407542)
XLA Ops:
  0.6 0.0 copy-start.1
  0.6 0.0 copy-start
  0.6 2.2 %pack.1 = (f32[1280,128]{1,0:T(8,128)S(1)}, f32[288,128]{1,0:T(8,128)S(1)}, f32[288,128]{1,0:T(8,128)S(1)}, f32[2,160,128]{2,1,0:T(8,128)S(1)}) custom-call(f32[4,8,64,512]{3,2,1,0:T(8,128)} %adj.3, f32[8,64,512]{2,1,0:T(8,128)} %sigma.3, s32[4]{0:T(128)} %elec_in.3), custom_call_target="tpu_custom_call" | custom-call | flops 8000000 | bytes 6000000 | tf_op jit(solution)/shard_map/pack/pallas_call | solution.py:185
  2.8 4.6 %collective-permute-start.2 = (f32[1280,128]{1,0:T(8,128)S(1)}, f32[1280,128]{1,0:T(8,128)S(1)}, u32[]{:S(2)}, u32[]{:S(2)}) collective-permute-start(f32[1280,128]{1,0:T(8,128)S(1)} %get-tuple-element.38), channel_id=1, source_target_pairs={{4,8},{5,9},{6,10},{7,11},{8,4},{9,5},{10,6},{11,7},{12,16},{13,17... | collective-permute-start | bytes 1966088 | tf_op jit(solution)/shard_map/ppermute | solution.py:789
  7.5 1.7 %collective-permute-start = (f32[288,128]{1,0:T(8,128)S(1)}, f32[288,128]{1,0:T(8,128)S(1)}, u32[]{:S(2)}, u32[]{:S(2)}) collective-permute-start(f32[288,128]{1,0:T(8,128)S(1)} %get-tuple-element.32), channel_id=1, source_target_pairs={{0,1},{1,0},{2,3},{3,2},{4,5},{5,4},{6,7},{7,6},{8,9},{9,8},{10,11... | collective-permute-start | bytes 442376 | tf_op jit(solution)/shard_map/ppermute | solution.py:789
  9.2 0.7 %collective-permute-start.1 = (f32[288,128]{1,0:T(8,128)S(1)}, f32[288,128]{1,0:T(8,128)S(1)}, u32[]{:S(2)}, u32[]{:S(2)}) collective-permute-start(f32[288,128]{1,0:T(8,128)S(1)} %get-tuple-element.33), channel_id=1, source_target_pairs={{1,2},{2,1},{5,6},{6,5},{9,10},{10,9},{13,14},{14,13},{17,18},{18,... | collective-permute-start | bytes 442376 | tf_op jit(solution)/shard_map/ppermute | solution.py:789
  9.9 0.0 copy-done.1
  9.9 0.0 copy-done
  9.9 4.7 %load.1 = (f32[4,8,4,80,128]{4,3,2,1,0:T(8,128)S(1)}, f32[10,4,80,128]{3,2,1,0:T(8,128)S(1)}, f32[4,10,4,80,128]{4,3,2,1,0:T(8,128)S(1)}, f32[10,8,128]{2,1,0:T(8,128)S(1)}) custom-call(f32[4,8,64,512]{3,2,1,0:T(8,128)S(1)} %copy-done, f32[8,64,512]{2,1,0:T(8,128)S(1)} %copy-done.1, s32[4]{0:T(128)} %elec_in.3), custom_call_target="tpu_custom_call" | custom-call | flops 8000000 | bytes 6000000 | tf_op jit(solution)/shard_map/load/pallas_call | solution.py:261
  14.6 0.0 collective-permute-done.r0
  14.6 0.0 collective-permute-done.1.r1
  14.6 1.3 %far_edge.1 = (f32[4,8,4,80,128]{4,3,2,1,0:T(8,128)S(1)}, f32[10,4,80,128]{3,2,1,0:T(8,128)S(1)}, f32[4,10,4,80,128]{4,3,2,1,0:T(8,128)S(1)}, f32[1072,128]{1,0:T(8,128)S(1)}, f32[2352,128]{1,0:T(8,128)S(1)}) custom-call(f32[4,8,4,80,128]{4,3,2,1,0:T(8,128)S(1)} %get-tuple-element.28.b_in, ...), custom_call_target="tpu_custom_call", output_to_operand_aliasing={{0}: (0, {}), {1}: (1, {}), {2}: (2, {})} | custom-call | flops 40000000 | bytes 30000000 | tf_op jit(solution)/shard_map/far_edge/pallas_call | solution.py:397
  15.9 0.0 collective-permute-done.2.rl1
  15.9 0.2 border.1
  16.1 0.1 collective-permute-start.3
  16.2 3.5 %collective-permute-start.4 = (f32[1072,128]{1,0:T(8,128)S(1)}, f32[1072,128]{1,0:T(8,128)S(1)}, u32[]{:S(2)}, u32[]{:S(2)}) collective-permute-start(f32[1072,128]{1,0:T(8,128)S(1)} %get-tuple-element.46), channel_id=1, source_target_pairs={{4,8},{5,9},{6,10},{7,11},{8,4},{9,5},{10,6},{11,7},{12,16},{13,17... | collective-permute-start | bytes 1646600 | tf_op jit(solution)/shard_map/ppermute | solution.py:789
  19.7 4.9 %inner.1 = (f32[4,10,4,80,128]{4,3,2,1,0:T(8,128)S(1)}, f32[4,8,4,64,128]{4,3,2,1,0:T(8,128)S(1)}, f32[30,8,128]{2,1,0:T(8,128)S(1)}) custom-call(f32[4,8,4,80,128]{4,3,2,1,0:T(8,128)S(1)} %get-tuple-element.34.b, f32[10,4,80,128]{3,2,1,0:T(8,128)S(1)} %get-tuple-element.39.h.h_in, ...), custom_call_target="tpu_custom_call", output_to_operand_aliasing={{0}: (5, {})} | custom-call | tf_op jit(solution)/shard_map/inner/pallas_call | solution.py:522
  24.6 0.0 collective-permute-done.3.rin
  24.7 1.8 %near.1 = (f32[10,4,80,128]{3,2,1,0:T(8,128)S(1)}, f32[4,10,4,80,128]{4,3,2,1,0:T(8,128)S(1)}, f32[4,8,4,64,128]{4,3,2,1,0:T(8,128)S(1)}, f32[30,8,128]{2,1,0:T(8,128)S(1)}) custom-call(f32[4,8,4,80,128]{4,3,2,1,0:T(8,128)S(1)} %get-tuple-element.34.b, ...), custom_call_target="tpu_custom_call", output_to_operand_aliasing={{0}: (1, {}), {1}: (3, {}), {2}: (4, {})} | custom-call | tf_op jit(solution)/shard_map/near/pallas_call | solution.py:586
  26.4 0.5 collective-permute-done.4.rl2
  27.0 1.0 %far.1 = (f32[4,10,4,80,128]{4,3,2,1,0:T(8,128)S(1)}, f32[4,8,4,64,128]{4,3,2,1,0:T(8,128)S(1)}, f32[8,128]{1,0:T(8,128)S(1)}) custom-call(f32[4,8,4,80,128]{4,3,2,1,0:T(8,128)S(1)} %get-tuple-element.34.b, f32[10,4,80,128]{3,2,1,0:T(8,128)S(1)} %get-tuple-element.45.h, ...), custom_call_target="tpu_custom_call", output_to_operand_aliasing={{0}: (4, {}), {1}: (5, {})} | custom-call | flops 12000000 | bytes 9000000 | tf_op jit(solution)/shard_map/far/pallas_call | solution.py:626
  27.9 0.1 broadcast_in_dim.9
  28.0 23.3 %all_to_all.5 = f32[128,1,128]{2,1,0:T(1,128)S(1)} all-to-all(f32[128,1,128]{2,1,0:T(1,128)S(1)} %broadcast_in_dim.9), channel_id=1, replica_groups=mesh['gx'=32,'gy'=4] {'gx','gy'}, dimensions={0} | all-to-all | bytes 131072 | tf_op jit(solution)/shard_map/all_to_all | solution.py:810
  51.3 6.1 %final.1 = (f32[4,8,64,512]{3,2,1,0:T(8,128)}, f32[4,8,64,512]{3,2,1,0:T(8,128)}) custom-call(f32[128,128]{1,0:T(8,128)S(1)} %bitcast.3, f32[4,8,4,80,128]{4,3,2,1,0:T(8,128)S(1)} %get-tuple-element.34.b, f32[4,10,4,80,128]{4,3,2,1,0:T(8,128)S(1)} %get-tuple-element.52.y, f32[4,8,4,64,128]{4,3,2,1,0:T(8,128)S(1)} %get-tuple-element.53.d), custom_call_target="tpu_custom_call" | custom-call | flops 20000000 | bytes 15000000 | tf_op jit(solution)/shard_map/final/pallas_call | solution.py:764
  (1 shorter events, 0.0 us)
Async XLA Ops:
  0.6 9.2 %copy-start.1 = (f32[8,64,512]{2,1,0:T(8,128)S(1)}, f32[8,64,512]{2,1,0:T(8,128)}, u32[]{:S(2)}) copy-start(f32[8,64,512]{2,1,0:T(8,128)} %sigma.3) | copy-start | bytes 3145732
  0.6 9.2 %copy-start = (f32[4,8,64,512]{3,2,1,0:T(8,128)S(1)}, f32[4,8,64,512]{3,2,1,0:T(8,128)}, u32[]{:S(2)}) copy-start(f32[4,8,64,512]{3,2,1,0:T(8,128)} %adj.3) | copy-start | bytes 12582916
  2.8 13.1 %collective-permute-start.2 = (f32[1280,128]{1,0:T(8,128)S(1)}, f32[1280,128]{1,0:T(8,128)S(1)}, u32[]{:S(2)}, u32[]{:S(2)}) collective-permute-start(f32[1280,128]{1,0:T(8,128)S(1)} %get-tuple-element.38), channel_id=1, source_target_pairs={{4,8},{5,9},{6,10},{7,11},{8,4},{9,5},{10,6},{11,7},{12,16},{13,17... | collective-permute-start | bytes 1966088 | tf_op jit(solution)/shard_map/ppermute | solution.py:789
  7.5 7.1 %collective-permute-start = (f32[288,128]{1,0:T(8,128)S(1)}, f32[288,128]{1,0:T(8,128)S(1)}, u32[]{:S(2)}, u32[]{:S(2)}) collective-permute-start(f32[288,128]{1,0:T(8,128)S(1)} %get-tuple-element.32), channel_id=1, source_target_pairs={{0,1},{1,0},{2,3},{3,2},{4,5},{5,4},{6,7},{7,6},{8,9},{9,8},{10,11... | collective-permute-start | bytes 442376 | tf_op jit(solution)/shard_map/ppermute | solution.py:789
  9.2 5.4 %collective-permute-start.1 = (f32[288,128]{1,0:T(8,128)S(1)}, f32[288,128]{1,0:T(8,128)S(1)}, u32[]{:S(2)}, u32[]{:S(2)}) collective-permute-start(f32[288,128]{1,0:T(8,128)S(1)} %get-tuple-element.33), channel_id=1, source_target_pairs={{1,2},{2,1},{5,6},{6,5},{9,10},{10,9},{13,14},{14,13},{17,18},{18,... | collective-permute-start | bytes 442376 | tf_op jit(solution)/shard_map/ppermute | solution.py:789
  16.1 8.6 %collective-permute-start.3 = (f32[2352,128]{1,0:T(8,128)S(1)}, f32[2352,128]{1,0:T(8,128)S(1)}, u32[]{:S(2)}, u32[]{:S(2)}) collective-permute-start(f32[2352,128]{1,0:T(8,128)S(1)} %get-tuple-element.40), channel_id=1, source_target_pairs={{0,4},{1,5},{2,6},{3,7},{4,0},{5,1},{6,2},{7,3},{8,12},{9,13},{10,... | collective-permute-start | bytes 3612680 | tf_op jit(solution)/shard_map/ppermute | solution.py:789
  16.2 10.8 %collective-permute-start.4 = (f32[1072,128]{1,0:T(8,128)S(1)}, f32[1072,128]{1,0:T(8,128)S(1)}, u32[]{:S(2)}, u32[]{:S(2)}) collective-permute-start(f32[1072,128]{1,0:T(8,128)S(1)} %get-tuple-element.46), channel_id=1, source_target_pairs={{4,8},{5,9},{6,10},{7,11},{8,4},{9,5},{10,6},{11,7},{12,16},{13,17... | collective-permute-start | bytes 1646600 | tf_op jit(solution)/shard_map/ppermute | solution.py:789
